TPU v7x, 32 devices: a whole 2x2x4 slice. The times are simulated.
32 devices in a mesh: lon: 8 (over z, y), lat: 4 (over x, core).
Axes of the slice: x: 2, y: 2, z: 4, core: 2. Of those that a mesh axis runs over, the one named last changes fastest.
Arguments:
- hidden_in: bfloat16 [8, 128, 128, 512], P(None, None, 'lon', 'lat'), may hold values from -6 to 6
- w_conv1: bfloat16 [3, 3, 128, 128], replicated, may hold values from -0.1875 to 0.1875
- b_conv1: float32 [128], replicated, may hold values from -3 to 3
- w_conv2: bfloat16 [3, 3, 128, 12], replicated, may hold values from -0.1875 to 0.1875
- b_conv2: float32 [12], replicated, may hold values from -3.5 to 3.5
- state: float32 [6, 8, 128, 512], P(None, None, 'lon', 'lat'), may hold values from -6 to 6
Outputs:
- velocity: float32 [12, 8, 128, 512], P(None, None, 'lon', 'lat')
- tendency: float32 [6, 8, 128, 512], P(None, None, 'lon', 'lat')
All inputs are finite; a program needn't handle non-finite values.
Results may differ from a plain program's by a relative error of at most 0.0013.
Values may be sent and summed in bfloat16 or wider, within the bound.
No kernel may reach another device: no remote copies, remote signals or barrier semaphores. Data moves between devices by JAX's collectives and lax.ppermute only.
A program may use at most 128 MiB of HBM per device.

v0:
```python
import math

import jax
import jax.numpy as jnp
from jax import lax
from jax.sharding import PartitionSpec as P

time_step = 0.5
speed_cap = 0.6
cos_floor = 0.5


def padded_2(block, sides, width):
    for axis, dim in sides:
        count = lax.axis_size(axis)
        forward = [(i, i + 1) for i in range(count - 1)]
        forward.append((count - 1, 0))
        backward = [(target, source) for source, target in forward]
        low = lax.ppermute(
            lax.slice_in_dim(block, block.shape[dim] - width, None, axis=dim), axis, forward
        )
        high = lax.ppermute(lax.slice_in_dim(block, 0, width, axis=dim), axis, backward)
        block = jnp.concatenate([low, block, high], axis=dim)
    return block


def crop(field, have, want):
    depth = have - want
    if depth == 0:
        return field
    return field[..., depth : field.shape[-2] - depth, depth : field.shape[-1] - depth]


def lat_profile(margin, lat_dev):
    n_lat = lat_dev * lax.axis_size("lat")
    global_rows = (
        lax.axis_index("lat") * lat_dev + jnp.arange(lat_dev + 2 * margin, dtype=jnp.int32) - margin
    )
    inside = ((global_rows >= 0) & (global_rows < n_lat)).astype(jnp.float32)
    latitude = (global_rows.astype(jnp.float32) + 0.5) * (math.pi / n_lat) - 0.5 * math.pi
    cosine = jnp.maximum(jnp.cos(latitude), cos_floor)
    return (inside, cosine, 1.0 / cosine)


def conv_block(padded, weight):
    out_x = padded.shape[1] - 2
    out_y = padded.shape[2] - 2
    taps = jnp.stack(
        [
            padded[:, row_off : row_off + out_x, col_off : col_off + out_y]
            for row_off in range(3)
            for col_off in range(3)
        ]
    )
    stacked = weight.reshape(9, weight.shape[2], weight.shape[3])
    return jnp.einsum("tcxy,tco->oxy", taps, stacked, preferred_element_type=jnp.float32)


def body(hidden_in, w_conv1, b_conv1, w_conv2, b_conv2, state):
    lat_dev = state.shape[3]
    reach = 1

    def first_layer(features):
        return jax.nn.silu(conv_block(features, w_conv1) + b_conv1[:, None, None]).astype(
            jnp.bfloat16
        )

    def second_layer(hidden):
        return speed_cap * jnp.tanh(conv_block(hidden, w_conv2) + b_conv2[:, None, None])

    in_width = reach + 2
    padded = padded_2(hidden_in, (("lon", 2), ("lat", 3)), in_width)
    padded = padded * lat_profile(in_width, lat_dev)[0].astype(jnp.bfloat16)
    hidden_keep = lat_profile(reach + 1, lat_dev)[0].astype(jnp.bfloat16)
    speed_keep = lat_profile(reach, lat_dev)[0]

    def level(features):
        hidden = first_layer(features) * hidden_keep
        return second_layer(hidden) * speed_keep

    wide = jnp.transpose(lax.map(level, padded), (1, 0, 2, 3))
    velocity = crop(wide, reach, 0)
    zonal_wide = wide[0::2]
    north_wide = wide[1::2]
    cosine_wide = lat_profile(reach, lat_dev)[1]
    flux = north_wide * cosine_wide
    metric_rows = lat_profile(reach - 1, lat_dev)[2]
    divergence = metric_rows * (
        (zonal_wide[..., 2:, 1:-1] - zonal_wide[..., :-2, 1:-1]) * 0.5
        + (flux[..., 1:-1, 2:] - flux[..., 1:-1, :-2]) * 0.5
    )
    zonal_in = crop(zonal_wide, reach, reach - 1)
    north_in = crop(north_wide, reach, reach - 1)

    def section_rate(q_padded, margin_in):
        margin_out = margin_in - 1
        zonal = crop(zonal_in, reach - 1, margin_out)
        north = crop(north_in, reach - 1, margin_out)
        spread = crop(divergence, reach - 1, margin_out)
        centre = q_padded[..., 1:-1, 1:-1]
        back_x = centre - q_padded[..., :-2, 1:-1]
        fore_x = q_padded[..., 2:, 1:-1] - centre
        back_y = centre - q_padded[..., 1:-1, :-2]
        fore_y = q_padded[..., 1:-1, 2:] - centre
        advect = (
            metric_rows * (jnp.maximum(zonal, 0.0) * back_x + jnp.minimum(zonal, 0.0) * fore_x)
            + jnp.maximum(north, 0.0) * back_y
            + jnp.minimum(north, 0.0) * fore_y
        )
        return -(advect + centre * spread)

    keep_one = lat_profile(1, lat_dev)[0]

    def section_from(field):
        edged = padded_2(field, (("lon", 2), ("lat", 3)), 1) * keep_one
        return section_rate(edged, 1)

    rate_one = section_from(state)
    rate_two = section_from(state + 0.5 * time_step * rate_one)
    rate_three = section_from(state + 0.5 * time_step * rate_two)
    rate_four = section_from(state + time_step * rate_three)
    tendency = (rate_one + 2.0 * rate_two + 2.0 * rate_three + rate_four) / 6.0
    return (velocity, tendency)


def solution(mesh):
    placed = (P(None, None, "lon", "lat"), P(), P(), P(), P(), P(None, None, "lon", "lat"))
    return jax.shard_map(
        body,
        mesh=mesh,
        in_specs=placed,
        out_specs=(P(None, None, "lon", "lat"), P(None, None, "lon", "lat")),
        check_vma=False,
    )
```

profile of v0, /device:TPU:1, one launch (start us, length us, event | category | flops | bytes accessed | tf_op | source)
XLA Modules:
  0.0 250.1 jit_solution(15972550135474372832)
XLA Ops:
  0.6 6.8 %copy.86 = bf16[8,128,16,128]{1,3,2,0:T(8,128)(2,1)} copy(bf16[8,128,16,128]{3,2,1,0:T(8,128)(2,1)} %param.8) | data formatting | bytes 8388608 | tf_op args[0]
  7.5 2.7 %fusion.81 = (bf16[8,128,3,128]{1,3,2,0:T(8,128)(2,1)}, bf16[8,128,3,128]{1,3,2,0:T(8,128)(2,1)}) fusion(bf16[8,128,16,128]{1,3,2,0:T(8,128)(2,1)} %copy.86), kind=kLoop, calls=%fused_computation.144 | loop fusion | bytes 3145728 | tf_op jit(solution)/shard_map/slice | solution.py:20
  10.2 2.1 collective-permute-start
  12.3 3.0 %collective-permute-start.1 = (bf16[8,128,3,128]{1,3,2,0:T(8,128)(2,1)}, bf16[8,128,3,128]{1,3,2,0:T(8,128)(2,1)}, u32[]{:S(2)}, u32[]{:S(2)}) collective-permute-start(bf16[8,128,3,128]{1,3,2,0:T(8,128)(2,1)} %get-tuple-element.126), channel_id=1, source_target_pairs={{4,0},{8,4},{12,8},{16,12},{20,16},{24,20},{28,24},{0,28},{5,1},{9... | collective-permute-start | bytes 2359304 | tf_op jit(solution)/shard_map/ppermute | solution.py:22
  15.4 4.1 %collective-permute-start.5 = (f32[6,8,1,128]{3,1,2,0:T(8,128)S(1)}, f32[6,8,1,128]{3,1,2,0:T(8,128)S(1)}, u32[]{:S(2)}, u32[]{:S(2)}) collective-permute-start(f32[6,8,1,128]{3,1,2,0:T(8,128)S(1)} %copy.128), channel_id=1, source_target_pairs={{4,0},{8,4},{12,8},{16,12},{20,16},{24,20},{28,24},{0,28},{5,1},{9... | collective-permute-start | bytes 73736 | tf_op jit(solution)/shard_map/ppermute | solution.py:22
  19.7 2.3 copy.93
  22.0 24.6 %collective-permute-done.4 = f32[6,8,1,128]{3,1,2,0:T(8,128)S(1)} collective-permute-done((f32[6,8,1,128]{3,1,2,0:T(8,128)S(1)}, f32[6,8,1,128]{3,1,2,0:T(8,128)S(1)}, u32[]{:S(2)}, u32[]{:S(2)}) %collective-permute-start.4) | collective-permute-done | bytes 24608 | tf_op jit(solution)/shard_map/ppermute | solution.py:19
  46.6 2.3 copy.92
  48.9 2.2 copy.94
  51.0 5.4 %pad_maximum_fusion = f32[6,8,18,128]{2,1,3,0:T(8,128)S(1)} fusion(f32[6,8,1,128]{2,1,3,0:T(8,128)} %copy.94, f32[6,8,16,128]{2,1,3,0:T(8,128)} %copy.93, f32[6,8,1,128]{2,1,3,0:T(8,128)} %copy.92), kind=kLoop, calls=%fused_computation.56 | loop fusion | flops 221184 | bytes 884736 | tf_op jit(solution)/shard_map/concatenate | solution.py:23
  57.1 2.6 %collective-permute-start.6 = (f32[6,8,18,1]{2,1,3,0:T(8,128)}, f32[6,8,18,1]{2,1,3,0:T(8,128)}, u32[]{:S(2)}, u32[]{:S(2)}) collective-permute-start(f32[6,8,18,1]{2,1,3,0:T(8,128)} %get-tuple-element.127), channel_id=1, source_target_pairs={{0,1},{1,2},{2,3},{3,0},{4,5},{5,6},{6,7},{7,4},{8,9},{9,10},{10,1... | collective-permute-start | bytes 10376 | tf_op jit(solution)/shard_map/ppermute | solution.py:19
  60.3 1.9 copy.96
  62.2 1.2 copy.95
  64.5 1.4 pad_maximum_fusion.6
  65.9 1.8 collective-permute-start.2
  68.2 3.1 %collective-permute-done.2 = bf16[8,128,22,3]{1,3,2,0:T(4,128)(2,1)S(1)} collective-permute-done((bf16[8,128,22,3]{1,3,2,0:T(4,128)(2,1)S(1)}, bf16[8,128,22,3]{1,3,2,0:T(4,128)(2,1)S(1)}, u32[]{:S(2)}, u32[]{:S(2)}) %collective-permute-start.2) | collective-permute-done | bytes 135200 | tf_op jit(solution)/shard_map/ppermute | solution.py:19
  71.3 1.5 collective-permute-done.3
  72.8 6.5 %maximum_multiply_fusion = bf16[8,128,22,134]{1,3,2,0:T(8,128)(2,1)} fusion(bf16[8,128,22,3]{1,3,2,0:T(4,128)(2,1)S(1)} %collective-permute-done.3, bf16[8,128,3,128]{1,3,2,0:T(8,128)(2,1)} %collective-permute-done.1, bf16[8,128,16,128]{1,3,2,0:T(8,128)(2,1)S(1)} %copy-done, bf16[8,128,3,128]{1,3,2,0:T(8,128)(2,1)} %collective-permute-done, ...), kind=kLoop, calls=%fused_computation.55 | loop fusion | flops 36225024 | bytes 12075276 | tf_op jit(solution)/shard_map/mul | solution.py:73
  79.3 113.0 %while.12 = (s32[]{:T(128)}, f32[8,12,18,130]{3,0,2,1:T(8,128)}, bf16[8,128,22,134]{1,3,2,0:T(8,128)(2,1)}, bf16[3,3,128,128]{3,2,1,0:T(8,128)(2,1)S(1)}, f32[12...) while((s32[]{:T(128)}, f32[8,12,18,130]{3,0,2,1:T(8,128)}, ...), condition=%wide.region_1.2_spmd.clone.clone, body=%wide.region_0.1_spmd.clone.clone.sunk | while | flops 845687296 | bytes 38311556 | solution.py:81
  79.3 1.2 dynamic-slice_bitcast_fusion.2
  82.1 2.1 fusion.133
  85.7 1.8 fusion.143
  87.8 5.7 %dynamic_update_slice.7 = f32[8,12,18,130]{3,0,2,1:T(8,128)} dynamic-update-slice(f32[8,12,18,130]{3,0,2,1:T(8,128)} %get-tuple-element.208, f32[1,12,18,130]{3,0,2,1:T(1,128)S(1)} %copy.131, s32[]{:T(128)} %get-tuple-element.207, s32[]{:T(128)} %constant.25.clone.1..sunk, s32[]{:T(128)} %constant.25.clone.1..sunk, s32[]{:T(128)} %constant.25.clone.1..sunk) | dynamic-update-slice | bytes 224644 | tf_op jit(solution)/shard_map/while/body/jit(dynamic_update_index_in_dim)/dynamic_update_slice | solution.py:81
  96.3 2.1 fusion.133
  99.9 1.8 fusion.143
  101.9 5.7 %dynamic_update_slice.7 = f32[8,12,18,130]{3,0,2,1:T(8,128)} dynamic-update-slice(f32[8,12,18,130]{3,0,2,1:T(8,128)} %get-tuple-element.208, f32[1,12,18,130]{3,0,2,1:T(1,128)S(1)} %copy.131, s32[]{:T(128)} %get-tuple-element.207, s32[]{:T(128)} %constant.25.clone.1..sunk, s32[]{:T(128)} %constant.25.clone.1..sunk, s32[]{:T(128)} %constant.25.clone.1..sunk) | dynamic-update-slice | bytes 224644 | tf_op jit(solution)/shard_map/while/body/jit(dynamic_update_index_in_dim)/dynamic_update_slice | solution.py:81
  110.4 2.1 fusion.133
  114.0 1.8 fusion.143
  116.0 5.7 %dynamic_update_slice.7 = f32[8,12,18,130]{3,0,2,1:T(8,128)} dynamic-update-slice(f32[8,12,18,130]{3,0,2,1:T(8,128)} %get-tuple-element.208, f32[1,12,18,130]{3,0,2,1:T(1,128)S(1)} %copy.131, s32[]{:T(128)} %get-tuple-element.207, s32[]{:T(128)} %constant.25.clone.1..sunk, s32[]{:T(128)} %constant.25.clone.1..sunk, s32[]{:T(128)} %constant.25.clone.1..sunk) | dynamic-update-slice | bytes 224644 | tf_op jit(solution)/shard_map/while/body/jit(dynamic_update_index_in_dim)/dynamic_update_slice | solution.py:81
  124.5 2.1 fusion.133
  128.1 1.8 fusion.143
  130.2 5.7 %dynamic_update_slice.7 = f32[8,12,18,130]{3,0,2,1:T(8,128)} dynamic-update-slice(f32[8,12,18,130]{3,0,2,1:T(8,128)} %get-tuple-element.208, f32[1,12,18,130]{3,0,2,1:T(1,128)S(1)} %copy.131, s32[]{:T(128)} %get-tuple-element.207, s32[]{:T(128)} %constant.25.clone.1..sunk, s32[]{:T(128)} %constant.25.clone.1..sunk, s32[]{:T(128)} %constant.25.clone.1..sunk) | dynamic-update-slice | bytes 224644 | tf_op jit(solution)/shard_map/while/body/jit(dynamic_update_index_in_dim)/dynamic_update_slice | solution.py:81
  138.6 2.1 fusion.133
  142.2 1.8 fusion.143
  144.3 5.7 %dynamic_update_slice.7 = f32[8,12,18,130]{3,0,2,1:T(8,128)} dynamic-update-slice(f32[8,12,18,130]{3,0,2,1:T(8,128)} %get-tuple-element.208, f32[1,12,18,130]{3,0,2,1:T(1,128)S(1)} %copy.131, s32[]{:T(128)} %get-tuple-element.207, s32[]{:T(128)} %constant.25.clone.1..sunk, s32[]{:T(128)} %constant.25.clone.1..sunk, s32[]{:T(128)} %constant.25.clone.1..sunk) | dynamic-update-slice | bytes 224644 | tf_op jit(solution)/shard_map/while/body/jit(dynamic_update_index_in_dim)/dynamic_update_slice | solution.py:81
  152.8 2.1 fusion.133
  156.4 1.8 fusion.143
  158.4 5.7 %dynamic_update_slice.7 = f32[8,12,18,130]{3,0,2,1:T(8,128)} dynamic-update-slice(f32[8,12,18,130]{3,0,2,1:T(8,128)} %get-tuple-element.208, f32[1,12,18,130]{3,0,2,1:T(1,128)S(1)} %copy.131, s32[]{:T(128)} %get-tuple-element.207, s32[]{:T(128)} %constant.25.clone.1..sunk, s32[]{:T(128)} %constant.25.clone.1..sunk, s32[]{:T(128)} %constant.25.clone.1..sunk) | dynamic-update-slice | bytes 224644 | tf_op jit(solution)/shard_map/while/body/jit(dynamic_update_index_in_dim)/dynamic_update_slice | solution.py:81
  166.9 2.1 fusion.133
  170.5 1.8 fusion.143
  172.5 5.7 %dynamic_update_slice.7 = f32[8,12,18,130]{3,0,2,1:T(8,128)} dynamic-update-slice(f32[8,12,18,130]{3,0,2,1:T(8,128)} %get-tuple-element.208, f32[1,12,18,130]{3,0,2,1:T(1,128)S(1)} %copy.131, s32[]{:T(128)} %get-tuple-element.207, s32[]{:T(128)} %constant.25.clone.1..sunk, s32[]{:T(128)} %constant.25.clone.1..sunk, s32[]{:T(128)} %constant.25.clone.1..sunk) | dynamic-update-slice | bytes 224644 | tf_op jit(solution)/shard_map/while/body/jit(dynamic_update_index_in_dim)/dynamic_update_slice | solution.py:81
  181.0 2.1 fusion.133
  184.6 1.8 fusion.143
  186.7 5.7 %dynamic_update_slice.7 = f32[8,12,18,130]{3,0,2,1:T(8,128)} dynamic-update-slice(f32[8,12,18,130]{3,0,2,1:T(8,128)} %get-tuple-element.208, f32[1,12,18,130]{3,0,2,1:T(1,128)S(1)} %copy.131, s32[]{:T(128)} %get-tuple-element.207, s32[]{:T(128)} %constant.25.clone.1..sunk, s32[]{:T(128)} %constant.25.clone.1..sunk, s32[]{:T(128)} %constant.25.clone.1..sunk) | dynamic-update-slice | bytes 224644 | tf_op jit(solution)/shard_map/while/body/jit(dynamic_update_index_in_dim)/dynamic_update_slice | solution.py:81
  192.3 1.7 broadcast_multiply_fusion
  194.0 1.7 multiply_add_fusion.2
  195.8 2.2 collective-permute-start.8
  198.0 3.1 %collective-permute-start.9 = (f32[6,8,1,128]{3,1,2,0:T(8,128)S(1)}, f32[6,8,1,128]{3,1,2,0:T(8,128)S(1)}, u32[]{:S(2)}, u32[]{:S(2)}) collective-permute-start(f32[6,8,1,128]{3,1,2,0:T(8,128)S(1)} %get-tuple-element.143), channel_id=1, source_target_pairs={{4,0},{8,4},{12,8},{16,12},{20,16},{24,20},{28,24},{0,28},{5,1},{9... | collective-permute-start | bytes 73736 | tf_op jit(solution)/shard_map/ppermute | solution.py:22
  201.1 1.5 collective-permute-done.8
  203.5 1.4 copy.119
  204.9 1.8 collective-permute-start.10
  208.1 3.2 %collective-permute-done.11 = f32[6,8,18,1]{2,1,3,0:T(8,128)} collective-permute-done((f32[6,8,18,1]{2,1,3,0:T(8,128)}, f32[6,8,18,1]{2,1,3,0:T(8,128)}, u32[]{:S(2)}, u32[]{:S(2)}) %collective-permute-start.11) | collective-permute-done | bytes 3488 | tf_op jit(solution)/shard_map/ppermute | solution.py:22
  212.3 1.4 maximum_multiply_fusion.2
  213.8 1.5 multiply_add_fusion.1
  215.2 4.6 %collective-permute-start.13 = (f32[6,8,1,128]{3,1,2,0:T(8,128)S(1)}, f32[6,8,1,128]{3,1,2,0:T(8,128)S(1)}, u32[]{:S(2)}, u32[]{:S(2)}) collective-permute-start(f32[6,8,1,128]{3,1,2,0:T(8,128)S(1)} %get-tuple-element.141), channel_id=1, source_target_pairs={{4,0},{8,4},{12,8},{16,12},{20,16},{24,20},{28,24},{0,28},{5,1},{9... | collective-permute-start | bytes 73736 | tf_op jit(solution)/shard_map/ppermute | solution.py:22
  221.8 1.4 copy.121
  224.3 1.4 copy.122
  226.1 2.8 %collective-permute-done.15 = f32[6,8,18,1]{2,1,3,0:T(8,128)S(1)} collective-permute-done((f32[6,8,18,1]{2,1,3,0:T(8,128)S(1)}, f32[6,8,18,1]{2,1,3,0:T(8,128)S(1)}, u32[]{:S(2)}, u32[]{:S(2)}) %collective-permute-start.15) | collective-permute-done | bytes 3488 | tf_op jit(solution)/shard_map/ppermute | solution.py:22
  230.1 1.4 maximum_multiply_fusion.3
  231.5 1.5 multiply_add_fusion
  233.0 4.5 %collective-permute-start.17 = (f32[6,8,1,128]{3,1,2,0:T(8,128)S(1)}, f32[6,8,1,128]{3,1,2,0:T(8,128)S(1)}, u32[]{:S(2)}, u32[]{:S(2)}) collective-permute-start(f32[6,8,1,128]{3,1,2,0:T(8,128)S(1)} %get-tuple-element.139), channel_id=1, source_target_pairs={{4,0},{8,4},{12,8},{16,12},{20,16},{24,20},{28,24},{0,28},{5,1},{9... | collective-permute-start | bytes 73736 | tf_op jit(solution)/shard_map/ppermute | solution.py:22
  239.6 1.4 copy.123
  242.5 1.7 slice.306
  247.4 1.9 fusion.37
  (248 shorter events, 53.2 us)
Async XLA Ops:
  0.6 14.7 %copy-start.1 = (f32[6,8,16,128]{3,2,1,0:T(8,128)S(1)}, f32[6,8,16,128]{3,2,1,0:T(8,128)}, u32[]{:S(2)}) copy-start(f32[6,8,16,128]{3,2,1,0:T(8,128)} %param.13) | copy-start | bytes 1179652
  10.2 54.3 %collective-permute-start = (bf16[8,128,3,128]{1,3,2,0:T(8,128)(2,1)}, bf16[8,128,3,128]{1,3,2,0:T(8,128)(2,1)}, u32[]{:S(2)}, u32[]{:S(2)}) collective-permute-start(bf16[8,128,3,128]{1,3,2,0:T(8,128)(2,1)} %get-tuple-element.125), channel_id=1, source_target_pairs={{0,4},{4,8},{8,12},{12,16},{16,20},{20,24},{24,28},{28,0},{1,5},{5... | collective-permute-start | bytes 2359304 | tf_op jit(solution)/shard_map/ppermute | solution.py:19
  12.3 52.3 %collective-permute-start.1 = (bf16[8,128,3,128]{1,3,2,0:T(8,128)(2,1)}, bf16[8,128,3,128]{1,3,2,0:T(8,128)(2,1)}, u32[]{:S(2)}, u32[]{:S(2)}) collective-permute-start(bf16[8,128,3,128]{1,3,2,0:T(8,128)(2,1)} %get-tuple-element.126), channel_id=1, source_target_pairs={{4,0},{8,4},{12,8},{16,12},{20,16},{24,20},{28,24},{0,28},{5,1},{9... | collective-permute-start | bytes 2359304 | tf_op jit(solution)/shard_map/ppermute | solution.py:22
  15.4 31.2 %collective-permute-start.4 = (f32[6,8,1,128]{3,1,2,0:T(8,128)S(1)}, f32[6,8,1,128]{3,1,2,0:T(8,128)S(1)}, u32[]{:S(2)}, u32[]{:S(2)}) collective-permute-start(f32[6,8,1,128]{3,1,2,0:T(8,128)S(1)} %copy.129), channel_id=1, source_target_pairs={{0,4},{4,8},{8,12},{12,16},{16,20},{20,24},{24,28},{28,0},{1,5},{5... | collective-permute-start | bytes 73736 | tf_op jit(solution)/shard_map/ppermute | solution.py:19
  15.4 33.4 %collective-permute-start.5 = (f32[6,8,1,128]{3,1,2,0:T(8,128)S(1)}, f32[6,8,1,128]{3,1,2,0:T(8,128)S(1)}, u32[]{:S(2)}, u32[]{:S(2)}) collective-permute-start(f32[6,8,1,128]{3,1,2,0:T(8,128)S(1)} %copy.128), channel_id=1, source_target_pairs={{4,0},{8,4},{12,8},{16,12},{20,16},{24,20},{28,24},{0,28},{5,1},{9... | collective-permute-start | bytes 73736 | tf_op jit(solution)/shard_map/ppermute | solution.py:22
  57.1 5.1 %collective-permute-start.6 = (f32[6,8,18,1]{2,1,3,0:T(8,128)}, f32[6,8,18,1]{2,1,3,0:T(8,128)}, u32[]{:S(2)}, u32[]{:S(2)}) collective-permute-start(f32[6,8,18,1]{2,1,3,0:T(8,128)} %get-tuple-element.127), channel_id=1, source_target_pairs={{0,1},{1,2},{2,3},{3,0},{4,5},{5,6},{6,7},{7,4},{8,9},{9,10},{10,1... | collective-permute-start | bytes 10376 | tf_op jit(solution)/shard_map/ppermute | solution.py:19
  59.8 3.6 %collective-permute-start.7 = (f32[6,8,18,1]{2,1,3,0:T(8,128)}, f32[6,8,18,1]{2,1,3,0:T(8,128)}, u32[]{:S(2)}, u32[]{:S(2)}) collective-permute-start(f32[6,8,18,1]{2,1,3,0:T(8,128)} %get-tuple-element.128), channel_id=1, source_target_pairs={{1,0},{2,1},{3,2},{0,3},{5,4},{6,5},{7,6},{4,7},{9,8},{10,9},{11,1... | collective-permute-start | bytes 10376 | tf_op jit(solution)/shard_map/ppermute | solution.py:22
  62.2 5.6 %copy-start.3 = (f32[6,8,18,128]{3,1,2,0:T(8,128)S(1)}, f32[6,8,18,128]{3,1,2,0:T(8,128)}, u32[]{:S(2)}) copy-start(f32[6,8,18,128]{3,1,2,0:T(8,128)} %copy.96) | copy-start | bytes 1327108
  62.2 10.6 %copy-start.6 = (bf16[134]{0:T(256)(128)(2,1)S(1)}, bf16[134]{0:T(256)(128)(2,1)}, u32[]{:S(2)}) copy-start(bf16[134]{0:T(256)(128)(2,1)} %fusion.76) | copy-start | bytes 808
  64.5 8.3 %copy-start = (bf16[8,128,16,128]{1,3,2,0:T(8,128)(2,1)S(1)}, bf16[8,128,16,128]{1,3,2,0:T(8,128)(2,1)}, u32[]{:S(2)}) copy-start(bf16[8,128,16,128]{1,3,2,0:T(8,128)(2,1)} %copy.86) | copy-start | bytes 12582916
  65.9 5.4 %collective-permute-start.2 = (bf16[8,128,22,3]{1,3,2,0:T(4,128)(2,1)S(1)}, bf16[8,128,22,3]{1,3,2,0:T(4,128)(2,1)S(1)}, u32[]{:S(2)}, u32[]{:S(2)}) collective-permute-start(bf16[8,128,22,3]{1,3,2,0:T(4,128)(2,1)S(1)} %get-tuple-element.123), channel_id=1, source_target_pairs={{0,1},{1,2},{2,3},{3,0},{4,5},{5,6},{6,7},{7,4},{8,9},{9,10},{10,1... | collective-permute-start | bytes 405512 | tf_op jit(solution)/shard_map/ppermute | solution.py:19
  67.7 5.1 %collective-permute-start.3 = (bf16[8,128,22,3]{1,3,2,0:T(4,128)(2,1)S(1)}, bf16[8,128,22,3]{1,3,2,0:T(4,128)(2,1)S(1)}, u32[]{:S(2)}, u32[]{:S(2)}) collective-permute-start(bf16[8,128,22,3]{1,3,2,0:T(4,128)(2,1)S(1)} %get-tuple-element.124), channel_id=1, source_target_pairs={{1,0},{2,1},{3,2},{0,3},{5,4},{6,5},{7,6},{4,7},{9,8},{10,9},{11,1... | collective-permute-start | bytes 405512 | tf_op jit(solution)/shard_map/ppermute | solution.py:22
  68.2 11.1 %copy-start.4 = (bf16[3,3,128,12]{2,3,1,0:T(8,128)(2,1)S(1)}, bf16[3,3,128,12]{2,3,1,0:T(8,128)(2,1)}, u32[]{:S(2)}) copy-start(bf16[3,3,128,12]{2,3,1,0:T(8,128)(2,1)} %param.11) | copy-start | bytes 82948
  68.2 11.1 %copy-start.5 = (f32[12]{0:T(128)S(1)}, f32[12]{0:T(128)}, u32[]{:S(2)}) copy-start(f32[12]{0:T(128)} %param.12) | copy-start | bytes 148
  68.2 11.1 %copy-start.7 = (bf16[3,3,128,128]{3,2,1,0:T(8,128)(2,1)S(1)}, bf16[3,3,128,128]{3,2,1,0:T(8,128)(2,1)}, u32[]{:S(2)}) copy-start(bf16[3,3,128,128]{3,2,1,0:T(8,128)(2,1)} %param.9) | copy-start | bytes 884740
  68.2 11.1 %copy-start.8 = (f32[128]{0:T(128)S(1)}, f32[128]{0:T(128)}, u32[]{:S(2)}) copy-start(f32[128]{0:T(128)} %param.10) | copy-start | bytes 1540
  195.7 7.8 %copy-start.2 = (f32[6,8,16,128]{3,1,2,0:T(8,128)}, f32[6,8,16,128]{3,1,2,0:T(8,128)S(1)}, u32[]{:S(2)}) copy-start(f32[6,8,16,128]{3,1,2,0:T(8,128)S(1)} %get-tuple-element.120) | copy-start | bytes 1179652
  195.8 6.8 %collective-permute-start.8 = (f32[6,8,1,128]{3,1,2,0:T(8,128)S(1)}, f32[6,8,1,128]{3,1,2,0:T(8,128)S(1)}, u32[]{:S(2)}, u32[]{:S(2)}) collective-permute-start(f32[6,8,1,128]{3,1,2,0:T(8,128)S(1)} %get-tuple-element.142), channel_id=1, source_target_pairs={{0,4},{4,8},{8,12},{12,16},{16,20},{20,24},{24,28},{28,0},{1,5},{5... | collective-permute-start | bytes 73736 | tf_op jit(solution)/shard_map/ppermute | solution.py:19
  198.0 4.6 %collective-permute-start.9 = (f32[6,8,1,128]{3,1,2,0:T(8,128)S(1)}, f32[6,8,1,128]{3,1,2,0:T(8,128)S(1)}, u32[]{:S(2)}, u32[]{:S(2)}) collective-permute-start(f32[6,8,1,128]{3,1,2,0:T(8,128)S(1)} %get-tuple-element.143), channel_id=1, source_target_pairs={{4,0},{8,4},{12,8},{16,12},{20,16},{24,20},{28,24},{0,28},{5,1},{9... | collective-permute-start | bytes 73736 | tf_op jit(solution)/shard_map/ppermute | solution.py:22
  204.9 2.8 %collective-permute-start.10 = (f32[6,8,18,1]{2,1,3,0:T(8,128)S(1)}, f32[6,8,18,1]{2,1,3,0:T(8,128)S(1)}, u32[]{:S(2)}, u32[]{:S(2)}) collective-permute-start(f32[6,8,18,1]{2,1,3,0:T(8,128)S(1)} %copy.119), channel_id=1, source_target_pairs={{0,1},{1,2},{2,3},{3,0},{4,5},{5,6},{6,7},{7,4},{8,9},{9,10},{10,1... | collective-permute-start | bytes 10376 | tf_op jit(solution)/shard_map/ppermute | solution.py:19
  207.6 3.6 %collective-permute-start.11 = (f32[6,8,18,1]{2,1,3,0:T(8,128)}, f32[6,8,18,1]{2,1,3,0:T(8,128)}, u32[]{:S(2)}, u32[]{:S(2)}) collective-permute-start(f32[6,8,18,1]{2,1,3,0:T(8,128)} %copy.120), channel_id=1, source_target_pairs={{1,0},{2,1},{3,2},{0,3},{5,4},{6,5},{7,6},{4,7},{9,8},{10,9},{11,1... | collective-permute-start | bytes 10376 | tf_op jit(solution)/shard_map/ppermute | solution.py:22
  215.2 5.5 %collective-permute-start.12 = (f32[6,8,1,128]{3,1,2,0:T(8,128)S(1)}, f32[6,8,1,128]{3,1,2,0:T(8,128)S(1)}, u32[]{:S(2)}, u32[]{:S(2)}) collective-permute-start(f32[6,8,1,128]{3,1,2,0:T(8,128)S(1)} %get-tuple-element.140), channel_id=1, source_target_pairs={{0,4},{4,8},{8,12},{12,16},{16,20},{20,24},{24,28},{28,0},{1,5},{5... | collective-permute-start | bytes 73736 | tf_op jit(solution)/shard_map/ppermute | solution.py:19
  215.2 5.5 %collective-permute-start.13 = (f32[6,8,1,128]{3,1,2,0:T(8,128)S(1)}, f32[6,8,1,128]{3,1,2,0:T(8,128)S(1)}, u32[]{:S(2)}, u32[]{:S(2)}) collective-permute-start(f32[6,8,1,128]{3,1,2,0:T(8,128)S(1)} %get-tuple-element.141), channel_id=1, source_target_pairs={{4,0},{8,4},{12,8},{16,12},{20,16},{24,20},{28,24},{0,28},{5,1},{9... | collective-permute-start | bytes 73736 | tf_op jit(solution)/shard_map/ppermute | solution.py:22
  223.2 2.4 collective-permute-start.14
  225.6 3.3 %collective-permute-start.15 = (f32[6,8,18,1]{2,1,3,0:T(8,128)S(1)}, f32[6,8,18,1]{2,1,3,0:T(8,128)S(1)}, u32[]{:S(2)}, u32[]{:S(2)}) collective-permute-start(f32[6,8,18,1]{2,1,3,0:T(8,128)S(1)} %copy.122), channel_id=1, source_target_pairs={{1,0},{2,1},{3,2},{0,3},{5,4},{6,5},{7,6},{4,7},{9,8},{10,9},{11,1... | collective-permute-start | bytes 10376 | tf_op jit(solution)/shard_map/ppermute | solution.py:22
  233.0 5.7 %collective-permute-start.16 = (f32[6,8,1,128]{3,1,2,0:T(8,128)S(1)}, f32[6,8,1,128]{3,1,2,0:T(8,128)S(1)}, u32[]{:S(2)}, u32[]{:S(2)}) collective-permute-start(f32[6,8,1,128]{3,1,2,0:T(8,128)S(1)} %get-tuple-element.138), channel_id=1, source_target_pairs={{0,4},{4,8},{8,12},{12,16},{16,20},{20,24},{24,28},{28,0},{1,5},{5... | collective-permute-start | bytes 73736 | tf_op jit(solution)/shard_map/ppermute | solution.py:19
  233.0 5.7 %collective-permute-start.17 = (f32[6,8,1,128]{3,1,2,0:T(8,128)S(1)}, f32[6,8,1,128]{3,1,2,0:T(8,128)S(1)}, u32[]{:S(2)}, u32[]{:S(2)}) collective-permute-start(f32[6,8,1,128]{3,1,2,0:T(8,128)S(1)} %get-tuple-element.139), channel_id=1, source_target_pairs={{4,0},{8,4},{12,8},{16,12},{20,16},{24,20},{28,24},{0,28},{5,1},{9... | collective-permute-start | bytes 73736 | tf_op jit(solution)/shard_map/ppermute | solution.py:22
  241.0 4.2 %collective-permute-start.18 = (f32[6,8,18,1]{2,1,3,0:T(8,128)S(1)}, f32[6,8,18,1]{2,1,3,0:T(8,128)S(1)}, u32[]{:S(2)}, u32[]{:S(2)}) collective-permute-start(f32[6,8,18,1]{2,1,3,0:T(8,128)S(1)} %copy.123), channel_id=1, source_target_pairs={{0,1},{1,2},{2,3},{3,0},{4,5},{5,6},{6,7},{7,4},{8,9},{9,10},{10,1... | collective-permute-start | bytes 10376 | tf_op jit(solution)/shard_map/ppermute | solution.py:19
  242.4 3.4 %collective-permute-start.19 = (f32[6,8,18,1]{2,1,3,0:T(8,128)S(1)}, f32[6,8,18,1]{2,1,3,0:T(8,128)}, u32[]{:S(2)}, u32[]{:S(2)}) collective-permute-start(f32[6,8,18,1]{2,1,3,0:T(8,128)S(1)} %copy.124), channel_id=1, source_target_pairs={{1,0},{2,1},{3,2},{0,3},{5,4},{6,5},{7,6},{4,7},{9,8},{10,9},{11,1... | collective-permute-start | bytes 10376 | tf_op jit(solution)/shard_map/ppermute | solution.py:22
where the time goes:
time: 252 us; the launch traced here: 250 us
  local copies, waits for them, and re-layouts  120 us (48%)
  waiting for transfers between devices  39 us (15%)
  starting transfers between devices  32 us (13%)
  matrix products  31.2 us (12%)
  other arithmetic  26.1 us (10%)
    dynamic_update_slice x16, local copies, waits for them, and re-layouts, body(): wide = jnp.transpose(lax.map(level, padded), (1, 0, 2, 3))  47 us
    ppermute x10, waiting for transfers between devices, padded_2(): lax.ppermute(lax.slice_in_dim(block, block.shape[dim] - width, None, axis...  31.3 us
    dot_general x16, matrix products, conv_block(): jnp.einsum('tcxy,tco->oxy', taps, stacked, preferred_element_type=jnp.flo...  31.2 us
    while x128, local copies, waits for them, and re-layouts  20.9 us
    ppermute x10, starting transfers between devices, padded_2(): lax.ppermute(lax.slice_in_dim(block, 0, width, axis=dim), axis, backward)  19.5 us
    unnamed x30, local copies, waits for them, and re-layouts  18 us
    ppermute x10, starting transfers between devices, padded_2(): lax.ppermute(lax.slice_in_dim(block, block.shape[dim] - width, None, axis...  12.6 us
    squeeze x8, local copies, waits for them, and re-layouts, body(): wide = jnp.transpose(lax.map(level, padded), (1, 0, 2, 3))  9.44 us
  transfers between devices with their start and end apart: 20, of which 9 were waited for; matrix products, arithmetic and copies ran while one was open for 10% of the time, Pallas kernels for 0%

commit v1 on v0

v1 whole, which is shorter than its diff:
```python
import functools
import math

import jax
import jax.numpy as jnp
from jax import lax
from jax.experimental import pallas as pl
from jax.experimental.pallas import tpu as pltpu
from jax.sharding import PartitionSpec as P

time_step = 0.5
speed_cap = 0.6
cos_floor = 0.5

SIDE = 8
WIDE = 128
REACH = 4
VG = 8
VMEM_LIMIT = 40 * 2**20


def swap_pairs(count, first, closed):
    pairs = []
    for low in range(first, count, 2):
        high = low + 1
        if high >= count and not closed:
            continue
        pairs += [(low, high % count), (high % count, low)]
    return pairs


def swap(block, axis, first, closed):
    return lax.ppermute(block, axis, swap_pairs(lax.axis_size(axis), first, closed))


def exchange(low_edge, high_edge, axis, closed):
    even = lax.axis_index(axis) % 2 == 0
    got_a = swap(jnp.where(even, high_edge, low_edge), axis, 0, closed)
    got_b = swap(jnp.where(even, low_edge, high_edge), axis, 1, closed)
    before = jnp.where(even, got_b, got_a)
    after = jnp.where(even, got_a, got_b)
    return before, after


def turn_kernel(x_ref, g_ref, s_ref):
    rows = x_ref.shape[2]
    chans = x_ref.shape[1]
    s_ref[...] = x_ref[0].astype(jnp.float32).reshape(chans * rows, x_ref.shape[3])
    for row in range(rows):
        g_ref[0, row] = s_ref[pl.ds(row, chans, stride=rows), :].T.astype(jnp.bfloat16)


def turn(block):
    lev, ch, rows, cols = block.shape
    return pl.pallas_call(
        turn_kernel,
        grid=(lev,),
        in_specs=[pl.BlockSpec((1, ch, rows, cols), lambda i: (i, 0, 0, 0))],
        out_specs=pl.BlockSpec((1, rows, cols, ch), lambda i: (i, 0, 0, 0)),
        out_shape=jax.ShapeDtypeStruct((lev, rows, cols, ch), jnp.bfloat16),
        scratch_shapes=[pltpu.VMEM((ch * rows, cols), jnp.float32)],
        compiler_params=pltpu.CompilerParams(vmem_limit_bytes=VMEM_LIMIT),
    )(block)


def silu(s):
    return s / (1.0 + jnp.exp(-s))


def lay_row(e_ref, s_ref, slot, main, right, left):
    cols = main.shape[0]
    ext = cols + 2 * SIDE
    main = main.astype(jnp.float32)
    left = left.astype(jnp.float32)
    e_ref[slot, 0:SIDE] = left
    e_ref[slot, SIDE : SIDE + cols] = main
    e_ref[slot, SIDE + cols : 2 * SIDE + cols] = right.astype(jnp.float32)
    e_ref[slot, 2 * SIDE + cols : 3 * SIDE + cols] = left
    e_ref[slot, 3 * SIDE + cols : 4 * SIDE + cols] = main[0:SIDE]
    ch = main.shape[1]
    for b in range(3):
        s_ref[slot, :, b * ch : (b + 1) * ch] = e_ref[slot, pl.ds(SIDE - 1 + b, ext), :].astype(jnp.bfloat16)


def spread_row(hid, w2_ref, q_ref, qm_ref, row, cols):
    part = lax.dot_general(w2_ref[...], hid[0:cols], (((1,), (1,)), ((), ())), preferred_element_type=jnp.float32)
    marg = lax.dot_general(w2_ref[...], hid[cols:], (((1,), (1,)), ((), ())), preferred_element_type=jnp.float32)
    for a in range(3):
        at = row + 2 - a
        q_ref[at] += part[a * 6 * VG : (a + 1) * 6 * VG]
        qm_ref[at, :, 0 : 2 * SIDE] += marg[a * 6 * VG : (a + 1) * 6 * VG]


def col_before(main, marg):
    lane = lax.broadcasted_iota(jnp.int32, main.shape, main.ndim - 1)
    ax = main.ndim - 1
    turned = pltpu.roll(main, 1, ax)
    new_main = jnp.where(lane == 0, pltpu.roll(marg, WIDE - (2 * SIDE - 1), ax), turned)
    new_marg = jnp.where(lane == 0, turned, pltpu.roll(marg, 1, ax))
    return new_main, new_marg


def col_after(main, marg):
    lane = lax.broadcasted_iota(jnp.int32, main.shape, main.ndim - 1)
    ax = main.ndim - 1
    moved = pltpu.roll(marg, WIDE - 1, ax)
    new_main = jnp.where(lane == WIDE - 1, moved, pltpu.roll(main, WIDE - 1, ax))
    new_marg = jnp.where(lane == 2 * SIDE - 1, pltpu.roll(main, 2 * SIDE - 1, ax), moved)
    return new_main, new_marg


def join_cols(q_ref, qm_ref, at):
    vg = 2 * VG
    before = col_before(q_ref[at, 0:vg], qm_ref[at, 0:vg])
    after = col_after(q_ref[at, 2 * vg : 3 * vg], qm_ref[at, 2 * vg : 3 * vg])
    main = before[0] + q_ref[at, vg : 2 * vg] + after[0]
    marg = before[1] + qm_ref[at, vg : 2 * vg] + after[1]
    return main, marg


def inner_kernel(g_ref, r_ref, l_ref, w1_ref, w2_ref, b1_ref, keep_ref, ps_ref, pm_ref, e_ref, s_ref, q_ref, qm_ref):
    rows, cols, ch = g_ref.shape[1:]
    q_ref[...] = jnp.zeros_like(q_ref)
    qm_ref[...] = jnp.zeros_like(qm_ref)
    for row in range(rows):
        lay_row(e_ref, s_ref, row, g_ref[0, row], r_ref[0, row], l_ref[0, row])
    for row in range(1, rows - 1, 2):
        lhs = jnp.concatenate([s_ref[row - 1 + r] for r in range(4)], axis=1)
        acc = jnp.dot(lhs, w1_ref[...], preferred_element_type=jnp.float32) + b1_ref[...]
        hid = (silu(acc) * keep_ref[...]).astype(jnp.bfloat16)
        spread_row(hid[:, 0:ch], w2_ref, q_ref, qm_ref, row, cols)
        spread_row(hid[:, ch:], w2_ref, q_ref, qm_ref, row + 1, cols)
    for at in range(rows + 2):
        ps_ref[0, at], pm_ref[0, at] = join_cols(q_ref, qm_ref, at)


def edge_kernel(even_ref, g0_ref, g1_ref, r0_ref, r1_ref, l0_ref, l1_ref, a_ref, b_ref, w1_ref, w2_ref, b1_ref, keep_ref,
                pi_ref, pmi_ref, ps_ref, pm_ref, outa_ref, outb_ref, e_ref, s_ref, q_ref, qm_ref):
    cols, ch = g0_ref.shape[2:]
    rows = ps_ref.shape[1] - 2
    ext = cols + 2 * SIDE
    even = even_ref[0] == 0
    got_a = a_ref[0].astype(jnp.float32)
    got_b = b_ref[0].astype(jnp.float32)
    low = jnp.where(even, got_b, got_a)
    high = jnp.where(even, got_a, got_b)
    q_ref[...] = jnp.zeros_like(q_ref)
    qm_ref[...] = jnp.zeros_like(qm_ref)
    lay_row(e_ref, s_ref, 0, low[0:cols], low[cols : cols + SIDE], low[cols + SIDE : ext])
    lay_row(e_ref, s_ref, 5, high[0:cols], high[cols : cols + SIDE], high[cols + SIDE : ext])
    for k in range(2):
        lay_row(e_ref, s_ref, 1 + k, g0_ref[0, k], r0_ref[0, k], l0_ref[0, k])
        lay_row(e_ref, s_ref, 3 + k, g1_ref[0, k], r1_ref[0, k], l1_ref[0, k])
    for k in range(2):
        lhs = jnp.concatenate([s_ref[3 * k + r] for r in range(3)], axis=1)
        acc = jnp.dot(lhs, w1_ref[...], preferred_element_type=jnp.float32) + b1_ref[...]
        hid = (silu(acc) * keep_ref[...]).astype(jnp.bfloat16)
        spread_row(hid, w2_ref, q_ref, qm_ref, 3 * k, cols)
    ps_ref[...] = pi_ref[...]
    pm_ref[...] = pmi_ref[...]
    for at in range(6):
        main, marg = join_cols(q_ref, qm_ref, at)
        to = at if at < 3 else rows - 4 + at
        ps_ref[0, to] += main
        pm_ref[0, to] += marg

    def packed(start, skip):
        mains, slots = [], []
        for r in range(REACH + 1):
            for part in range(2):
                if (r, part) == (skip, 1):
                    continue
                mains.append(ps_ref[0, start + r, part * VG : (part + 1) * VG])
                slots.append(pm_ref[0, start + r, part * VG : (part + 1) * VG])
        lane = lax.broadcasted_iota(jnp.int32, (VG, WIDE), 1)
        tail = []
        for first in range(0, len(slots), WIDE // (2 * SIDE)):
            out = jnp.zeros((VG, WIDE), jnp.float32)
            for k, slot in enumerate(slots[first : first + WIDE // (2 * SIDE)]):
                moved = pltpu.roll(slot, k * 2 * SIDE, 1) if k else slot
                out = jnp.where(lane // (2 * SIDE) == k, moved, out)
            tail.append(out)
        return jnp.concatenate(mains + tail, axis=0)

    high_out = packed(rows + 1 - REACH, 0)
    low_out = packed(0, REACH)
    pad = jnp.zeros((outa_ref.shape[1] - high_out.shape[0], WIDE), jnp.float32)
    high_out = jnp.concatenate([high_out, pad], axis=0)
    low_out = jnp.concatenate([low_out, pad], axis=0)
    outa_ref[0] = jnp.where(even, high_out, low_out).astype(jnp.bfloat16)
    outb_ref[0] = jnp.where(even, low_out, high_out).astype(jnp.bfloat16)


HALVES = 2 * (REACH + 1) - 1
TAILS = -(-HALVES // (WIDE // (2 * SIDE)))
WIRE = -(-(HALVES + TAILS) * VG // 16) * 16


def unpack_wire(wire, skip):
    mains, margs = [], []
    k = 0
    zero = jnp.zeros((VG, WIDE), jnp.float32)
    per = WIDE // (2 * SIDE)
    for r in range(REACH + 1):
        main_row, marg_row = [], []
        for part in range(2):
            if (r, part) == (skip, 1):
                main_row.append(zero)
                marg_row.append(zero)
                continue
            main_row.append(wire[k * VG : (k + 1) * VG])
            tail = wire[(HALVES + k // per) * VG : (HALVES + k // per + 1) * VG]
            shift = (k % per) * 2 * SIDE
            marg_row.append(pltpu.roll(tail, WIDE - shift, 1) if shift else tail)
            k += 1
        mains.append(jnp.concatenate(main_row, axis=0))
        margs.append(jnp.concatenate(marg_row, axis=0))
    return mains, margs


def advect_kernel(even_ref, ps_ref, pm_ref, a_ref, b_ref, st_ref, slo_ref, shi_ref, sm_ref, b2_ref, lat_ref, latm_ref,
                  vel_ref, ten_ref, st8_ref, out_ref):
    nvar = st_ref.shape[0]
    rows = st_ref.shape[2]
    even = even_ref[0] == 0
    got_a = a_ref[0].astype(jnp.float32)
    got_b = b_ref[0].astype(jnp.float32)
    lo_main, lo_marg = unpack_wire(jnp.where(even, got_b, got_a), 0)
    hi_main, hi_marg = unpack_wire(jnp.where(even, got_a, got_b), REACH)
    main = lo_main[0:REACH] + [ps_ref[0, 1 + r] for r in range(rows)] + hi_main[1:]
    marg = lo_marg[0:REACH] + [pm_ref[0, 1 + r] for r in range(rows)] + hi_marg[1:]
    for stack, own, lo, hi in ((main, ps_ref, lo_main, hi_main), (marg, pm_ref, lo_marg, hi_marg)):
        stack[REACH - 1] += own[0, 0]
        stack[REACH] += lo[REACH]
        stack[REACH + rows - 1] += hi[0]
        stack[REACH + rows] += own[0, rows + 1]
    bias = b2_ref[...]
    total = rows + 2 * REACH
    main = speed_cap * jnp.tanh(jnp.stack(main) + bias)
    marg = speed_cap * jnp.tanh(jnp.stack(marg) + bias) * latm_ref[2:3]
    for part in range(2):
        out_ref[...] = main[REACH : REACH + rows, part * VG : (part + 1) * VG].reshape(rows * VG, WIDE)
        for n in range(nvar):
            vel_ref[2 * n + part, 0] = out_ref[pl.ds(n, rows, stride=VG), :]
    for n in range(nvar):
        st8_ref[0, pl.ds(n, REACH, stride=VG), :] = slo_ref[n, 0]
        st8_ref[0, pl.ds(REACH * VG + n, rows, stride=VG), :] = st_ref[n, 0]
        st8_ref[0, pl.ds((REACH + rows) * VG + n, REACH, stride=VG), :] = shi_ref[n, 0]
        st8_ref[1, pl.ds(n, total, stride=VG), 0 : 2 * SIDE] = sm_ref[n, 0]
    start = [st8_ref[0].reshape(total, VG, WIDE), st8_ref[1].reshape(total, VG, WIDE)]
    cosine = [lat_ref[0:1], latm_ref[0:1]]
    metric = [lat_ref[1:2], latm_ref[1:2]]
    u = [main[:, 0:VG], marg[:, 0:VG]]
    v = [main[1:-1, VG:], marg[1:-1, VG:]]
    flux = [v[k] * cosine[k] for k in range(2)]
    fb = col_before(*flux)
    fa = col_after(*flux)
    coef = []
    for k in range(2):
        div = metric[k] * ((u[k][2:] - u[k][:-2]) * 0.5 + (fa[k] - fb[k]) * 0.5)
        mid = u[k][1:-1]
        cl = metric[k] * jnp.maximum(mid, 0.0)
        cr = -metric[k] * jnp.minimum(mid, 0.0)
        cd = jnp.maximum(v[k], 0.0)
        cu = -jnp.minimum(v[k], 0.0)
        coef.append((-(cl + cr + cd + cu + div), cl, cr, cd, cu))

    def rate(q, depth):
        lo = depth - 1
        hi = total - 2 - lo
        mid = [f[1:-1] for f in q]
        qb = col_before(*mid)
        qa = col_after(*mid)
        out = []
        for k in range(2):
            c0, cl, cr, cd, cu = (c[lo:hi] for c in coef[k])
            out.append(c0 * mid[k] + cl * q[k][:-2] + cr * q[k][2:] + cd * qb[k] + cu * qa[k])
        return out

    one = rate(start, 1)
    two = rate([start[k][1:-1] + 0.5 * time_step * one[k] for k in range(2)], 2)
    three = rate([start[k][2:-2] + 0.5 * time_step * two[k] for k in range(2)], 3)
    four = rate([start[k][3:-3] + time_step * three[k] for k in range(2)], 4)
    ten = (one[0][3:-3] + 2.0 * two[0][2:-2] + 2.0 * three[0][1:-1] + four[0]) / 6.0
    out_ref[...] = ten.reshape(rows * VG, WIDE)
    for n in range(nvar):
        ten_ref[n, 0] = out_ref[pl.ds(n, rows, stride=VG), :]


def full(shape):
    return pl.BlockSpec(shape, lambda *i: (0,) * len(shape))


def per_level(shape):
    return pl.BlockSpec((1,) + shape[1:], lambda i: (i,) + (0,) * (len(shape) - 1))


def body(hidden_in, w_conv1, b_conv1, w_conv2, b_conv2, state):
    lev, ch, rows, cols = hidden_in.shape
    nvar = state.shape[0]
    ext = cols + 2 * SIDE
    f32 = jnp.float32
    params = pltpu.CompilerParams(vmem_limit_bytes=VMEM_LIMIT)
    smem = pl.BlockSpec(memory_space=pltpu.SMEM)

    taps = w_conv1.reshape(3, 3 * ch, ch)
    none = jnp.zeros_like(taps[0])
    w1_pair = jnp.concatenate(
        [
            jnp.concatenate([taps[0], taps[1], taps[2], none], axis=0),
            jnp.concatenate([none, taps[0], taps[1], taps[2]], axis=0),
        ],
        axis=1,
    )
    w1_one = taps.reshape(9 * ch, ch)
    w2 = w_conv2.reshape(3, 3, ch, nvar, 2).transpose(0, 1, 4, 3, 2)
    w2 = jnp.pad(w2, ((0, 0), (0, 0), (0, 0), (0, VG - nvar), (0, 0))).reshape(18 * VG, ch)
    b1 = b_conv1.reshape(1, ch)
    b2 = jnp.pad(b_conv2.reshape(nvar, 2).T, ((0, 0), (0, VG - nvar))).reshape(2 * VG, 1)
    b2 = jnp.broadcast_to(b2, (2 * VG, WIDE))

    n_lat = cols * lax.axis_size("lat")
    place = jnp.concatenate([jnp.arange(cols + SIDE), jnp.arange(-SIDE, 0)]).astype(jnp.int32)
    place = place + lax.axis_index("lat") * cols
    keep = ((place >= 0) & (place < n_lat)).astype(f32)
    phi = (place.astype(f32) + 0.5) * (math.pi / n_lat) - 0.5 * math.pi
    cosine = jnp.maximum(jnp.cos(phi), cos_floor)
    table = jnp.stack([cosine, 1.0 / cosine, keep])
    table = jnp.pad(table, ((0, VG - 3), (0, 0)))
    lat_main = table[:, 0:cols]
    lat_marg = jnp.pad(table[:, cols:], ((0, 0), (0, WIDE - 2 * SIDE)))
    keep_col = keep.reshape(ext, 1)
    even = (lax.axis_index("lon") % 2).astype(jnp.int32).reshape(1)

    before, after = exchange(state[..., 0:SIDE], state[..., cols - SIDE :], "lat", False)
    marg = jnp.concatenate([after, before], axis=-1)
    wide = jnp.concatenate([state, marg], axis=-1)
    lo, hi = exchange(
        wide[:, :, 0:REACH].reshape(-1, WIDE), wide[:, :, rows - REACH :].reshape(-1, WIDE), "lon", True
    )
    lo = lo.reshape(nvar, lev, REACH, ext)
    hi = hi.reshape(nvar, lev, REACH, ext)
    state_marg = jnp.concatenate([lo[..., cols:], marg, hi[..., cols:]], axis=2)
    state_lo = lo[..., 0:cols]
    state_hi = hi[..., 0:cols]

    g = turn(hidden_in)
    left, right = exchange(g[:, :, 0:SIDE], g[:, :, cols - SIDE :], "lat", False)
    row_lo = jnp.concatenate([g[:, 0], right[:, 0], left[:, 0]], axis=1)
    row_hi = jnp.concatenate([g[:, -1], right[:, -1], left[:, -1]], axis=1)
    is_even = lax.axis_index("lon") % 2 == 0
    got_a = swap(jnp.where(is_even, row_hi, row_lo), "lon", 0, True)
    got_b = swap(jnp.where(is_even, row_lo, row_hi), "lon", 1, True)

    ps_shape = (lev, rows + 2, 2 * VG, WIDE)
    ps_out = jax.ShapeDtypeStruct(ps_shape, f32)
    ps, pm = pl.pallas_call(
        inner_kernel,
        grid=(lev,),
        in_specs=[
            per_level(g.shape),
            per_level(right.shape),
            per_level(left.shape),
            full(w1_pair.shape),
            full(w2.shape),
            full((1, 2 * ch)),
            full((ext, 1)),
        ],
        out_specs=[per_level(ps_shape)] * 2,
        out_shape=[ps_out] * 2,
        scratch_shapes=[
            pltpu.VMEM((rows, ext + 2 * SIDE, ch), f32),
            pltpu.VMEM((rows, ext, 3 * ch), jnp.bfloat16),
            pltpu.VMEM((rows + 2, 6 * VG, WIDE), f32),
            pltpu.VMEM((rows + 2, 6 * VG, WIDE), f32),
        ],
        compiler_params=params,
        cost_estimate=pl.CostEstimate(flops=2 * lev * rows * ext * 9 * ch * ch, bytes_accessed=8 * 2**20, transcendentals=0),
    )(g, right, left, w1_pair, w2, jnp.concatenate([b1, b1], axis=1), keep_col)

    def pair_of(first):
        return lambda i: (i, first, 0, 0)

    g_pair = (1, 2, cols, ch)
    s_pair = (1, 2, SIDE, ch)
    top = rows // 2 - 1
    wire_shape = (lev, WIRE, WIDE)
    wire_out = jax.ShapeDtypeStruct(wire_shape, jnp.bfloat16)
    ps, pm, send_a, send_b = pl.pallas_call(
        edge_kernel,
        grid=(lev,),
        in_specs=[
            smem,
            pl.BlockSpec(g_pair, pair_of(0)),
            pl.BlockSpec(g_pair, pair_of(top)),
            pl.BlockSpec(s_pair, pair_of(0)),
            pl.BlockSpec(s_pair, pair_of(top)),
            pl.BlockSpec(s_pair, pair_of(0)),
            pl.BlockSpec(s_pair, pair_of(top)),
            per_level(got_a.shape),
            per_level(got_b.shape),
            full(w1_one.shape),
            full(w2.shape),
            full((1, ch)),
            full((ext, 1)),
            per_level(ps_shape),
            per_level(ps_shape),
        ],
        out_specs=[per_level(ps_shape)] * 2 + [per_level(wire_shape)] * 2,
        out_shape=[ps_out] * 2 + [wire_out] * 2,
        scratch_shapes=[
            pltpu.VMEM((6, ext + 2 * SIDE, ch), f32),
            pltpu.VMEM((6, ext, 3 * ch), jnp.bfloat16),
            pltpu.VMEM((6, 6 * VG, WIDE), f32),
            pltpu.VMEM((6, 6 * VG, WIDE), f32),
        ],
        compiler_params=params,
    )(even, g, g, right, right, left, left, got_a, got_b, w1_one, w2, b1, keep_col, ps, pm)

    wire_a = swap(send_a, "lon", 0, True)
    wire_b = swap(send_b, "lon", 1, True)

    def var_level(shape):
        return pl.BlockSpec((shape[0], 1) + shape[2:], lambda i: (0, i, 0, 0))

    vel_shape = (2 * nvar, lev, rows, cols)
    total = rows + 2 * REACH
    return pl.pallas_call(
        advect_kernel,
        grid=(lev,),
        in_specs=[
            smem,
            per_level(ps_shape),
            per_level(ps_shape),
            per_level(wire_shape),
            per_level(wire_shape),
            var_level(state.shape),
            var_level(state_lo.shape),
            var_level(state_hi.shape),
            var_level(state_marg.shape),
            full(b2.shape),
            full(lat_main.shape),
            full(lat_marg.shape),
        ],
        out_specs=[var_level(vel_shape), var_level(state.shape)],
        out_shape=[jax.ShapeDtypeStruct(vel_shape, f32), jax.ShapeDtypeStruct(state.shape, f32)],
        scratch_shapes=[pltpu.VMEM((2, total * VG, WIDE), f32), pltpu.VMEM((rows * VG, WIDE), f32)],
        compiler_params=params,
    )(even, ps, pm, wire_a, wire_b, state, state_lo, state_hi, state_marg, b2, lat_main, lat_marg)


def solution(mesh):
    placed = (P(None, None, "lon", "lat"), P(), P(), P(), P(), P(None, None, "lon", "lat"))
    return jax.shard_map(
        body,
        mesh=mesh,
        in_specs=placed,
        out_specs=(P(None, None, "lon", "lat"), P(None, None, "lon", "lat")),
        check_vma=False,
    )
```

time: 252 us -> 99.1 us (0.39)
  local copies, waits for them, and re-layouts: 120 us -> 19 us
  Pallas kernels: 0 us -> 48.9 us
  waiting for transfers between devices: 39 us -> 4.69 us
  matrix products: 31.2 us -> 0 us
  other arithmetic: 26.1 us -> 9.43 us
  starting transfers between devices: 32 us -> 15.5 us
    pallas_call x0 -> x4, Pallas kernels: none -> 48.9 us  [the longest x1 29.4 us: body(): pl.pallas_call(inner_kernel, grid=(lev,), in_specs=[per_level(g.shape), p...]
    dynamic_update_slice x16 -> x0, local copies, waits for them, and re-layouts: 47 us -> none  [body(): wide = jnp.transpose(lax.map(level, padded), (1, 0, 2, 3))]
    ppermute x20 -> x10, waiting for transfers between devices: 39 us -> 4.69 us  [swap(): lax.ppermute(block, axis, swap_pairs(lax.axis_size(axis), first, closed))]
    dot_general x16 -> x0, matrix products: 31.2 us -> none  [conv_block(): jnp.einsum('tcxy,tco->oxy', taps, stacked, preferred_element_type=jnp.flo...]
    while x128 -> x0, local copies, waits for them, and re-layouts: 20.9 us -> none
    ppermute x20 -> x10, starting transfers between devices: 32 us -> 15.5 us  [swap(): lax.ppermute(block, axis, swap_pairs(lax.axis_size(axis), first, closed))]
    mul x14 -> x0, other arithmetic: 11.9 us -> none  [the longest x1 6.47 us: body(): padded = padded * lat_profile(in_width, lat_dev)[0].astype(jnp.bfloat16)]
    ppermute x10 -> x0, local copies, waits for them, and re-layouts: 11.4 us -> none  [the longest x5 6.74 us: padded_2(): lax.ppermute(lax.slice_in_dim(block, 0, width, axis=dim), axis, backward)]
  transfers between devices with their start and end apart: 20 -> 10, of which waited for: 9 -> 1; matrix products, arithmetic and copies ran while one was open for 10% -> 20% of each run, Pallas kernels for 0% -> 38%
where the time goes in v1:
time: 99.1 us; the launch traced here: 98.5 us
  Pallas kernels  48.9 us (49%)
  local copies, waits for them, and re-layouts  19 us (19%)
  starting transfers between devices  15.5 us (16%)
  other arithmetic  9.43 us (10%)
  waiting for transfers between devices  4.69 us (5%)
  between operations  1.04 us (1%)
    pallas_call x1, Pallas kernels, body(): pl.pallas_call(inner_kernel, grid=(lev,), in_specs=[per_level(g.shape), p...  29.4 us
    ppermute x10, starting transfers between devices, swap(): lax.ppermute(block, axis, swap_pairs(lax.axis_size(axis), first, closed))  15.5 us
    pallas_call x1, Pallas kernels, body(): pl.pallas_call(edge_kernel, grid=(lev,), in_specs=[smem, pl.BlockSpec(g_p...  8.41 us
    pallas_call x1, Pallas kernels, body(): pl.pallas_call(advect_kernel, grid=(lev,), in_specs=[smem, per_level(ps_s...  7.73 us
    unnamed x23, local copies, waits for them, and re-layouts  7.19 us
    ppermute x10, waiting for transfers between devices, swap(): lax.ppermute(block, axis, swap_pairs(lax.axis_size(axis), first, closed))  4.69 us
    pallas_call x1, Pallas kernels, turn(): pl.pallas_call(turn_kernel, grid=(lev,), in_specs=[pl.BlockSpec((1, ch, r...  3.31 us
    select_n x2, other arithmetic, exchange(): after = jnp.where(even, got_a, got_b)  2.8 us
  transfers between devices with their start and end apart: 10, of which 1 were waited for; matrix products, arithmetic and copies ran while one was open for 20% of the time, Pallas kernels for 38%

profile of v1, /device:TPU:1, one launch (start us, length us, event | category | flops | bytes accessed | tf_op | source)
XLA Modules:
  0.0 98.5 jit_solution(17953839148524961558)
XLA Ops:
  0.6 0.0 copy-start.3
  0.6 2.2 %copy-done.3 = bf16[8,128,16,128]{3,2,1,0:T(8,128)(2,1)S(1)} copy-done((bf16[8,128,16,128]{3,2,1,0:T(8,128)(2,1)S(1)}, bf16[8,128,16,128]{3,2,1,0:T(8,128)(2,1)}, u32[]{:S(2)}) %copy-start.3) | copy-done | bytes 4194328
  2.8 3.3 %shard_map.77.g_ref.g0_ref.g1_ref = bf16[8,16,128,128]{3,2,1,0:T(8,128)(2,1)S(1)} custom-call(bf16[8,128,16,128]{3,2,1,0:T(8,128)(2,1)S(1)} %copy-done.3), custom_call_target="tpu_custom_call" | custom-call | tf_op jit(solution)/shard_map/pallas_call | solution.py:55
  6.1 0.0 copy-start
  6.2 1.9 %copy-done = bf16[8,16,128,128]{3,2,1,0:T(8,128)(2,1)} copy-done((bf16[8,16,128,128]{3,2,1,0:T(8,128)(2,1)}, bf16[8,16,128,128]{3,2,1,0:T(8,128)(2,1)S(1)}, u32[]{:S(2)}) %copy-start) | copy-done | bytes 4194328
  8.1 1.1 %fusion.2 = (bf16[8,16,8,128]{3,2,1,0:T(8,128)(2,1)S(1)}, bf16[8,16,8,128]{3,2,1,0:T(8,128)(2,1)S(1)}) fusion(bf16[8,16,128,128]{3,2,1,0:T(8,128)(2,1)} %copy-done), kind=kLoop, calls=%fused_computation.41 | loop fusion | bytes 1048576 | tf_op jit(solution)/shard_map/slice | solution.py:348
  9.2 0.9 broadcast_select_fusion.4
  10.1 4.6 %collective-permute-start.1 = (bf16[8,16,8,128]{3,2,0,1:T(8,128)(2,1)}, bf16[8,16,8,128]{3,2,0,1:T(8,128)(2,1)}, u32[]{:S(2)}, u32[]{:S(2)}) collective-permute-start(bf16[8,16,8,128]{3,2,0,1:T(8,128)(2,1)} %get-tuple-element.30), channel_id=1, source_target_pairs={{1,2},{2,1},{5,6},{6,5},{9,10},{10,9},{13,14},{14,13},{17,18},{18,... | collective-permute-start | bytes 786440 | tf_op jit(solution)/shard_map/ppermute | solution.py:33
  14.7 0.1 collective-permute-start
  14.8 0.0 copy-done.2
  14.8 1.1 %slice_select_fusion.1 = (f32[6,8,16,8]{3,2,1,0:T(8,128)}, f32[6,8,16,8]{3,2,1,0:T(8,128)}) fusion(f32[6,8,16,128]{3,2,1,0:T(8,128)S(1)} %copy-done.2, pred[]{:T(512)S(6)} %eq.14), kind=kLoop, calls=%fused_computation.3 | loop fusion | flops 12288 | bytes 98305 | tf_op jit(solution)/shard_map/jit(_where)/select_n | solution.py:38
  15.9 0.5 collective-permute-start.6
  16.4 2.0 %collective-permute-start.7 = (f32[6,8,16,8]{3,2,1,0:T(8,128)}, f32[6,8,16,8]{3,2,1,0:T(8,128)}, u32[]{:S(2)}, u32[]{:S(2)}) collective-permute-start(f32[6,8,16,8]{3,2,1,0:T(8,128)} %get-tuple-element.33), channel_id=1, source_target_pairs={{1,2},{2,1},{5,6},{6,5},{9,10},{10,9},{13,14},{14,13},{17,18},{18,... | collective-permute-start | bytes 73736 | tf_op jit(solution)/shard_map/ppermute | solution.py:33
  18.4 1.1 %slice_bitcast_fusion.1 = (bf16[8,128,128]{2,1,0:T(8,128)(2,1)S(1)}, bf16[8,128,128]{2,1,0:T(8,128)(2,1)S(1)}) fusion(bf16[8,16,128,128]{3,2,1,0:T(8,128)(2,1)} %copy-done), kind=kLoop, calls=%fused_computation.9 | loop fusion | bytes 1048576 | tf_op jit(solution)/shard_map/squeeze | solution.py:350
  19.5 0.1 pad_add_fusion
  19.6 0.1 copy.52
  19.7 0.0 copy-done.4
  19.8 0.1 broadcast_divide_fusion
  20.0 0.1 maximum_maximum_fusion.w1_ref
  20.1 0.0 copy-done.9
  20.2 0.1 reshape.148
  20.3 0.1 copy.65
  20.4 0.1 broadcast_in_dim.11
  20.5 0.0 collective-permute-done.6
  20.5 0.7 copy-done.8
  21.3 4.7 %collective-permute-done.7 = f32[6,8,16,8]{3,2,1,0:T(8,128)} collective-permute-done((f32[6,8,16,8]{3,2,1,0:T(8,128)}, f32[6,8,16,8]{3,2,1,0:T(8,128)}, u32[]{:S(2)}, u32[]{:S(2)}) %collective-permute-start.7) | collective-permute-done | bytes 24608 | tf_op jit(solution)/shard_map/ppermute | solution.py:33
  25.9 1.2 %broadcast_select_fusion.7 = (f32[6,8,16,8]{3,2,1,0:T(8,128)S(1)}, f32[6,8,16,8]{3,2,1,0:T(8,128)S(1)}) fusion(f32[6,8,16,8]{3,2,1,0:T(8,128)} %copy-done.8, f32[6,8,16,8]{3,2,1,0:T(8,128)} %collective-permute-done.7, pred[]{:T(512)S(6)} %eq.14), kind=kLoop, calls=%fused_computation.18 | loop fusion | flops 12288 | bytes 98305 | tf_op jit(solution)/shard_map/jit(_where)/select_n | solution.py:41
  27.1 0.0 copy-start.6
  27.1 0.0 copy-start.7
  27.1 0.9 broadcast_select_fusion.8
  28.1 0.9 select_n.117
  28.9 1.2 %collective-permute-start.9 = (f32[216,128]{1,0:T(8,128)}, f32[216,128]{1,0:T(8,128)}, u32[]{:S(2)}, u32[]{:S(2)}) collective-permute-start(f32[216,128]{1,0:T(8,128)} %select_n.117), channel_id=1, source_target_pairs={{0,4},{4,0},{8,12},{12,8},{16,20},{20,16},{24,28},{28,24},{1,5},{5... | collective-permute-start | bytes 331784 | tf_op jit(solution)/shard_map/ppermute | solution.py:33
  30.1 1.0 broadcast_select_fusion.9
  31.1 0.9 select_n.115
  32.0 2.3 %collective-permute-start.8 = (f32[216,128]{1,0:T(8,128)}, f32[216,128]{1,0:T(8,128)S(1)}, u32[]{:S(2)}, u32[]{:S(2)}) collective-permute-start(f32[216,128]{1,0:T(8,128)} %select_n.115), channel_id=1, source_target_pairs={{4,8},{8,4},{12,16},{16,12},{20,24},{24,20},{28,0},{0,28},{5,9},{9... | collective-permute-start | bytes 331784 | tf_op jit(solution)/shard_map/ppermute | solution.py:33
  34.3 0.0 collective-permute-done.1
  34.3 0.0 collective-permute-done
  34.3 1.1 %broadcast_select_fusion.2 = (bf16[8,16,8,128]{3,2,0,1:T(8,128)(2,1)S(1)}, bf16[8,16,8,128]{3,2,0,1:T(8,128)(2,1)S(1)}) fusion(bf16[8,16,8,128]{3,2,0,1:T(8,128)(2,1)} %collective-permute-done.1, bf16[8,16,8,128]{3,2,0,1:T(8,128)(2,1)} %collective-permute-done, pred[]{:T(512)S(6)} %eq.14), kind=kLoop, calls=%fused_computation.10 | loop fusion | flops 262144 | bytes 1048577 | tf_op jit(solution)/shard_map/jit(_where)/select_n | solution.py:40
  35.5 0.1 broadcast_select_fusion
  35.6 0.2 collective-permute-start.2
  35.8 2.0 %collective-permute-start.3 = (bf16[8,144,128]{2,1,0:T(8,128)(2,1)S(1)}, bf16[8,144,128]{2,1,0:T(8,128)(2,1)S(1)}, u32[]{:S(2)}, u32[]{:S(2)}) collective-permute-start(bf16[8,144,128]{2,1,0:T(8,128)(2,1)S(1)} %get-tuple-element.26), channel_id=1, source_target_pairs={{4,8},{8,4},{12,16},{16,12},{20,24},{24,20},{28,0},{0,28},{5,9},{9... | collective-permute-start | bytes 884744 | tf_op jit(solution)/shard_map/ppermute | solution.py:33
  37.9 2.2 %copy-done.1 = bf16[8,16,128,128]{3,2,1,0:T(8,128)(2,1)S(1)} copy-done((bf16[8,16,128,128]{3,2,1,0:T(8,128)(2,1)S(1)}, bf16[8,16,128,128]{3,2,1,0:T(8,128)(2,1)}, u32[]{:S(2)}) %copy-start.1) | copy-done | bytes 4194328
  40.1 29.4 %shard_map.78 = (f32[8,18,16,128]{3,2,1,0:T(8,128)S(1)}, f32[8,18,16,128]{3,2,1,0:T(8,128)S(1)}) custom-call(bf16[8,16,128,128]{3,2,1,0:T(8,128)(2,1)S(1)} %copy-done.1, bf16[8,16,8,128]{3,2,1,0:T(8,128)(2,1)S(1)} %copy.56.r_ref.r0_ref.r1_ref, bf16[8,16,8,128]{3,2,1,0:T(8,128)(2,1)S(1)} %copy.58.l_ref.l0_ref.l1_ref, ...), custom_call_target="tpu_custom_call" | custom-call | flops 5435817984 | bytes 8388608 | tf_op jit(solution)/shard_map/pallas_call | solution.py:357
  69.5 0.0 copy-done.6
  69.5 0.0 copy-done.7
  69.5 0.0 collective-permute-done.2.a_ref
  69.5 0.0 collective-permute-done.3.b_ref
  69.6 8.4 %shard_map.79 = (f32[8,18,16,128]{3,2,1,0:T(8,128)S(1)}, f32[8,18,16,128]{3,2,1,0:T(8,128)S(1)}, bf16[8,96,128]{2,1,0:T(8,128)(2,1)}, bf16[8,96,128]{2,1,0:T(8,128)(2,1)S(1)}) custom-call(s32[1]{0:T(128)} %bitcast.even_ref, bf16[8,16,128,128]{3,2,1,0:T(8,128)(2,1)S(1)} %copy-done.1, bf16[8,16,128,128]{3,2,1,0:T(8,128)(2,1)S(1)} %copy-done.1, ...), custom_call_target="tpu_custom_call" | custom-call | tf_op jit(solution)/shard_map/pallas_call | solution.py:389
  78.0 0.5 collective-permute-start.4
  78.4 2.0 %collective-permute-start.5 = (bf16[8,96,128]{2,1,0:T(8,128)(2,1)S(1)}, bf16[8,96,128]{2,1,0:T(8,128)(2,1)S(1)}, u32[]{:S(2)}, u32[]{:S(2)}) collective-permute-start(bf16[8,96,128]{2,1,0:T(8,128)(2,1)S(1)} %get-tuple-element.13), channel_id=1, source_target_pairs={{4,8},{8,4},{12,16},{16,12},{20,24},{24,20},{28,0},{0,28},{5,9},{9... | collective-permute-start | bytes 589832 | tf_op jit(solution)/shard_map/ppermute | solution.py:33
  80.4 0.0 collective-permute-done.9
  80.4 0.0 collective-permute-done.8
  80.4 1.6 %broadcast_select_fusion.10 = (f32[216,128]{1,0:T(8,128)}, f32[216,128]{1,0:T(8,128)}) fusion(f32[216,128]{1,0:T(8,128)} %collective-permute-done.9, f32[216,128]{1,0:T(8,128)S(1)} %collective-permute-done.8, pred[]{:T(512)S(6)} %eq.15), kind=kLoop, calls=%fused_computation.22 | loop fusion | flops 55296 | bytes 442369 | tf_op jit(solution)/shard_map/jit(_where)/select_n | solution.py:41
  82.0 1.9 %reshape.147 = f32[6,8,4,144]{3,2,1,0:T(4,128)} reshape(f32[216,128]{1,0:T(8,128)} %get-tuple-element.41) | data formatting | bytes 221184 | tf_op jit(solution)/shard_map/reshape | solution.py:342
  83.9 0.9 slice.99.shi_ref
  84.8 0.9 slice.101
  85.7 1.9 %reshape.146 = f32[6,8,4,144]{3,2,1,0:T(4,128)} reshape(f32[216,128]{1,0:T(8,128)} %get-tuple-element.42) | data formatting | bytes 221184 | tf_op jit(solution)/shard_map/reshape | solution.py:341
  87.5 0.9 slice.98.slo_ref
  88.4 0.9 slice.100
  89.3 1.3 %pad_maximum_fusion.sm_ref = f32[6,8,24,16]{3,2,1,0:T(8,128)S(1)} fusion(f32[6,8,4,16]{3,2,1,0:T(4,128)S(1)} %slice.101, f32[6,8,16,8]{3,2,1,0:T(8,128)} %copy-done.7, f32[6,8,16,8]{3,2,1,0:T(8,128)} %copy-done.6, f32[6,8,4,16]{3,2,1,0:T(4,128)S(1)} %slice.100), kind=kLoop, calls=%fused_computation.1 | loop fusion | flops 55296 | bytes 147456 | tf_op jit(solution)/shard_map/concatenate | solution.py:343
  90.7 0.0 collective-permute-done.4.a_ref
  90.7 0.0 collective-permute-done.5.b_ref
  90.7 0.1 broadcast_in_dim.12.b2_ref
  90.8 7.7 %shard_map.80 = (f32[12,8,16,128]{3,2,1,0:T(8,128)}, f32[6,8,16,128]{3,2,1,0:T(8,128)}) custom-call(s32[1]{0:T(128)} %bitcast.even_ref, f32[8,18,16,128]{3,2,1,0:T(8,128)S(1)} %get-tuple-element.10.ps_ref, f32[8,18,16,128]{3,2,1,0:T(8,128)S(1)} %get-tuple-element.11.pm_ref, bf16[8,96,128]{2,1,0:T(8,128)(2,1)S(1)} %collective-permute-done.4.a_ref, ...), custom_call_target="tpu_custom_call" | custom-call | tf_op jit(solution)/shard_map/pallas_call | solution.py:428
  (29 shorter events, 0.3 us)
Async XLA Ops:
  0.6 2.2 %copy-start.3 = (bf16[8,128,16,128]{3,2,1,0:T(8,128)(2,1)S(1)}, bf16[8,128,16,128]{3,2,1,0:T(8,128)(2,1)}, u32[]{:S(2)}) copy-start(bf16[8,128,16,128]{3,2,1,0:T(8,128)(2,1)} %x_ref.1) | copy-start | bytes 12582916
  6.1 2.0 %copy-start = (bf16[8,16,128,128]{3,2,1,0:T(8,128)(2,1)}, bf16[8,16,128,128]{3,2,1,0:T(8,128)(2,1)S(1)}, u32[]{:S(2)}) copy-start(bf16[8,16,128,128]{3,2,1,0:T(8,128)(2,1)S(1)} %shard_map.77.g_ref.g0_ref.g1_ref) | copy-start | bytes 12582916
  8.1 6.7 %copy-start.2 = (f32[6,8,16,128]{3,2,1,0:T(8,128)S(1)}, f32[6,8,16,128]{3,2,1,0:T(8,128)}, u32[]{:S(2)}) copy-start(f32[6,8,16,128]{3,2,1,0:T(8,128)} %st_ref.1) | copy-start | bytes 1179652
  10.1 9.6 %copy-start.4 = (bf16[3,3,128,128]{3,2,1,0:T(8,128)(2,1)S(1)}, bf16[3,3,128,128]{3,2,1,0:T(8,128)(2,1)}, u32[]{:S(2)}) copy-start(bf16[3,3,128,128]{3,2,1,0:T(8,128)(2,1)} %param.7) | copy-start | bytes 884740
  10.1 24.2 %collective-permute-start.1 = (bf16[8,16,8,128]{3,2,0,1:T(8,128)(2,1)}, bf16[8,16,8,128]{3,2,0,1:T(8,128)(2,1)}, u32[]{:S(2)}, u32[]{:S(2)}) collective-permute-start(bf16[8,16,8,128]{3,2,0,1:T(8,128)(2,1)} %get-tuple-element.30), channel_id=1, source_target_pairs={{1,2},{2,1},{5,6},{6,5},{9,10},{10,9},{13,14},{14,13},{17,18},{18,... | collective-permute-start | bytes 786440 | tf_op jit(solution)/shard_map/ppermute | solution.py:33
  14.7 19.6 %collective-permute-start = (bf16[8,16,8,128]{3,2,0,1:T(8,128)(2,1)}, bf16[8,16,8,128]{3,2,0,1:T(8,128)(2,1)}, u32[]{:S(2)}, u32[]{:S(2)}) collective-permute-start(bf16[8,16,8,128]{3,2,0,1:T(8,128)(2,1)} %get-tuple-element.31), channel_id=1, source_target_pairs={{0,1},{1,0},{2,3},{3,2},{4,5},{5,4},{6,7},{7,6},{8,9},{9,8},{10,11... | collective-permute-start | bytes 786440 | tf_op jit(solution)/shard_map/ppermute | solution.py:33
  15.9 4.6 %collective-permute-start.6 = (f32[6,8,16,8]{3,2,1,0:T(8,128)}, f32[6,8,16,8]{3,2,1,0:T(8,128)S(1)}, u32[]{:S(2)}, u32[]{:S(2)}) collective-permute-start(f32[6,8,16,8]{3,2,1,0:T(8,128)} %get-tuple-element.32), channel_id=1, source_target_pairs={{0,1},{1,0},{2,3},{3,2},{4,5},{5,4},{6,7},{7,6},{8,9},{9,8},{10,11... | collective-permute-start | bytes 73736 | tf_op jit(solution)/shard_map/ppermute | solution.py:33
  16.4 3.7 %copy-start.5 = (f32[128]{0:T(128)S(1)}, f32[128]{0:T(128)}, u32[]{:S(2)}) copy-start(f32[128]{0:T(128)} %param.8) | copy-start | bytes 1540
  16.4 3.7 %copy-start.9 = (bf16[3,3,128,12]{2,3,1,0:T(8,128)(2,1)S(1)}, bf16[3,3,128,12]{2,3,1,0:T(8,128)(2,1)}, u32[]{:S(2)}) copy-start(bf16[3,3,128,12]{2,3,1,0:T(8,128)(2,1)} %param.9) | copy-start | bytes 82948
  16.4 3.8 %copy-start.10 = (f32[12]{0:T(128)S(1)}, f32[12]{0:T(128)}, u32[]{:S(2)}) copy-start(f32[12]{0:T(128)} %param.10) | copy-start | bytes 148
  16.4 9.5 %collective-permute-start.7 = (f32[6,8,16,8]{3,2,1,0:T(8,128)}, f32[6,8,16,8]{3,2,1,0:T(8,128)}, u32[]{:S(2)}, u32[]{:S(2)}) collective-permute-start(f32[6,8,16,8]{3,2,1,0:T(8,128)} %get-tuple-element.33), channel_id=1, source_target_pairs={{1,2},{2,1},{5,6},{6,5},{9,10},{10,9},{13,14},{14,13},{17,18},{18,... | collective-permute-start | bytes 73736 | tf_op jit(solution)/shard_map/ppermute | solution.py:33
  20.5 0.8 copy-start.8
  27.1 42.4 %copy-start.6 = (f32[6,8,16,8]{3,2,1,0:T(8,128)}, f32[6,8,16,8]{3,2,1,0:T(8,128)S(1)}, u32[]{:S(2)}) copy-start(f32[6,8,16,8]{3,2,1,0:T(8,128)S(1)} %get-tuple-element.24) | copy-start | bytes 73732
  27.1 42.4 %copy-start.7 = (f32[6,8,16,8]{3,2,1,0:T(8,128)}, f32[6,8,16,8]{3,2,1,0:T(8,128)S(1)}, u32[]{:S(2)}) copy-start(f32[6,8,16,8]{3,2,1,0:T(8,128)S(1)} %get-tuple-element.25) | copy-start | bytes 73732
  28.9 51.5 %collective-permute-start.9 = (f32[216,128]{1,0:T(8,128)}, f32[216,128]{1,0:T(8,128)}, u32[]{:S(2)}, u32[]{:S(2)}) collective-permute-start(f32[216,128]{1,0:T(8,128)} %select_n.117), channel_id=1, source_target_pairs={{0,4},{4,0},{8,12},{12,8},{16,20},{20,16},{24,28},{28,24},{1,5},{5... | collective-permute-start | bytes 331784 | tf_op jit(solution)/shard_map/ppermute | solution.py:33
  32.0 48.4 %collective-permute-start.8 = (f32[216,128]{1,0:T(8,128)}, f32[216,128]{1,0:T(8,128)S(1)}, u32[]{:S(2)}, u32[]{:S(2)}) collective-permute-start(f32[216,128]{1,0:T(8,128)} %select_n.115), channel_id=1, source_target_pairs={{4,8},{8,4},{12,16},{16,12},{20,24},{24,20},{28,0},{0,28},{5,9},{9... | collective-permute-start | bytes 331784 | tf_op jit(solution)/shard_map/ppermute | solution.py:33
  35.6 33.9 %collective-permute-start.2 = (bf16[8,144,128]{2,1,0:T(8,128)(2,1)S(1)}, bf16[8,144,128]{2,1,0:T(8,128)(2,1)S(1)}, u32[]{:S(2)}, u32[]{:S(2)}) collective-permute-start(bf16[8,144,128]{2,1,0:T(8,128)(2,1)S(1)} %get-tuple-element.27), channel_id=1, source_target_pairs={{0,4},{4,0},{8,12},{12,8},{16,20},{20,16},{24,28},{28,24},{1,5},{5... | collective-permute-start | bytes 884744 | tf_op jit(solution)/shard_map/ppermute | solution.py:33
  35.8 33.7 %collective-permute-start.3 = (bf16[8,144,128]{2,1,0:T(8,128)(2,1)S(1)}, bf16[8,144,128]{2,1,0:T(8,128)(2,1)S(1)}, u32[]{:S(2)}, u32[]{:S(2)}) collective-permute-start(bf16[8,144,128]{2,1,0:T(8,128)(2,1)S(1)} %get-tuple-element.26), channel_id=1, source_target_pairs={{4,8},{8,4},{12,16},{16,12},{20,24},{24,20},{28,0},{0,28},{5,9},{9... | collective-permute-start | bytes 884744 | tf_op jit(solution)/shard_map/ppermute | solution.py:33
  37.9 2.2 %copy-start.1 = (bf16[8,16,128,128]{3,2,1,0:T(8,128)(2,1)S(1)}, bf16[8,16,128,128]{3,2,1,0:T(8,128)(2,1)}, u32[]{:S(2)}) copy-start(bf16[8,16,128,128]{3,2,1,0:T(8,128)(2,1)} %copy-done) | copy-start | bytes 12582916
  78.0 12.7 %collective-permute-start.4 = (bf16[8,96,128]{2,1,0:T(8,128)(2,1)}, bf16[8,96,128]{2,1,0:T(8,128)(2,1)S(1)}, u32[]{:S(2)}, u32[]{:S(2)}) collective-permute-start(bf16[8,96,128]{2,1,0:T(8,128)(2,1)} %get-tuple-element.12), channel_id=1, source_target_pairs={{0,4},{4,0},{8,12},{12,8},{16,20},{20,16},{24,28},{28,24},{1,5},{5... | collective-permute-start | bytes 589832 | tf_op jit(solution)/shard_map/ppermute | solution.py:33
  78.4 12.3 %collective-permute-start.5 = (bf16[8,96,128]{2,1,0:T(8,128)(2,1)S(1)}, bf16[8,96,128]{2,1,0:T(8,128)(2,1)S(1)}, u32[]{:S(2)}, u32[]{:S(2)}) collective-permute-start(bf16[8,96,128]{2,1,0:T(8,128)(2,1)S(1)} %get-tuple-element.13), channel_id=1, source_target_pairs={{4,8},{8,4},{12,16},{16,12},{20,24},{24,20},{28,0},{0,28},{5,9},{9... | collective-permute-start | bytes 589832 | tf_op jit(solution)/shard_map/ppermute | solution.py:33

commit v2 on v0

v2 whole, which is shorter than its diff:
```python
import functools
import math

import jax
import jax.numpy as jnp
from jax import lax
from jax.experimental import pallas as pl
from jax.experimental.pallas import tpu as pltpu
from jax.sharding import PartitionSpec as P

time_step = 0.5
speed_cap = 0.6
cos_floor = 0.5

SIDE = 8
SLOT = 2 * SIDE
WIDE = 128
REACH = 4
VG = 8
VMEM_LIMIT = 40 * 2**20
f32 = jnp.float32
bf16 = jnp.bfloat16


def swap_pairs(count, first, closed):
    pairs = []
    for low in range(first, count, 2):
        high = low + 1
        if high >= count and not closed:
            continue
        pairs += [(low, high % count), (high % count, low)]
    return pairs


def swap(block, axis, first, closed):
    return lax.ppermute(block, axis, swap_pairs(lax.axis_size(axis), first, closed))


def place(row, rows):
    half, par = row // 2, row % 2
    own = 0 <= half < rows // 2
    return (0 if own else 2) + par, SLOT * (half % (rows // 2))


def lanes(shape):
    return lax.broadcasted_iota(jnp.int32, shape, len(shape) - 1)


def roll(x, by):
    by = by % WIDE
    return pltpu.roll(x, by, x.ndim - 1) if by else x


def col_before(mains, sides, at):
    lane = lanes(next(iter(mains.values())).shape)
    new_sides = {k: roll(s, 1) for k, s in sides.items()}
    new_mains = {}
    for row, main in mains.items():
        k, base = at(row)
        new_mains[row] = jnp.where(lane == 0, roll(sides[k], -(base + SLOT - 1)), roll(main, 1))
        new_sides[k] = jnp.where(lane == base, roll(main, base + 1), new_sides[k])
    return new_mains, new_sides


def col_after(mains, sides, at):
    lane = lanes(next(iter(mains.values())).shape)
    new_sides = {k: roll(s, -1) for k, s in sides.items()}
    new_mains = {}
    for row, main in mains.items():
        k, base = at(row)
        new_mains[row] = jnp.where(lane == WIDE - 1, roll(sides[k], WIDE - 1 - base), roll(main, -1))
        new_sides[k] = jnp.where(lane == base + SLOT - 1, roll(main, base + SLOT - 1), new_sides[k])
    return new_mains, new_sides


def join_taps(mains, sides, at):
    def part(group, b):
        return {k: x[b * SLOT : (b + 1) * SLOT] for k, x in group.items()}

    mb, sb = col_before(part(mains, 0), part(sides, 0), at)
    ma, sa = col_after(part(mains, 2), part(sides, 2), at)
    mm, sm = part(mains, 1), part(sides, 1)
    return {r: mb[r] + mm[r] + ma[r] for r in mains}, {k: sb[k] + sm[k] + sa[k] for k in sides}


def two_terms(x):
    first = x.astype(bf16)
    return [first, (x - first.astype(f32)).astype(bf16)]


def nt(lhs, rhs):
    return lax.dot_general(lhs, rhs, (((1,), (1,)), ((), ())), preferred_element_type=f32)


def silu(s):
    return s / (1.0 + jnp.exp(-s))


def turn_kernel(flag_ref, x_ref, st_ref, g_ref, st8_ref, outa_ref, outb_ref, s_ref, v_ref):
    chans, rows, cols = x_ref.shape[1:]
    nvar = st_ref.shape[0]
    even = flag_ref[1] == 0
    s_ref[...] = x_ref[0].astype(f32).reshape(chans * rows, cols)
    for row in range(rows):
        block = s_ref[pl.ds(row, chans, stride=rows), :].T
        g_ref[0, row] = block.astype(bf16)
        first, last = block[0:SIDE], block[cols - SIDE :]
        v_ref[0, row * SIDE : (row + 1) * SIDE] = jnp.where(even, last, first)
        v_ref[1, row * SIDE : (row + 1) * SIDE] = jnp.where(even, first, last)
    outa_ref[0, 0 : rows * SIDE] = v_ref[0].astype(bf16)
    outb_ref[0, 0 : rows * SIDE] = v_ref[1].astype(bf16)
    for n in range(nvar):
        s_ref[pl.ds(n, rows, stride=VG), :] = st_ref[n, 0]
    lane = lanes((VG, WIDE))
    toright = [jnp.zeros((VG, WIDE), f32)] * 2
    toleft = [jnp.zeros((VG, WIDE), f32)] * 2
    for row in range(rows):
        block = s_ref[row * VG : (row + 1) * VG]
        block = jnp.where(lax.broadcasted_iota(jnp.int32, (VG, WIDE), 0) < nvar, block, 0.0)
        st8_ref[0, row] = block
        par, base = place(row, rows)
        mine = lane // SLOT == base // SLOT
        toleft[par] = jnp.where(mine, roll(block, base), toleft[par])
        toright[par] = jnp.where(mine, roll(block, base + SLOT), toright[par])
    for out, pick in ((outa_ref, [jnp.where(even, r, l) for r, l in zip(toright, toleft)]),
                      (outb_ref, [jnp.where(even, l, r) for r, l in zip(toright, toleft)])):
        out[0, rows * SIDE :] = jnp.concatenate(two_terms(pick[0]) + two_terms(pick[1]), axis=0)


def state_sides(right, left, start):
    both = [x[start:].astype(f32) for x in (right, left)]
    out = []
    for par in range(2):
        r, l = (x[2 * par * VG : (2 * par + 1) * VG] + x[(2 * par + 1) * VG : (2 * par + 2) * VG] for x in both)
        out.append(jnp.where(lanes(r.shape) % SLOT < SIDE, r, l))
    return out


def sides_of(even, a_ref, b_ref):
    a, b = a_ref[0], b_ref[0]
    return jnp.where(even, a, b), jnp.where(even, b, a)


def pack_kernel(flag_ref, a_ref, b_ref, glo_ref, ghi_ref, outa_ref, outb_ref, sst_ref):
    rows = (a_ref.shape[1] - 4 * VG) // SIDE
    cols = glo_ref.shape[2]
    even = flag_ref[0] == 0
    right, left = sides_of(flag_ref[1] == 0, a_ref, b_ref)
    st = state_sides(right, left, rows * SIDE)
    sst_ref[0, 0], sst_ref[0, 1] = st
    lane = lanes((VG, WIDE))
    st_lo = jnp.where(lane < 2 * SLOT, st[0], roll(st[1], 2 * SLOT))
    st_hi = jnp.where(lane >= WIDE - 2 * SLOT, st[0], roll(st[1], -2 * SLOT))

    def wire(g_ref, row, s):
        side = [x[row * SIDE : (row + 1) * SIDE] for x in (right, left)]
        return g_ref[0, 0], jnp.concatenate(side + two_terms(s), axis=0)

    lo, hi = wire(glo_ref, 0, st_lo), wire(ghi_ref, rows - 1, st_hi)
    for out, first, second in ((outa_ref, hi, lo), (outb_ref, lo, hi)):
        out[0, 0:cols] = jnp.where(even, first[0], second[0])
        out[0, cols:] = jnp.where(even, first[1], second[1])


def lay_row(e_ref, slot, s_ref, to, main, right, left):
    cols, ch = main.shape
    ext = cols + SLOT
    main = main.astype(f32)
    left = left.astype(f32)
    e_ref[slot, 0:SIDE] = left
    e_ref[slot, SIDE : SIDE + cols] = main
    e_ref[slot, SIDE + cols : SLOT + cols] = right.astype(f32)
    e_ref[slot, SLOT + cols : SLOT + SIDE + cols] = left
    e_ref[slot, SLOT + SIDE + cols : 2 * SLOT + cols] = main[0:SIDE]
    for b in range(3):
        s_ref[to, :, b * ch : (b + 1) * ch] = e_ref[slot, pl.ds(SIDE - 1 + b, ext), :].astype(bf16)


def inner_kernel(flag_ref, g_ref, a_ref, b_ref, w1_ref, w2_ref, b1_ref, keep_ref, ps_ref, pm_ref,
                 e_ref, se_ref, so_ref, h_ref, hs_ref):
    rows, cols, ch = g_ref.shape[1:]
    half = rows // 2
    right, left = sides_of(flag_ref[1] == 0, a_ref, b_ref)
    right, left = right.astype(f32), left.astype(f32)
    for row in range(rows):
        side = slice(row * SIDE, (row + 1) * SIDE)
        lay_row(e_ref, row, se_ref if row % 2 == 0 else so_ref, row // 2, g_ref[0, row], right[side], left[side])
    none = jnp.zeros((cols, ch), bf16)
    for at in (0, 1, rows, rows + 1):
        h_ref[at] = none
    for par in range(2):
        for at in (0, half):
            hs_ref[par, at * SLOT : (at + 1) * SLOT] = none[0:SLOT]
    for m in range(half - 1):
        lhs = jnp.concatenate([se_ref[m], so_ref[m], se_ref[m + 1], so_ref[m + 1]], axis=1)
        acc = jnp.dot(lhs, w1_ref[...], preferred_element_type=f32) + b1_ref[...]
        hid = silu(acc)
        for k in range(2):
            here = hid[:, k * ch : (k + 1) * ch]
            h_ref[2 * m + 2 + k] = here[0:cols].astype(bf16)
            hs_ref[k, (m + 1) * SLOT : (m + 2) * SLOT] = (here[cols:] * keep_ref[...]).astype(bf16)
    mains = {}
    for m in range(half):
        q = nt(w2_ref[...], jnp.concatenate([h_ref[2 * m + r] for r in range(4)], axis=1))
        for k in range(2):
            mains[2 * m + k] = q[k * 3 * SLOT : (k + 1) * 3 * SLOT]
    part = [hs_ref[r % 2, (r // 2) * SLOT : (r // 2 + half) * SLOT] for r in range(4)]
    q = nt(w2_ref[...], jnp.concatenate(part, axis=1))
    sides = {k: q[k * 3 * SLOT : (k + 1) * 3 * SLOT] for k in range(2)}
    mains, sides = join_taps(mains, sides, lambda row: place(row, rows))
    for row in range(rows):
        ps_ref[0, row] = mains[row]
    for k in range(2):
        pm_ref[0, k] = sides[k]


def edge_kernel(flag_ref, g0_ref, g1_ref, la_ref, lb_ref, a_ref, b_ref, w1_ref, w2_ref, b1_ref, keep_ref,
                ps0_ref, ps1_ref, pmi_ref, pe_ref, pm_ref, outa_ref, outb_ref, e_ref, s_ref, z_ref):
    cols, ch = g0_ref.shape[2:]
    rows = (la_ref.shape[1] - 4 * VG) // SIDE
    ext = cols + SLOT
    even = flag_ref[0] == 0
    right, left = sides_of(flag_ref[1] == 0, la_ref, lb_ref)
    right, left = right.astype(f32), left.astype(f32)
    got_a = a_ref[0].astype(f32)
    got_b = b_ref[0].astype(f32)
    low = jnp.where(even, got_b, got_a)
    high = jnp.where(even, got_a, got_b)
    for to, got in ((0, low), (5, high)):
        lay_row(e_ref, to, s_ref, to, got[0:cols], got[cols : cols + SIDE], got[cols + SIDE : ext])
    for k in range(2):
        for to, g_ref, row in ((1 + k, g0_ref, k), (3 + k, g1_ref, rows - 2 + k)):
            side = slice(row * SIDE, (row + 1) * SIDE)
            lay_row(e_ref, to, s_ref, to, g_ref[0, k], right[side], left[side])
    z_ref[...] = jnp.zeros_like(z_ref)
    mains = {}
    for k in range(2):
        lhs = jnp.concatenate([s_ref[3 * k + r] for r in range(3)], axis=1)
        acc = jnp.dot(lhs, w1_ref[...], preferred_element_type=f32) + b1_ref[...]
        hid = silu(acc)
        z_ref[k * SLOT : (k + 1) * SLOT] = (hid[cols:] * keep_ref[...]).astype(bf16)
        q = nt(w2_ref[...], hid[0:cols].astype(bf16))
        for a in range(3):
            mains[k * (rows - 1) + 1 - a] = q[a * 3 * SLOT : (a + 1) * 3 * SLOT]
    q = nt(w2_ref[...], z_ref[...])
    sides = {a: q[a * 3 * SLOT : (a + 1) * 3 * SLOT] for a in range(3)}

    def at(row):
        k = row > rows // 2
        return k * (rows - 1) + 1 - row, k * SLOT

    mains, sides = join_taps(mains, sides, at)
    for row, own in ((0, ps0_ref[0, 0]), (1, ps0_ref[0, 1]), (rows - 2, ps1_ref[0, 2]), (rows - 1, ps1_ref[0, 3])):
        mains[row] = mains[row] + own
    for k, row in enumerate((-1, 0, 1, rows - 2, rows - 1, rows)):
        pe_ref[0, k] = mains[row]
    lane = lanes((2 * VG, WIDE))
    begin, end = lane < SLOT, lane >= WIDE - SLOT
    to_end = -2 * SLOT
    own_e = pmi_ref[0, 0] + jnp.where(begin, sides[1], 0.0) + jnp.where(end, roll(sides[2], to_end), 0.0)
    own_o = pmi_ref[0, 1] + jnp.where(begin, sides[0], 0.0) + jnp.where(end, roll(sides[1], to_end), 0.0)
    next_e = jnp.where(begin, roll(sides[0], -SLOT), 0.0)
    prev_o = jnp.where(end, roll(sides[2], -SLOT), 0.0)
    for k, x in enumerate((own_e, own_o, next_e, prev_o)):
        pm_ref[0, k] = x
    side_lo = jnp.where(lane < 2 * SLOT, own_e, jnp.where(lane < 4 * SLOT, roll(own_o, 2 * SLOT), prev_o))
    side_hi = jnp.where(lane >= WIDE - 2 * SLOT, own_e, jnp.where(lane >= WIDE - 4 * SLOT, roll(own_o, -2 * SLOT), next_e))
    out_lo = jnp.concatenate([mains[-1], mains[0], mains[1], ps0_ref[0, 2], side_lo, ps0_ref[0, 3]], axis=0)
    out_hi = jnp.concatenate([mains[rows], mains[rows - 1], mains[rows - 2], ps1_ref[0, 1], side_hi, ps1_ref[0, 0]], axis=0)
    outa_ref[0] = jnp.where(even, out_hi, out_lo).astype(bf16)
    outb_ref[0] = jnp.where(even, out_lo, out_hi).astype(bf16)


def advect_kernel(flag_ref, ps_ref, pe_ref, pm_ref, a_ref, b_ref, st8_ref, sst_ref, sa_ref, sb_ref, ha_ref, hb_ref,
                  b2_ref, lat_ref, lats_ref, vel_ref, ten_ref, x_ref, out_ref):
    rows = st8_ref.shape[1]
    nvar = ten_ref.shape[0]
    even = flag_ref[0] == 0
    lane16 = lanes((2 * VG, WIDE))
    lane = lanes((VG, WIDE))
    pair = 2 * VG

    def halos(xa, xb):
        return jnp.where(even, xb, xa), jnp.where(even, xa, xb)

    lo, hi = halos(a_ref[0].astype(f32), b_ref[0].astype(f32))
    main = {row: ps_ref[0, row] for row in range(2, rows - 2)}
    for k, row in enumerate((-1, 0, 1, rows - 2, rows - 1, rows)):
        main[row] = pe_ref[0, k]
    for k in range(REACH + 1):
        there = slice(k * pair, (k + 1) * pair) if k < REACH else slice((k + 1) * pair, (k + 2) * pair)
        for got, row in ((lo, -k), (hi, rows - 1 + k)):
            main[row] = main[row] + got[there] if row in main else got[there]
    slo, shi = (got[REACH * pair : (REACH + 1) * pair] for got in (lo, hi))
    zero = jnp.zeros((pair, WIDE), f32)
    last, front = lane16 >= WIDE - 2 * SLOT, lane16 < 2 * SLOT
    side = {
        0: pm_ref[0, 0] + jnp.where(lane16 < SLOT, slo, zero),
        1: pm_ref[0, 1] + jnp.where(lane16 >= WIDE - SLOT, shi, zero),
        2: pm_ref[0, 2] + jnp.where(last, slo, jnp.where(front, shi, zero)),
        3: pm_ref[0, 3] + jnp.where(last, roll(slo, 2 * SLOT), jnp.where(front, roll(shi, -2 * SLOT), zero)),
    }
    bias = b2_ref[...]
    main = {r: speed_cap * jnp.tanh(x + bias) for r, x in main.items()}
    side = {k: speed_cap * jnp.tanh(x + bias) * lats_ref[2:3] for k, x in side.items()}
    for part in range(2):
        for row in range(rows):
            out_ref[part, row * VG : (row + 1) * VG] = main[row][part * VG : (part + 1) * VG]
        for n in range(nvar):
            vel_ref[2 * n + part, 0] = out_ref[part, pl.ds(n, rows, stride=VG), :]

    x_ref[...] = jnp.zeros_like(x_ref)
    for n in range(nvar):
        down, up = halos(sa_ref[n, 0], sb_ref[n, 0])
        x_ref[0, pl.ds(n, REACH, stride=VG), :] = down
        x_ref[1, pl.ds(n, REACH, stride=VG), :] = up
    q0 = {row: st8_ref[0, row] for row in range(rows)}
    for k in range(REACH):
        q0[k - REACH] = x_ref[0, k * VG : (k + 1) * VG]
        q0[rows + k] = x_ref[1, k * VG : (k + 1) * VG]
    hlo, hhi = halos(ha_ref[0].astype(f32), hb_ref[0].astype(f32))
    hlo, hhi = hlo[0:VG] + hlo[VG:], hhi[0:VG] + hhi[VG:]
    last, front = lane >= WIDE - 2 * SLOT, lane < 2 * SLOT
    nil = jnp.zeros((VG, WIDE), f32)
    s0 = {
        0: sst_ref[0, 0],
        1: sst_ref[0, 1],
        2: jnp.where(last, hlo, jnp.where(front, hhi, nil)),
        3: jnp.where(last, roll(hlo, 2 * SLOT), jnp.where(front, roll(hhi, -2 * SLOT), nil)),
    }

    def at(row):
        return place(row, rows)

    def side_rows(s):
        def turned(own, halo, by, first):
            own, halo = roll(own, by), roll(halo, by)
            return jnp.where(first, halo, own), jnp.where(first, own, halo)

        odd_back = turned(s[1], s[3], SLOT, lane < SLOT)
        even_on = turned(s[0], s[2], -SLOT, lane >= WIDE - SLOT)
        before = {0: odd_back[0], 2: odd_back[1], 1: s[0], 3: s[2]}
        after = {0: s[1], 2: s[3], 1: even_on[0], 3: even_on[1]}
        return before, after

    u = {r: x[0:VG] for r, x in main.items()}
    us = {k: x[0:VG] for k, x in side.items()}
    inside = range(1 - REACH, rows + REACH - 1)
    v = {r: main[r][VG:] for r in inside}
    vs = {k: x[VG:] for k, x in side.items()}
    cosine, metric = lat_ref[0:1], lat_ref[1:2]
    cosine_s, metric_s = lats_ref[0:1], lats_ref[1:2]
    flux = {r: x * cosine for r, x in v.items()}
    flux_s = {k: x * cosine_s for k, x in vs.items()}
    fb, fbs = col_before(flux, flux_s, at)
    fa, fas = col_after(flux, flux_s, at)
    ub, ua = side_rows(us)

    def coefs(m, uu, vv, udiff, vdiff):
        div = m * (udiff * 0.5 + vdiff * 0.5)
        cl = m * jnp.maximum(uu, 0.0)
        cr = -(m * jnp.minimum(uu, 0.0))
        cd = jnp.maximum(vv, 0.0)
        cu = -jnp.minimum(vv, 0.0)
        return -(cl + cr + cd + cu + div), cl, cr, cd, cu

    cm = {r: coefs(metric, u[r], v[r], u[r + 1] - u[r - 1], fa[r] - fb[r]) for r in inside}
    cs = {k: coefs(metric_s, us[k], vs[k], ua[k] - ub[k], fas[k] - fbs[k]) for k in range(4)}

    def stencil(c, x, left, right, down, up):
        return c[0] * x + c[1] * left + c[2] * right + c[3] * down + c[4] * up

    def rate(q, s, depth):
        centre = {r: q[r] for r in range(depth - REACH, rows + REACH - depth)}
        qb, sb = col_before(centre, s, at)
        qa, sa = col_after(centre, s, at)
        rb, ra = side_rows(s)
        out = {r: stencil(cm[r], q[r], q[r - 1], q[r + 1], qb[r], qa[r]) for r in centre}
        if depth == REACH:
            return out, None
        return out, {k: stencil(cs[k], s[k], rb[k], ra[k], sb[k], sa[k]) for k in range(4)}

    def moved(rates, by):
        return {r: q0[r] + by * x for r, x in rates[0].items()}, {k: s0[k] + by * x for k, x in rates[1].items()}

    one = rate(q0, s0, 1)
    two = rate(*moved(one, 0.5 * time_step), 2)
    three = rate(*moved(two, 0.5 * time_step), 3)
    four = rate(*moved(three, time_step), 4)
    for row in range(rows):
        ten = (one[0][row] + 2.0 * two[0][row] + 2.0 * three[0][row] + four[0][row]) / 6.0
        out_ref[0, row * VG : (row + 1) * VG] = ten
    for n in range(nvar):
        ten_ref[n, 0] = out_ref[0, pl.ds(n, rows, stride=VG), :]


def full(shape):
    return pl.BlockSpec(shape, lambda *i: (0,) * len(shape))


def per_level(shape):
    return pl.BlockSpec((1,) + shape[1:], lambda i: (i,) + (0,) * (len(shape) - 1))


def level_part(shape, index):
    return pl.BlockSpec((1,) + shape, lambda i: (i, index) + (0,) * (len(shape) - 1))


def var_level(shape):
    return pl.BlockSpec((shape[0], 1) + shape[2:], lambda i: (0, i, 0, 0))


def body(hidden_in, w_conv1, b_conv1, w_conv2, b_conv2, state):
    lev, ch, rows, cols = hidden_in.shape
    nvar = state.shape[0]
    ext = cols + SLOT
    half = rows // 2
    params = pltpu.CompilerParams(vmem_limit_bytes=VMEM_LIMIT)
    smem = pl.BlockSpec(memory_space=pltpu.SMEM)
    sds = jax.ShapeDtypeStruct

    def call(kernel, ins, outs, scratch, args, cost=None):
        return pl.pallas_call(
            kernel,
            grid=(lev,),
            in_specs=ins,
            out_specs=[per_level(o.shape) if len(o.shape) == 3 or o.shape[0] == lev else var_level(o.shape) for o in outs],
            out_shape=outs,
            scratch_shapes=scratch,
            compiler_params=params,
            cost_estimate=cost,
        )(*args)

    taps = w_conv1.reshape(3, 3 * ch, ch)
    w1_pair = jnp.pad(taps.reshape(9 * ch, ch), ((0, 3 * ch), (0, 0)))
    w1_pair = jnp.concatenate([w1_pair, jnp.pad(taps.reshape(9 * ch, ch), ((3 * ch, 0), (0, 0)))], axis=1)
    w1_one = taps.reshape(9 * ch, ch)
    w2 = w_conv2.reshape(3, 3, ch, nvar, 2).transpose(0, 1, 4, 3, 2)
    w2 = jnp.pad(w2, ((0, 0), (0, 0), (0, 0), (0, VG - nvar), (0, 0))).reshape(3, 3 * SLOT, ch)
    w2_row = w2.transpose(1, 0, 2).reshape(3 * SLOT, 3 * ch)
    w2_pair = jnp.concatenate([jnp.pad(w2_row, ((0, 0), (0, ch))), jnp.pad(w2_row, ((0, 0), (ch, 0)))], axis=0)
    w2_one = w2.reshape(9 * SLOT, ch)
    b1 = b_conv1.reshape(1, ch)
    b2 = jnp.pad(b_conv2.reshape(nvar, 2).T, ((0, 0), (0, VG - nvar))).reshape(2 * VG, 1)
    b2 = jnp.broadcast_to(b2, (2 * VG, WIDE))

    n_lat = cols * lax.axis_size("lat")
    side_place = jnp.concatenate([jnp.arange(cols, cols + SIDE), jnp.arange(-SIDE, 0)]).astype(jnp.int32)

    def latitudes(place_in):
        place_in = place_in + lax.axis_index("lat") * cols
        keep = ((place_in >= 0) & (place_in < n_lat)).astype(f32)
        phi = (place_in.astype(f32) + 0.5) * (math.pi / n_lat) - 0.5 * math.pi
        cosine = jnp.maximum(jnp.cos(phi), cos_floor)
        return jnp.pad(jnp.stack([cosine, 1.0 / cosine, keep]), ((0, VG - 3), (0, 0)))

    lat_main = latitudes(jnp.arange(cols, dtype=jnp.int32))
    lat_side = latitudes(jnp.tile(side_place, WIDE // SLOT))
    keep = jnp.broadcast_to(lat_side[2, 0:SLOT].reshape(SLOT, 1), (SLOT, ch))
    is_even = lax.axis_index("lon") % 2 == 0
    flags = jnp.stack([lax.axis_index("lon") % 2, lax.axis_index("lat") % 2]).astype(jnp.int32)

    st_lo, st_hi = state[:, :, 0:REACH], state[:, :, rows - REACH :]
    state_a = swap(jnp.where(is_even, st_hi, st_lo), "lon", 0, True)
    state_b = swap(jnp.where(is_even, st_lo, st_hi), "lon", 1, True)

    lat_wire = (lev, rows * SIDE + 4 * VG, WIDE)
    g, st8, lat_a, lat_b = call(
        turn_kernel,
        [smem, per_level(hidden_in.shape), var_level(state.shape)],
        [sds((lev, rows, cols, ch), bf16), sds((lev, rows, VG, WIDE), f32), sds(lat_wire, bf16), sds(lat_wire, bf16)],
        [pltpu.VMEM((ch * rows, cols), f32), pltpu.VMEM((2, rows * SIDE, ch), f32)],
        (flags, hidden_in, state),
    )
    lat_a = swap(lat_a, "lat", 0, False)
    lat_b = swap(lat_b, "lat", 1, False)

    lon_wire = (lev, cols + 2 * SLOT, WIDE)
    lon_a, lon_b, side_state = call(
        pack_kernel,
        [smem, per_level(lat_wire), per_level(lat_wire), level_part((1, cols, ch), 0), level_part((1, cols, ch), rows - 1)],
        [sds(lon_wire, bf16), sds(lon_wire, bf16), sds((lev, 2, VG, WIDE), f32)],
        [],
        (flags, lat_a, lat_b, g, g),
    )
    lon_a = swap(lon_a, "lon", 0, True)
    lon_b = swap(lon_b, "lon", 1, True)

    ps_shape = (lev, rows, 2 * VG, WIDE)
    pm_shape = (lev, 2, 2 * VG, WIDE)
    ps, pm = call(
        inner_kernel,
        [smem, per_level(g.shape), per_level(lat_wire), per_level(lat_wire), full(w1_pair.shape), full(w2_pair.shape),
         full((1, 2 * ch)), full((SLOT, ch))],
        [sds(ps_shape, f32), sds(pm_shape, f32)],
        [
            pltpu.VMEM((rows, cols + 2 * SLOT, ch), f32),
            pltpu.VMEM((half, ext, 3 * ch), bf16),
            pltpu.VMEM((half, ext, 3 * ch), bf16),
            pltpu.VMEM((rows + 2, cols, ch), bf16),
            pltpu.VMEM((2, (half + 1) * SLOT, ch), bf16),
        ],
        (flags, g, lat_a, lat_b, w1_pair, w2_pair, jnp.concatenate([b1, b1], axis=1), keep),
        pl.CostEstimate(flops=2 * lev * rows * ext * 9 * ch * ch, bytes_accessed=8 * 2**20, transcendentals=0),
    )

    g_pair, four = (2, cols, ch), (4, 2 * VG, WIDE)
    wire = (lev, 2 * VG * (REACH + 2), WIDE)
    pe_shape = (lev, 6, 2 * VG, WIDE)
    pe, pm, out_a, out_b = call(
        edge_kernel,
        [smem, level_part(g_pair, 0), level_part(g_pair, half - 1), per_level(lat_wire), per_level(lat_wire),
         per_level(lon_wire), per_level(lon_wire), full(w1_one.shape), full(w2_one.shape), full((1, ch)), full((SLOT, ch)),
         level_part(four, 0), level_part(four, rows // 4 - 1), per_level(pm_shape)],
        [sds(pe_shape, f32), sds((lev, 4, 2 * VG, WIDE), f32), sds(wire, bf16), sds(wire, bf16)],
        [
            pltpu.VMEM((6, cols + 2 * SLOT, ch), f32),
            pltpu.VMEM((6, ext, 3 * ch), bf16),
            pltpu.VMEM((WIDE, ch), bf16),
        ],
        (flags, g, g, lat_a, lat_b, lon_a, lon_b, w1_one, w2_one, b1, keep, ps, ps, pm),
    )
    out_a = swap(out_a, "lon", 0, True)
    out_b = swap(out_b, "lon", 1, True)

    tail = level_part((SLOT, WIDE), (cols + SLOT) // SLOT)
    return call(
        advect_kernel,
        [smem, per_level(ps_shape), per_level(pe_shape), per_level((lev, 4, 2 * VG, WIDE)), per_level(wire), per_level(wire),
         per_level(st8.shape), per_level(side_state.shape), var_level(state_a.shape), var_level(state_b.shape), tail, tail,
         full(b2.shape), full(lat_main.shape), full(lat_side.shape)],
        [sds((2 * nvar, lev, rows, cols), f32), sds(state.shape, f32)],
        [pltpu.VMEM((2, REACH * VG, WIDE), f32), pltpu.VMEM((2, rows * VG, WIDE), f32)],
        (flags, ps, pe, pm, out_a, out_b, st8, side_state, state_a, state_b, lon_a, lon_b, b2, lat_main, lat_side),
    )


def solution(mesh):
    placed = (P(None, None, "lon", "lat"), P(), P(), P(), P(), P(None, None, "lon", "lat"))
    return jax.shard_map(
        body,
        mesh=mesh,
        in_specs=placed,
        out_specs=(P(None, None, "lon", "lat"), P(None, None, "lon", "lat")),
        check_vma=False,
    )
```

time: 252 us -> 69 us (0.27)
  local copies, waits for them, and re-layouts: 120 us -> 7.98 us
  Pallas kernels: 0 us -> 37.7 us
  waiting for transfers between devices: 39 us -> 6.95 us
  matrix products: 31.2 us -> 0 us
  other arithmetic: 26.1 us -> 0.41 us
  starting transfers between devices: 32 us -> 14.8 us
    dynamic_update_slice x16 -> x0, local copies, waits for them, and re-layouts: 47 us -> none  [body(): wide = jnp.transpose(lax.map(level, padded), (1, 0, 2, 3))]
    pallas_call x0 -> x5, Pallas kernels: none -> 37.7 us  [call(): pl.pallas_call(kernel, grid=(lev,), in_specs=ins, out_specs=[per_level(o....]
    ppermute x20 -> x8, waiting for transfers between devices: 39 us -> 6.95 us  [swap(): lax.ppermute(block, axis, swap_pairs(lax.axis_size(axis), first, closed))]
    dot_general x16 -> x0, matrix products: 31.2 us -> none  [conv_block(): jnp.einsum('tcxy,tco->oxy', taps, stacked, preferred_element_type=jnp.flo...]
    while x128 -> x0, local copies, waits for them, and re-layouts: 20.9 us -> none
    ppermute x20 -> x8, starting transfers between devices: 32 us -> 14.8 us  [swap(): lax.ppermute(block, axis, swap_pairs(lax.axis_size(axis), first, closed))]
    mul x14 -> x0, other arithmetic: 11.9 us -> none  [the longest x1 6.47 us: body(): padded = padded * lat_profile(in_width, lat_dev)[0].astype(jnp.bfloat16)]
    ppermute x10 -> x0, local copies, waits for them, and re-layouts: 11.4 us -> none  [the longest x5 6.74 us: padded_2(): lax.ppermute(lax.slice_in_dim(block, 0, width, axis=dim), axis, backward)]
  transfers between devices with their start and end apart: 20 -> 8, of which waited for: 9 -> 1; matrix products, arithmetic and copies ran while one was open for 10% -> 1% of each run, Pallas kernels for 0% -> 35%
where the time goes in v2:
time: 69 us; the launch traced here: 68.7 us
  Pallas kernels  37.7 us (55%)
  starting transfers between devices  14.8 us (21%)
  local copies, waits for them, and re-layouts  7.98 us (12%)
  waiting for transfers between devices  6.95 us (10%)
  between operations  0.89 us (1%)
    pallas_call x5, Pallas kernels, call(): pl.pallas_call(kernel, grid=(lev,), in_specs=ins, out_specs=[per_level(o....  37.7 us
    ppermute x8, starting transfers between devices, swap(): lax.ppermute(block, axis, swap_pairs(lax.axis_size(axis), first, closed))  14.8 us
    unnamed x20, local copies, waits for them, and re-layouts  7.43 us
    ppermute x8, waiting for transfers between devices, swap(): lax.ppermute(block, axis, swap_pairs(lax.axis_size(axis), first, closed))  6.95 us
  transfers between devices with their start and end apart: 8, of which 1 were waited for; matrix products, arithmetic and copies ran while one was open for 1% of the time, Pallas kernels for 35%

profile of v2, /device:TPU:1, one launch (start us, length us, event | category | flops | bytes accessed | tf_op | source)
XLA Modules:
  0.0 68.7 jit_solution(16367902941033704659)
XLA Ops:
  0.6 0.1 pad_add_fusion.flag_ref
  0.7 0.0 copy-start.2
  0.7 2.2 %copy-done.2 = bf16[8,128,16,128]{3,2,1,0:T(8,128)(2,1)S(1)} copy-done((bf16[8,128,16,128]{3,2,1,0:T(8,128)(2,1)S(1)}, bf16[8,128,16,128]{3,2,1,0:T(8,128)(2,1)}, u32[]{:S(2)}) %copy-start.2) | copy-done | bytes 4194328
  2.9 0.0 copy-start.4
  2.9 1.0 %copy-done.4 = f32[6,8,16,128]{3,2,1,0:T(8,128)S(1)} copy-done((f32[6,8,16,128]{3,2,1,0:T(8,128)S(1)}, f32[6,8,16,128]{3,2,1,0:T(8,128)}, u32[]{:S(2)}) %copy-start.4) | copy-done | bytes 393240
  3.9 0.0 copy-start.5
  3.9 0.0 copy-start.7
  3.9 0.0 copy-start.8
  3.9 0.0 copy-start.6
  3.9 0.0 copy-start.3
  3.9 4.6 %shard_map.77 = (bf16[8,16,128,128]{3,2,1,0:T(8,128)(2,1)S(1)}, f32[8,16,8,128]{3,2,1,0:T(8,128)S(1)}, bf16[8,160,128]{2,1,0:T(8,128)(2,1)S(1)}, bf16[8,160,128]{2,1,0:T(8,128)(2,1)S(1)}) custom-call(s32[2]{0:T(128)S(1)} %pad_add_fusion.flag_ref, bf16[8,128,16,128]{3,2,1,0:T(8,128)(2,1)S(1)} %copy-done.2, f32[6,8,16,128]{3,2,1,0:T(8,128)S(1)} %copy-done.4), custom_call_target="tpu_custom_call" | custom-call | tf_op jit(solution)/shard_map/pallas_call | solution.py:423
  8.6 0.0 copy-start
  8.6 1.9 %copy-done = bf16[8,16,128,128]{3,2,1,0:T(8,128)(2,1)} copy-done((bf16[8,16,128,128]{3,2,1,0:T(8,128)(2,1)}, bf16[8,16,128,128]{3,2,1,0:T(8,128)(2,1)S(1)}, u32[]{:S(2)}) %copy-start) | copy-done | bytes 4194328
  10.5 0.1 collective-permute-start
  10.6 4.4 %collective-permute-start.1 = (bf16[8,160,128]{2,1,0:T(8,128)(2,1)S(1)}, bf16[8,160,128]{2,1,0:T(8,128)(2,1)S(1)}, u32[]{:S(2)}, u32[]{:S(2)}) collective-permute-start(bf16[8,160,128]{2,1,0:T(8,128)(2,1)S(1)} %get-tuple-element.17), channel_id=1, source_target_pairs={{1,2},{2,1},{5,6},{6,5},{9,10},{10,9},{13,14},{14,13},{17,18},{18,... | collective-permute-start | bytes 983048 | tf_op jit(solution)/shard_map/ppermute | solution.py:36
  15.0 0.0 copy-done.5
  15.1 1.3 %collective-permute-start.6 = (f32[6,8,4,128]{3,2,1,0:T(4,128)S(1)}, f32[6,8,4,128]{3,2,1,0:T(4,128)S(1)}, u32[]{:S(2)}, u32[]{:S(2)}) collective-permute-start(f32[6,8,4,128]{3,2,1,0:T(4,128)S(1)} %get-tuple-element.31), channel_id=1, source_target_pairs={{0,4},{4,0},{8,12},{12,8},{16,20},{20,16},{24,28},{28,24},{1,5},{5... | collective-permute-start | bytes 294920 | tf_op jit(solution)/shard_map/ppermute | solution.py:36
  16.4 3.3 %collective-permute-start.7 = (f32[6,8,4,128]{3,2,1,0:T(4,128)S(1)}, f32[6,8,4,128]{3,2,1,0:T(4,128)S(1)}, u32[]{:S(2)}, u32[]{:S(2)}) collective-permute-start(f32[6,8,4,128]{3,2,1,0:T(4,128)S(1)} %get-tuple-element.30), channel_id=1, source_target_pairs={{4,8},{8,4},{12,16},{16,12},{20,24},{24,20},{28,0},{0,28},{5,9},{9... | collective-permute-start | bytes 294920 | tf_op jit(solution)/shard_map/ppermute | solution.py:36
  19.7 0.1 cosine_maximum_fusion
  19.8 0.1 convert_element_type.70
  19.9 0.0 copy-done.7
  20.1 0.1 reshape.138
  20.2 0.0 copy-done.8
  20.2 0.1 reshape.133
  20.3 0.1 copy.14
  20.4 0.1 broadcast_in_dim.16
  20.5 0.0 copy-done.6
  20.5 0.0 copy-done.3
  20.5 0.1 fusion.2.w1_ref
  20.5 0.0 collective-permute-done.a_ref.la_ref
  20.6 0.0 collective-permute-done.1.b_ref.lb_ref
  20.6 0.0 copy-start.1
  20.6 2.2 %copy-done.1 = bf16[8,16,128,128]{3,2,1,0:T(8,128)(2,1)S(1)} copy-done((bf16[8,16,128,128]{3,2,1,0:T(8,128)(2,1)S(1)}, bf16[8,16,128,128]{3,2,1,0:T(8,128)(2,1)}, u32[]{:S(2)}) %copy-start.1) | copy-done | bytes 4194328
  22.8 1.3 %shard_map.79 = (bf16[8,160,128]{2,1,0:T(8,128)(2,1)S(1)}, bf16[8,160,128]{2,1,0:T(8,128)(2,1)S(1)}, f32[8,2,8,128]{3,2,1,0:T(8,128)S(1)}) custom-call(s32[2]{0:T(128)S(1)} %pad_add_fusion.flag_ref, bf16[8,160,128]{2,1,0:T(8,128)(2,1)S(1)} %collective-permute-done.a_ref.la_ref, bf16[8,160,128]{2,1,0:T(8,128)(2,1)S(1)} %collective-permute-done.1.b_ref.lb_ref, ...), custom_call_target="tpu_custom_call" | custom-call | tf_op jit(solution)/shard_map/pallas_call | solution.py:423
  24.1 1.1 %collective-permute-start.2 = (bf16[8,160,128]{2,1,0:T(8,128)(2,1)S(1)}, bf16[8,160,128]{2,1,0:T(8,128)(2,1)S(1)}, u32[]{:S(2)}, u32[]{:S(2)}) collective-permute-start(bf16[8,160,128]{2,1,0:T(8,128)(2,1)S(1)} %get-tuple-element.19), channel_id=1, source_target_pairs={{0,4},{4,0},{8,12},{12,8},{16,20},{20,16},{24,28},{28,24},{1,5},{5... | collective-permute-start | bytes 983048 | tf_op jit(solution)/shard_map/ppermute | solution.py:36
  25.2 3.3 %collective-permute-start.3 = (bf16[8,160,128]{2,1,0:T(8,128)(2,1)S(1)}, bf16[8,160,128]{2,1,0:T(8,128)(2,1)S(1)}, u32[]{:S(2)}, u32[]{:S(2)}) collective-permute-start(bf16[8,160,128]{2,1,0:T(8,128)(2,1)S(1)} %get-tuple-element.20), channel_id=1, source_target_pairs={{4,8},{8,4},{12,16},{16,12},{20,24},{24,20},{28,0},{0,28},{5,9},{9... | collective-permute-start | bytes 983048 | tf_op jit(solution)/shard_map/ppermute | solution.py:36
  28.4 0.1 broadcast_in_dim.15.keep_ref
  28.5 14.6 %shard_map.78 = (f32[8,16,16,128]{3,2,1,0:T(8,128)S(1)}, f32[8,2,16,128]{3,2,1,0:T(8,128)S(1)}) custom-call(s32[2]{0:T(128)S(1)} %pad_add_fusion.flag_ref, bf16[8,16,128,128]{3,2,1,0:T(8,128)(2,1)S(1)} %copy-done.1, bf16[8,160,128]{2,1,0:T(8,128)(2,1)S(1)} %collective-permute-done.a_ref.la_ref, bf16[8,160,128]{2,1,0:T(8,128)(2,1)S(1)} %collective-permute-done.1.b_ref.lb_ref, ...), custom_call_target="tpu_custom_call" | custom-call | flops 5435817984 | bytes 8388608 | tf_op jit(solution)/shard_map/pallas_call | solution.py:423
  43.1 0.0 collective-permute-done.2.a_ref.ha_ref
  43.1 0.0 collective-permute-done.3.b_ref.hb_ref
  43.1 8.4 %shard_map.80 = (f32[8,6,16,128]{3,2,1,0:T(8,128)S(1)}, f32[8,4,16,128]{3,2,1,0:T(8,128)S(1)}, bf16[8,96,128]{2,1,0:T(8,128)(2,1)S(1)}, bf16[8,96,128]{2,1,0:T(8,128)(2,1)S(1)}) custom-call(s32[2]{0:T(128)S(1)} %pad_add_fusion.flag_ref, bf16[8,16,128,128]{3,2,1,0:T(8,128)(2,1)S(1)} %copy-done.1, bf16[8,16,128,128]{3,2,1,0:T(8,128)(2,1)S(1)} %copy-done.1, ...), custom_call_target="tpu_custom_call" | custom-call | tf_op jit(solution)/shard_map/pallas_call | solution.py:423
  51.5 0.1 collective-permute-start.4
  51.5 1.4 %collective-permute-start.5 = (bf16[8,96,128]{2,1,0:T(8,128)(2,1)S(1)}, bf16[8,96,128]{2,1,0:T(8,128)(2,1)S(1)}, u32[]{:S(2)}, u32[]{:S(2)}) collective-permute-start(bf16[8,96,128]{2,1,0:T(8,128)(2,1)S(1)} %get-tuple-element.25), channel_id=1, source_target_pairs={{4,8},{8,4},{12,16},{16,12},{20,24},{24,20},{28,0},{0,28},{5,9},{9... | collective-permute-start | bytes 589832 | tf_op jit(solution)/shard_map/ppermute | solution.py:36
  52.9 0.0 collective-permute-done.6.sa_ref
  52.9 0.0 collective-permute-done.7.sb_ref
  52.9 6.9 %collective-permute-done.4.a_ref = bf16[8,96,128]{2,1,0:T(8,128)(2,1)S(1)} collective-permute-done((bf16[8,96,128]{2,1,0:T(8,128)(2,1)S(1)}, bf16[8,96,128]{2,1,0:T(8,128)(2,1)S(1)}, u32[]{:S(2)}, u32[]{:S(2)}) %collective-permute-start.4) | collective-permute-done | bytes 196640 | tf_op jit(solution)/shard_map/ppermute | solution.py:36
  59.9 0.0 collective-permute-done.5.b_ref
  59.9 0.1 broadcast_in_dim.17.b2_ref
  59.9 8.8 %shard_map.81 = (f32[12,8,16,128]{3,2,1,0:T(8,128)}, f32[6,8,16,128]{3,2,1,0:T(8,128)}) custom-call(s32[2]{0:T(128)S(1)} %pad_add_fusion.flag_ref, f32[8,16,16,128]{3,2,1,0:T(8,128)S(1)} %get-tuple-element.18.ps0_ref.ps1_ref.ps_ref, f32[8,6,16,128]{3,2,1,0:T(8,128)S(1)} %get-tuple-element.22.pe_ref, f32[8,4,16,128]{3,2,1,0:T(8,128)S(1)} %get-tuple-element.23.pm_ref, ...), custom_call_target="tpu_custom_call" | custom-call | tf_op jit(solution)/shard_map/pallas_call | solution.py:423
  (19 shorter events, 0.2 us)
Async XLA Ops:
  0.7 2.2 %copy-start.2 = (bf16[8,128,16,128]{3,2,1,0:T(8,128)(2,1)S(1)}, bf16[8,128,16,128]{3,2,1,0:T(8,128)(2,1)}, u32[]{:S(2)}) copy-start(bf16[8,128,16,128]{3,2,1,0:T(8,128)(2,1)} %x_ref.1) | copy-start | bytes 12582916
  2.9 1.0 %copy-start.4 = (f32[6,8,16,128]{3,2,1,0:T(8,128)S(1)}, f32[6,8,16,128]{3,2,1,0:T(8,128)}, u32[]{:S(2)}) copy-start(f32[6,8,16,128]{3,2,1,0:T(8,128)} %st_ref.1) | copy-start | bytes 1179652
  3.9 11.1 %copy-start.5 = (f32[6,8,16,128]{3,2,1,0:T(8,128)S(1)}, f32[6,8,16,128]{3,2,1,0:T(8,128)}, u32[]{:S(2)}) copy-start(f32[6,8,16,128]{3,2,1,0:T(8,128)} %st_ref.1) | copy-start | bytes 1179652
  3.9 16.0 %copy-start.7 = (bf16[3,3,128,12]{2,3,1,0:T(8,128)(2,1)S(1)}, bf16[3,3,128,12]{2,3,1,0:T(8,128)(2,1)}, u32[]{:S(2)}) copy-start(bf16[3,3,128,12]{2,3,1,0:T(8,128)(2,1)} %param.9) | copy-start | bytes 82948
  3.9 16.3 %copy-start.8 = (f32[12]{0:T(128)S(1)}, f32[12]{0:T(128)}, u32[]{:S(2)}) copy-start(f32[12]{0:T(128)} %param.10) | copy-start | bytes 148
  3.9 16.5 %copy-start.6 = (f32[128]{0:T(128)S(1)}, f32[128]{0:T(128)}, u32[]{:S(2)}) copy-start(f32[128]{0:T(128)} %param.8) | copy-start | bytes 1540
  3.9 16.6 %copy-start.3 = (bf16[3,3,128,128]{3,2,1,0:T(8,128)(2,1)S(1)}, bf16[3,3,128,128]{3,2,1,0:T(8,128)(2,1)}, u32[]{:S(2)}) copy-start(bf16[3,3,128,128]{3,2,1,0:T(8,128)(2,1)} %param.7) | copy-start | bytes 884740
  8.6 1.9 %copy-start = (bf16[8,16,128,128]{3,2,1,0:T(8,128)(2,1)}, bf16[8,16,128,128]{3,2,1,0:T(8,128)(2,1)S(1)}, u32[]{:S(2)}) copy-start(bf16[8,16,128,128]{3,2,1,0:T(8,128)(2,1)S(1)} %get-tuple-element.15.g_ref.glo_ref.ghi_ref.g0_ref.g1_ref) | copy-start | bytes 12582916
  10.5 10.1 %collective-permute-start = (bf16[8,160,128]{2,1,0:T(8,128)(2,1)S(1)}, bf16[8,160,128]{2,1,0:T(8,128)(2,1)S(1)}, u32[]{:S(2)}, u32[]{:S(2)}) collective-permute-start(bf16[8,160,128]{2,1,0:T(8,128)(2,1)S(1)} %get-tuple-element.16), channel_id=1, source_target_pairs={{0,1},{1,0},{2,3},{3,2},{4,5},{5,4},{6,7},{7,6},{8,9},{9,8},{10,11... | collective-permute-start | bytes 983048 | tf_op jit(solution)/shard_map/ppermute | solution.py:36
  10.6 10.0 %collective-permute-start.1 = (bf16[8,160,128]{2,1,0:T(8,128)(2,1)S(1)}, bf16[8,160,128]{2,1,0:T(8,128)(2,1)S(1)}, u32[]{:S(2)}, u32[]{:S(2)}) collective-permute-start(bf16[8,160,128]{2,1,0:T(8,128)(2,1)S(1)} %get-tuple-element.17), channel_id=1, source_target_pairs={{1,2},{2,1},{5,6},{6,5},{9,10},{10,9},{13,14},{14,13},{17,18},{18,... | collective-permute-start | bytes 983048 | tf_op jit(solution)/shard_map/ppermute | solution.py:36
  15.1 37.8 %collective-permute-start.6 = (f32[6,8,4,128]{3,2,1,0:T(4,128)S(1)}, f32[6,8,4,128]{3,2,1,0:T(4,128)S(1)}, u32[]{:S(2)}, u32[]{:S(2)}) collective-permute-start(f32[6,8,4,128]{3,2,1,0:T(4,128)S(1)} %get-tuple-element.31), channel_id=1, source_target_pairs={{0,4},{4,0},{8,12},{12,8},{16,20},{20,16},{24,28},{28,24},{1,5},{5... | collective-permute-start | bytes 294920 | tf_op jit(solution)/shard_map/ppermute | solution.py:36
  16.4 36.6 %collective-permute-start.7 = (f32[6,8,4,128]{3,2,1,0:T(4,128)S(1)}, f32[6,8,4,128]{3,2,1,0:T(4,128)S(1)}, u32[]{:S(2)}, u32[]{:S(2)}) collective-permute-start(f32[6,8,4,128]{3,2,1,0:T(4,128)S(1)} %get-tuple-element.30), channel_id=1, source_target_pairs={{4,8},{8,4},{12,16},{16,12},{20,24},{24,20},{28,0},{0,28},{5,9},{9... | collective-permute-start | bytes 294920 | tf_op jit(solution)/shard_map/ppermute | solution.py:36
  20.6 2.2 %copy-start.1 = (bf16[8,16,128,128]{3,2,1,0:T(8,128)(2,1)S(1)}, bf16[8,16,128,128]{3,2,1,0:T(8,128)(2,1)}, u32[]{:S(2)}) copy-start(bf16[8,16,128,128]{3,2,1,0:T(8,128)(2,1)} %copy-done) | copy-start | bytes 12582916
  24.1 19.0 %collective-permute-start.2 = (bf16[8,160,128]{2,1,0:T(8,128)(2,1)S(1)}, bf16[8,160,128]{2,1,0:T(8,128)(2,1)S(1)}, u32[]{:S(2)}, u32[]{:S(2)}) collective-permute-start(bf16[8,160,128]{2,1,0:T(8,128)(2,1)S(1)} %get-tuple-element.19), channel_id=1, source_target_pairs={{0,4},{4,0},{8,12},{12,8},{16,20},{20,16},{24,28},{28,24},{1,5},{5... | collective-permute-start | bytes 983048 | tf_op jit(solution)/shard_map/ppermute | solution.py:36
  25.2 17.9 %collective-permute-start.3 = (bf16[8,160,128]{2,1,0:T(8,128)(2,1)S(1)}, bf16[8,160,128]{2,1,0:T(8,128)(2,1)S(1)}, u32[]{:S(2)}, u32[]{:S(2)}) collective-permute-start(bf16[8,160,128]{2,1,0:T(8,128)(2,1)S(1)} %get-tuple-element.20), channel_id=1, source_target_pairs={{4,8},{8,4},{12,16},{16,12},{20,24},{24,20},{28,0},{0,28},{5,9},{9... | collective-permute-start | bytes 983048 | tf_op jit(solution)/shard_map/ppermute | solution.py:36
  51.5 8.4 %collective-permute-start.4 = (bf16[8,96,128]{2,1,0:T(8,128)(2,1)S(1)}, bf16[8,96,128]{2,1,0:T(8,128)(2,1)S(1)}, u32[]{:S(2)}, u32[]{:S(2)}) collective-permute-start(bf16[8,96,128]{2,1,0:T(8,128)(2,1)S(1)} %get-tuple-element.24), channel_id=1, source_target_pairs={{0,4},{4,0},{8,12},{12,8},{16,20},{20,16},{24,28},{28,24},{1,5},{5... | collective-permute-start | bytes 589832 | tf_op jit(solution)/shard_map/ppermute | solution.py:36
  51.5 8.3 %collective-permute-start.5 = (bf16[8,96,128]{2,1,0:T(8,128)(2,1)S(1)}, bf16[8,96,128]{2,1,0:T(8,128)(2,1)S(1)}, u32[]{:S(2)}, u32[]{:S(2)}) collective-permute-start(bf16[8,96,128]{2,1,0:T(8,128)(2,1)S(1)} %get-tuple-element.25), channel_id=1, source_target_pairs={{4,8},{8,4},{12,16},{16,12},{20,24},{24,20},{28,0},{0,28},{5,9},{9... | collective-permute-start | bytes 589832 | tf_op jit(solution)/shard_map/ppermute | solution.py:36

commit v3 on v0

v3 whole, which is shorter than its diff:
```python
import functools
import math

import jax
import jax.numpy as jnp
from jax import lax
from jax.experimental import pallas as pl
from jax.experimental.pallas import tpu as pltpu
from jax.sharding import PartitionSpec as P

time_step = 0.5
speed_cap = 0.6
cos_floor = 0.5

SIDE = 8
SLOT = 2 * SIDE
WIDE = 128
REACH = 4
VG = 8
VMEM_LIMIT = 24 * 2**20
EDGE_LEVELS = 4
SIDE_LEVELS = 2
PARTS = 1
f32 = jnp.float32
bf16 = jnp.bfloat16


def swap_pairs(count, first, closed):
    pairs = []
    for low in range(first, count, 2):
        high = low + 1
        if high >= count and not closed:
            continue
        pairs += [(low, high % count), (high % count, low)]
    return pairs


def swap(block, axis, first, closed):
    return lax.ppermute(block, axis, swap_pairs(lax.axis_size(axis), first, closed))


def place(row, rows):
    half, par = row // 2, row % 2
    own = 0 <= half < rows // 2
    return (0 if own else 2) + par, SLOT * (half % (rows // 2))


def lanes(shape):
    return lax.broadcasted_iota(jnp.int32, shape, len(shape) - 1)


def roll(x, by):
    by = by % WIDE
    return pltpu.roll(x, by, x.ndim - 1) if by else x


def col_before(mains, sides, at):
    lane = lanes(next(iter(mains.values())).shape)
    new_sides = {k: roll(s, 1) for k, s in sides.items()}
    new_mains = {}
    for row, main in mains.items():
        k, base = at(row)
        new_mains[row] = jnp.where(lane == 0, roll(sides[k], 1 - base - SIDE), roll(main, 1))
        new_sides[k] = jnp.where(lane == base + SIDE, roll(main, base + SIDE + 1), new_sides[k])
    return new_mains, new_sides


def col_after(mains, sides, at):
    lane = lanes(next(iter(mains.values())).shape)
    new_sides = {k: roll(s, -1) for k, s in sides.items()}
    new_mains = {}
    for row, main in mains.items():
        k, base = at(row)
        new_mains[row] = jnp.where(lane == WIDE - 1, roll(sides[k], WIDE - 1 - base - SIDE), roll(main, -1))
        new_sides[k] = jnp.where(lane == base + SIDE - 1, roll(main, base + SIDE - 1), new_sides[k])
    return new_mains, new_sides


def join_taps(x):
    return roll(x[0:SLOT], 1) + x[SLOT : 2 * SLOT] + roll(x[2 * SLOT : 3 * SLOT], -1)


def mix(first, second):
    return jnp.where(lanes(first.shape) % SLOT < SIDE, first, second)


def add_columns(main, side, base):
    lane = lanes(main.shape)
    return main + jnp.where((lane < SIDE) | (lane >= WIDE - SIDE), roll(side, -(base + SIDE)), 0.0)


def two_terms(x):
    first = x.astype(bf16)
    return [first, (x - first.astype(f32)).astype(bf16)]


def nt(lhs, rhs):
    return lax.dot_general(lhs, rhs, (((1,), (1,)), ((), ())), preferred_element_type=f32)


def silu(s):
    return s / (1.0 + jnp.exp(-s))


def shifted(e_ref, start, s_ref, to, count, first=0):
    ch = e_ref.shape[-1]
    for b in range(3):
        lane0 = first + b * ch
        s_ref[to, :, lane0 : lane0 + ch] = e_ref[pl.ds(start - 1 + b, count), :].astype(bf16)


def prep_kernel(flag_ref, n_lat, b2_ref, x_ref, st_ref, w1_ref, w2_ref, b1_ref,
                outa_ref, outb_ref, w1p_ref, w2p_ref, w2o_ref, w2e_ref, b1p_ref, b2o_ref, lat_ref, lats_ref, keep_ref,
                x32_ref, w2s_ref):
    levels, ch, rows, cols = x_ref.shape
    nvar = st_ref.shape[0]
    even = flag_ref[0] == 0

    def one(lv, carry):
        x32_ref[...] = x_ref[lv].astype(f32).reshape(ch * rows, cols)
        lo, hi = (x32_ref[pl.ds(row, ch, stride=rows), :].astype(bf16) for row in (0, rows - 1))
        outa_ref[lv, 0:ch] = jnp.where(even, hi, lo)
        outb_ref[lv, 0:ch] = jnp.where(even, lo, hi)
        x32_ref[0 : 2 * REACH * VG] = jnp.zeros((2 * REACH * VG, WIDE), f32)
        for n in range(nvar):
            x32_ref[pl.ds(n, REACH, stride=VG), :] = st_ref[n, lv, 0:REACH]
            x32_ref[pl.ds(REACH * VG + n, REACH, stride=VG), :] = st_ref[n, lv, rows - REACH :]
        lo = x32_ref[0 : REACH * VG]
        hi = x32_ref[REACH * VG : 2 * REACH * VG]
        outa_ref[lv, ch:] = jnp.concatenate(two_terms(jnp.where(even, hi, lo)), axis=0)
        outb_ref[lv, ch:] = jnp.concatenate(two_terms(jnp.where(even, lo, hi)), axis=0)
        return carry

    lax.fori_loop(0, levels, one, 0)
    size = w1_ref.shape[0]
    w1p_ref[0:size, 0:ch] = w1_ref[...]
    w1p_ref[size:, 0:ch] = jnp.zeros((3 * ch, ch), bf16)
    w1p_ref[0 : 3 * ch, ch:] = jnp.zeros((3 * ch, ch), bf16)
    w1p_ref[3 * ch :, ch:] = w1_ref[...]
    b1p_ref[:, 0:ch] = b1_ref[...]
    b1p_ref[:, ch:] = b1_ref[...]
    w2p_ref[...] = jnp.zeros_like(w2p_ref)
    w2s_ref[0 : 2 * VG] = jnp.zeros((2 * VG, ch), f32)
    for a in range(3):
        for b in range(3):
            w2s_ref[2 * VG : 2 * VG + 2 * nvar] = w2_ref[3 * a + b].astype(f32)
            for part in range(2):
                w2s_ref[part * VG : part * VG + nvar] = w2s_ref[pl.ds(2 * VG + part, nvar, stride=2), :]
            here = w2s_ref[0 : 2 * VG].astype(bf16)
            at = 3 * a + b
            w2o_ref[at * SLOT : (at + 1) * SLOT] = here
            for k in range(2):
                first = (3 * k + b) * SLOT
                w2p_ref[first : first + SLOT, (a + k) * ch : (a + k + 1) * ch] = here
            if a != 1:
                first = (3 * (a // 2) + b) * SLOT
                w2e_ref[first : first + SLOT] = here
    b2o_ref[...] = jnp.zeros_like(b2o_ref)
    for v in range(2 * nvar):
        row = (v % 2) * VG + v // 2
        b2o_ref[row : row + 1] = jnp.full((1, WIDE), b2_ref[v], f32)

    def table(place_in):
        place_in = place_in + flag_ref[2] * cols
        keep = ((place_in >= 0) & (place_in < n_lat)).astype(f32)
        phi = (place_in.astype(f32) + 0.5) * (math.pi / n_lat) - 0.5 * math.pi
        cosine = jnp.maximum(jnp.cos(phi), cos_floor)
        return cosine, 1.0 / cosine, keep

    lane = lanes((VG, WIDE))
    slot = lane % SLOT
    for ref, place_in in ((lat_ref, lane), (lats_ref, jnp.where(slot < SIDE, slot - SIDE, cols + slot - SIDE))):
        for k, x in enumerate(table(place_in)):
            ref[k] = x
    spot = lax.broadcasted_iota(jnp.int32, keep_ref.shape, 0)
    counts = ((spot > 0) & (spot <= SIDE)) | ((spot >= 3 * SIDE - 1) & (spot < 4 * SIDE - 1))
    place_in = jnp.where(spot < SLOT, spot - SIDE, cols - SIDE + spot - SLOT) + flag_ref[2] * cols
    keep_ref[...] = (counts & (place_in >= 0) & (place_in < n_lat)).astype(f32)


def main_kernel(x_ref, st_ref, w1_ref, w2_ref, b1_ref, glo_ref, ghi_ref, first_ref, last_ref, st8_ref, own_ref, ps_ref,
                x32_ref, e_ref, s_ref, h_ref):
    chans, rows, cols = x_ref.shape[1:]
    nvar = st_ref.shape[0]
    half = rows // 2
    pitch = cols + SLOT
    x32_ref[...] = x_ref[0].astype(f32).reshape(chans * rows, cols)

    @pl.when(pl.program_id(0) == 0)
    def _():
        e_ref[...] = jnp.zeros_like(e_ref)
        h_ref[...] = jnp.zeros_like(h_ref)

    sides = [[], []]
    for row in range(rows):
        block = x32_ref[pl.ds(row, chans, stride=rows), :].T
        start = row * pitch + SIDE
        e_ref[start : start + cols] = block
        for k, part in enumerate((block[0:SIDE], block[cols - SIDE :])):
            sides[k].append(part)
        if row < 2:
            glo_ref[0, row] = block.astype(bf16)
        if row >= rows - 2:
            ghi_ref[0, row - (rows - 2)] = block.astype(bf16)
        shifted(e_ref, start, s_ref, row, cols)
    first_ref[0] = jnp.concatenate(sides[0], axis=0).astype(bf16)
    last_ref[0] = jnp.concatenate(sides[1], axis=0).astype(bf16)
    place_in = lax.broadcasted_iota(jnp.int32, (cols, 2 * chans), 0)
    within = (place_in > 0) & (place_in < cols - 1)
    for m in range(half - 1):
        lhs = jnp.concatenate([s_ref[2 * m + r] for r in range(4)], axis=1)
        acc = jnp.dot(lhs, w1_ref[...], preferred_element_type=f32) + b1_ref[...]
        hid = jnp.where(within, silu(acc), 0.0).astype(bf16)
        for k in range(2):
            h_ref[2 * m + 2 + k] = hid[:, k * chans : (k + 1) * chans]
    for m in range(half):
        q = nt(w2_ref[...], jnp.concatenate([h_ref[2 * m + r] for r in range(4)], axis=1))
        for k in range(2):
            ps_ref[0, 2 * m + k] = join_taps(q[k * 3 * SLOT : (k + 1) * 3 * SLOT])
    for n in range(nvar):
        x32_ref[pl.ds(n, rows, stride=VG), :] = st_ref[n, 0]
    lane = lanes((VG, WIDE))
    own = [jnp.zeros((VG, WIDE), f32)] * 2
    for row in range(rows):
        block = x32_ref[row * VG : (row + 1) * VG]
        block = jnp.where(lax.broadcasted_iota(jnp.int32, (VG, WIDE), 0) < nvar, block, 0.0)
        st8_ref[0, row] = block
        par, base = place(row, rows)
        own[par] = jnp.where(lane // SLOT == base // SLOT, roll(block, base + SIDE), own[par])
    own_ref[0, 0], own_ref[0, 1] = own


def pack_kernel(flag_ref, a_ref, b_ref, first_ref, last_ref, own_ref, row_ref, halo_ref, own4_ref, outa_ref, outb_ref):
    cols = a_ref.shape[2]
    ch = row_ref.shape[3]
    even = flag_ref[0] == 0
    lat_even = flag_ref[1] == 0
    got_a, got_b = a_ref[0].astype(f32), b_ref[0].astype(f32)
    low, high = jnp.where(even, got_b, got_a), jnp.where(even, got_a, got_b)
    size = REACH * VG
    states = [x[ch : ch + size] + x[ch + size : ch + 2 * size] for x in (low, high)]
    low, high = low[0:ch].T, high[0:ch].T
    row_ref[0, 0] = low.astype(bf16)
    row_ref[0, 1] = high.astype(bf16)
    rows = first_ref.shape[1] // SIDE
    lane = lanes((VG, WIDE))
    own = [jnp.zeros((VG, WIDE), f32)] * 2
    for k in range(2 * REACH):
        row = k - REACH if k < REACH else rows + k - REACH
        block = states[k // REACH][(k % REACH) * VG : (k % REACH + 1) * VG]
        halo_ref[0, k] = block
        at, base = place(row, rows)
        own[at - 2] = jnp.where(lane // SLOT == base // SLOT, roll(block, base + SIDE), own[at - 2])
    own = [own_ref[0, 0], own_ref[0, 1]] + own
    terms = []
    for k in range(4):
        own4_ref[0, k] = own[k]
        terms += two_terms(own[k])
    first = [low[0:SIDE].astype(bf16), first_ref[0], high[0:SIDE].astype(bf16)]
    last = [low[cols - SIDE :].astype(bf16), last_ref[0], high[cols - SIDE :].astype(bf16)]
    first, last = jnp.concatenate(first, axis=0), jnp.concatenate(last, axis=0)
    count = first.shape[0]
    for out, pick in ((outa_ref, jnp.where(lat_even, last, first)), (outb_ref, jnp.where(lat_even, first, last))):
        out[0, 0:count] = pick
        out[0, count:] = jnp.concatenate(terms, axis=0)


def edge_kernel(row_ref, g0_ref, g1_ref, w1_ref, w2_ref, b1_ref, ps0_ref, ps1_ref, pe_ref, e_ref, s_ref, h_ref):
    levels = row_ref.shape[0]
    cols, ch = row_ref.shape[2:]
    pitch = cols + SLOT
    e_ref[...] = jnp.zeros_like(e_ref)
    for lv in range(levels):
        for k in range(2):
            part = [g0_ref[lv, 0], g0_ref[lv, 1]] if k == 0 else [g1_ref[lv, 0], g1_ref[lv, 1]]
            part = [row_ref[lv, 0]] + part if k == 0 else part + [row_ref[lv, 1]]
            for r in range(3):
                start = (6 * lv + 3 * k + r) * pitch + SIDE
                e_ref[start : start + cols] = part[r].astype(f32)
                shifted(e_ref, start, s_ref, 2 * lv + k, cols, 3 * ch * r)
    acc = jnp.dot(s_ref[...].reshape(2 * levels * cols, 9 * ch), w1_ref[...], preferred_element_type=f32) + b1_ref[...]
    place_in = lax.broadcasted_iota(jnp.int32, (cols, ch), 0)
    within = (place_in > 0) & (place_in < cols - 1)
    hid = silu(acc)
    for n in range(2 * levels):
        here = slice(n * cols, (n + 1) * cols)
        h_ref[here] = jnp.where(within, hid[here], 0.0).astype(bf16)
    q = nt(w2_ref[...], h_ref[...])
    for lv in range(levels):
        for k in range(2):
            here = slice((2 * lv + k) * cols, (2 * lv + k + 1) * cols)
            for a in range(3):
                x = join_taps(q[a * 3 * SLOT : (a + 1) * 3 * SLOT, here])
                if k == 0 and a < 2:
                    x = x + ps0_ref[lv, 1 - a]
                if k == 1 and a > 0:
                    x = x + ps1_ref[lv, 4 - a]
                pe_ref[lv, 3 * k + 2 - a] = x


def side_kernel(flag_ref, first_ref, last_ref, row_ref, la_ref, lb_ref, own_ref, w1_ref, w2_ref, w2e_ref, b1_ref, keep_ref,
                pe_ref, ps0_ref, ps1_ref, sst_ref, pm_ref, cm_ref, pec_ref, outa_ref, outb_ref, e_ref, s_ref, hs_ref, z_ref):
    levels = row_ref.shape[0]
    cols, ch = row_ref.shape[2:]
    rows = first_ref.shape[1] // SIDE
    half = rows // 2
    even = flag_ref[0] == 0
    lat_even = flag_ref[1] == 0
    wide = 2 * SLOT
    total = (rows + 2) * wide
    lane = lanes((2 * VG, WIDE))
    begin, end = lane < SLOT, lane >= WIDE - SLOT
    e_ref[...] = jnp.zeros_like(e_ref)
    hs_ref[...] = jnp.zeros_like(hs_ref)
    z_ref[...] = jnp.zeros_like(z_ref)
    for lv in range(levels):
        a, b = la_ref[lv], lb_ref[lv]
        right, left = jnp.where(lat_even, a, b), jnp.where(lat_even, b, a)
        count = (rows + 2) * SIDE
        for k in range(4):
            st = []
            for x in (left, right):
                x = x[count + 2 * k * VG : count + (2 * k + 2) * VG].astype(f32)
                st.append(x[0:VG] + x[VG:])
            sst_ref[lv, k] = mix(st[0], st[1])
        right, left = right[0:count].astype(f32), left[0:count].astype(f32)
        first, last = first_ref[lv].astype(f32), last_ref[lv].astype(f32)
        low, high = row_ref[lv, 0].astype(f32), row_ref[lv, 1].astype(f32)
        for row in range(-1, rows + 1):
            side = slice((row + 1) * SIDE, (row + 2) * SIDE)
            if 0 <= row < rows:
                own = slice(row * SIDE, (row + 1) * SIDE)
                mine = first[own], last[own]
            else:
                x = low if row < 0 else high
                mine = x[0:SIDE], x[cols - SIDE :]
            start = SIDE + (row + 1) * wide
            for k, part in enumerate((left[side], mine[0], mine[1], right[side])):
                e_ref[lv, start + k * SIDE : start + (k + 1) * SIDE] = part
        for b in range(3):
            s_ref[:, b * ch : (b + 1) * ch] = e_ref[lv, pl.ds(SIDE - 1 + b, total), :].astype(bf16)
        s = s_ref[...].reshape(half + 1, 2, wide, 3 * ch)
        part = [s[0:half, 0], s[0:half, 1], s[1:, 0], s[1:, 1]]
        lhs = jnp.concatenate([p.reshape(half * wide, 3 * ch) for p in part], axis=1)
        acc = jnp.dot(lhs, w1_ref[...], preferred_element_type=f32) + b1_ref[...]
        hid = silu(acc).reshape(half, wide, 2 * ch) * keep_ref[...]
        for m in range(half):
            for side in range(2):
                here = hid[m, side * SLOT : (side + 1) * SLOT].astype(bf16)
                hs_ref[lv, side, 0, m * SLOT : (m + 1) * SLOT] = here[:, 0:ch]
                hs_ref[lv, side, 1, (m + 1) * SLOT : (m + 2) * SLOT] = here[:, ch:]
                if m == 0:
                    z_ref[lv, side * SLOT : (side + 1) * SLOT] = here[:, 0:ch]
                if m == half - 1:
                    z_ref[lv, (2 + side) * SLOT : (3 + side) * SLOT] = here[:, ch:]
        tiles = []
        for side in range(2):
            odd, ev = hs_ref.at[lv, side, 1], hs_ref.at[lv, side, 0]
            size = half * SLOT
            rhs = [odd[0:size], ev[0:size], odd[SLOT : size + SLOT], ev[SLOT : size + SLOT]]
            q = nt(w2_ref[...], jnp.concatenate(rhs, axis=1))
            tiles.append([join_taps(q[k * 3 * SLOT : (k + 1) * 3 * SLOT]) for k in range(2)])
        q = nt(w2e_ref[...], z_ref[lv])
        prev = join_taps(q[3 * SLOT : 6 * SLOT])
        nxt = join_taps(q[0 : 3 * SLOT])
        out, inn = {}, {}
        for k in range(2):
            out[k] = mix(tiles[0][k], tiles[1][k])
            inn[k] = mix(tiles[1][k], tiles[0][k])
        for k, x, s0 in ((3, prev, 0), (2, nxt, 2)):
            spot = end if k == 3 else begin
            to = WIDE - SLOT if k == 3 else 0
            at_l, at_r = roll(x, to - s0 * SLOT), roll(x, to - (s0 + 1) * SLOT)
            out[k] = jnp.where(spot, mix(at_l, at_r), 0.0)
            inn[k] = jnp.where(spot, mix(at_r, at_l), 0.0)
        for k in range(4):
            pm_ref[lv, k] = out[k]
            cm_ref[lv, k] = inn[k]
        mains = {}
        for k, row in enumerate((-1, 0, 1, rows - 2, rows - 1, rows)):
            mains[row] = pe_ref[lv, k]
        mains[2], mains[3] = ps0_ref[lv, 2], ps0_ref[lv, 3]
        mains[rows - 4], mains[rows - 3] = ps1_ref[lv, 0], ps1_ref[lv, 1]
        for row in mains:
            k, base = place(row, rows)
            mains[row] = add_columns(mains[row], inn[k], base)
        for k, row in enumerate((-1, 0, 1, rows - 2, rows - 1, rows)):
            pec_ref[lv, k] = mains[row]
        side_lo = jnp.where(lane < 2 * SLOT, out[0], jnp.where(lane < 4 * SLOT, roll(out[1], 2 * SLOT), out[3]))
        side_hi = jnp.where(lane >= WIDE - 2 * SLOT, out[0],
                            jnp.where(lane >= WIDE - 4 * SLOT, roll(out[1], -2 * SLOT), out[2]))
        out_lo = jnp.concatenate([mains[-1], mains[0], mains[1], mains[2], side_lo, mains[3]], axis=0)
        out_hi = jnp.concatenate([mains[rows - k] for k in range(4)] + [side_hi, mains[rows - 4]], axis=0)
        outa_ref[lv] = jnp.where(even, out_hi, out_lo).astype(bf16)
        outb_ref[lv] = jnp.where(even, out_lo, out_hi).astype(bf16)


def advect_kernel(flag_ref, ps_ref, pe_ref, pm_ref, cm_ref, a_ref, b_ref, st8_ref, halo_ref, sst_ref,
                  b2_ref, lat_ref, lats_ref, *rest):
    vel_ref, ten_ref, out_ref = rest[-3:]
    rows = st8_ref.shape[1]
    nvar = ten_ref.shape[0]
    even = flag_ref[0] == 0
    lane16 = lanes((2 * VG, WIDE))
    lane = lanes((VG, WIDE))
    pair = 2 * VG

    def halos(xa, xb):
        return jnp.where(even, xb, xa), jnp.where(even, xa, xb)

    lo, hi = halos(a_ref[0].astype(f32), b_ref[0].astype(f32))
    main = {}
    for row in range(2, rows - 2):
        k, base = place(row, rows)
        main[row] = add_columns(ps_ref[0, row], cm_ref[0, k], base)
    for k, row in enumerate((-1, 0, 1, rows - 2, rows - 1, rows)):
        main[row] = pe_ref[0, k]
    for k in range(REACH + 1):
        there = slice(k * pair, (k + 1) * pair) if k < REACH else slice((k + 1) * pair, (k + 2) * pair)
        for got, row in ((lo, -k), (hi, rows - 1 + k)):
            main[row] = main[row] + got[there] if row in main else got[there]
    slo, shi = (got[REACH * pair : (REACH + 1) * pair] for got in (lo, hi))
    zero = jnp.zeros((pair, WIDE), f32)
    last, front = lane16 >= WIDE - 2 * SLOT, lane16 < 2 * SLOT
    side = {
        0: pm_ref[0, 0] + jnp.where(lane16 < SLOT, slo, zero),
        1: pm_ref[0, 1] + jnp.where(lane16 >= WIDE - SLOT, shi, zero),
        2: pm_ref[0, 2] + jnp.where(last, slo, jnp.where(front, shi, zero)),
        3: pm_ref[0, 3] + jnp.where(last, roll(slo, 2 * SLOT), jnp.where(front, roll(shi, -2 * SLOT), zero)),
    }
    bias = b2_ref[...]
    main = {r: speed_cap * jnp.tanh(x + bias) for r, x in main.items()}
    side = {k: speed_cap * jnp.tanh(x + bias) * lats_ref[2, 0:1] for k, x in side.items()}
    for part in range(2):
        for row in range(rows):
            out_ref[part, row * VG : (row + 1) * VG] = main[row][part * VG : (part + 1) * VG]
        for n in range(nvar):
            vel_ref[2 * n + part, 0] = out_ref[part, pl.ds(n, rows, stride=VG), :]

    q0 = {row: st8_ref[0, row] for row in range(rows)}
    for k in range(REACH):
        q0[k - REACH] = halo_ref[0, k]
        q0[rows + k] = halo_ref[0, REACH + k]
    s0 = {k: sst_ref[0, k] for k in range(4)}

    def at(row):
        return place(row, rows)

    def side_rows(s):
        def turned(own, halo, by, first):
            own, halo = roll(own, by), roll(halo, by)
            return jnp.where(first, halo, own), jnp.where(first, own, halo)

        odd_back = turned(s[1], s[3], SLOT, lane < SLOT)
        even_on = turned(s[0], s[2], -SLOT, lane >= WIDE - SLOT)
        before = {0: odd_back[0], 2: odd_back[1], 1: s[0], 3: s[2]}
        after = {0: s[1], 2: s[3], 1: even_on[0], 3: even_on[1]}
        return before, after

    u = {r: x[0:VG] for r, x in main.items()}
    us = {k: x[0:VG] for k, x in side.items()}
    inside = range(1 - REACH, rows + REACH - 1)
    v = {r: main[r][VG:] for r in inside}
    vs = {k: x[VG:] for k, x in side.items()}
    cosine, metric = lat_ref[0], lat_ref[1]
    cosine_s, metric_s = lats_ref[0], lats_ref[1]
    flux = {r: x * cosine for r, x in v.items()}
    flux_s = {k: x * cosine_s for k, x in vs.items()}
    fb, fbs = col_before(flux, flux_s, at)
    fa, fas = col_after(flux, flux_s, at)
    ub, ua = side_rows(us)

    def coefs(m, uu, vv, udiff, vdiff):
        div = m * (udiff * 0.5 + vdiff * 0.5)
        cl = m * jnp.maximum(uu, 0.0)
        cr = -(m * jnp.minimum(uu, 0.0))
        cd = jnp.maximum(vv, 0.0)
        cu = -jnp.minimum(vv, 0.0)
        return -(cl + cr + cd + cu + div), cl, cr, cd, cu

    cm = {r: coefs(metric, u[r], v[r], u[r + 1] - u[r - 1], fa[r] - fb[r]) for r in inside}
    cs = {k: coefs(metric_s, us[k], vs[k], ua[k] - ub[k], fas[k] - fbs[k]) for k in range(4)}

    def stencil(c, x, left, right, down, up):
        return c[0] * x + c[1] * left + c[2] * right + c[3] * down + c[4] * up

    def rate(q, s, depth):
        centre = {r: q[r] for r in range(depth - REACH, rows + REACH - depth)}
        qb, sb = col_before(centre, s, at)
        qa, sa = col_after(centre, s, at)
        rb, ra = side_rows(s)
        out = {r: stencil(cm[r], q[r], q[r - 1], q[r + 1], qb[r], qa[r]) for r in centre}
        if depth == REACH:
            return out, None
        return out, {k: stencil(cs[k], s[k], rb[k], ra[k], sb[k], sa[k]) for k in range(4)}

    def moved(rates, by):
        return {r: q0[r] + by * x for r, x in rates[0].items()}, {k: s0[k] + by * x for k, x in rates[1].items()}

    one = rate(q0, s0, 1)
    two = rate(*moved(one, 0.5 * time_step), 2)
    three = rate(*moved(two, 0.5 * time_step), 3)
    four = rate(*moved(three, time_step), 4)
    for row in range(rows):
        ten = (one[0][row] + 2.0 * two[0][row] + 2.0 * three[0][row] + four[0][row]) / 6.0
        out_ref[0, row * VG : (row + 1) * VG] = ten
    for n in range(nvar):
        ten_ref[n, 0] = out_ref[0, pl.ds(n, rows, stride=VG), :]


def full(shape):
    return pl.BlockSpec(shape, lambda *i: (0,) * len(shape))


def per_level(shape):
    return pl.BlockSpec((1,) + shape[1:], lambda i: (i,) + (0,) * (len(shape) - 1))


def level_part(shape, index, block=1, offset=0):
    return pl.BlockSpec((block,) + shape, lambda i: (i + offset, index) + (0,) * (len(shape) - 1))


def levels_of(shape, block=1, offset=0):
    return pl.BlockSpec((block,) + shape[1:], lambda i: (i + offset,) + (0,) * (len(shape) - 1))


def var_level(shape, offset=0):
    return pl.BlockSpec((shape[0], 1) + shape[2:], lambda i: (0, i + offset, 0, 0))


def body(hidden_in, w_conv1, b_conv1, w_conv2, b_conv2, state):
    lev, ch, rows, cols = hidden_in.shape
    nvar = state.shape[0]
    ext = cols + SLOT
    half = rows // 2
    params = pltpu.CompilerParams(vmem_limit_bytes=VMEM_LIMIT)
    smem = pl.BlockSpec(memory_space=pltpu.SMEM)
    sds = jax.ShapeDtypeStruct

    def call(kernel, steps, ins, outs, out_specs, scratch, args, cost=None, aliases={}):
        return pl.pallas_call(
            kernel,
            grid=(steps,),
            in_specs=ins,
            out_specs=out_specs,
            out_shape=outs,
            scratch_shapes=scratch,
            compiler_params=params,
            cost_estimate=cost,
            input_output_aliases=aliases,
        )(*args)

    flags = jnp.stack([lax.axis_index("lon") % 2, lax.axis_index("lat") % 2, lax.axis_index("lat")]).astype(jnp.int32)
    lon_wire = (lev, ch + 2 * REACH * VG, WIDE)
    shapes = [(lon_wire, bf16), (lon_wire, bf16), ((12 * ch, 2 * ch), bf16), ((6 * SLOT, 4 * ch), bf16), ((9 * SLOT, ch), bf16),
              ((6 * SLOT, ch), bf16), ((1, 2 * ch), f32), ((2 * VG, WIDE), f32), ((3, VG, WIDE), f32), ((3, VG, WIDE), f32),
              ((2 * SLOT, 2 * ch), f32)]
    vmem = pl.BlockSpec(memory_space=pltpu.VMEM)
    w1_one = w_conv1.reshape(9 * ch, ch)
    b1 = b_conv1.reshape(1, ch)
    n_lat = cols * lax.axis_size("lat")
    lon_a, lon_b, w1_pair, w2_pair, w2_one, w2_ends, b1_pair, b2, lat_main, lat_side, keep = pl.pallas_call(
        lambda flag_ref, *refs: prep_kernel(flag_ref, n_lat, *refs),
        in_specs=[smem, smem] + [vmem] * 5,
        out_specs=[vmem] * len(shapes),
        out_shape=[sds(*x) for x in shapes],
        scratch_shapes=[pltpu.VMEM((ch * rows, cols), f32), pltpu.VMEM((4 * VG, ch), f32)],
        compiler_params=params,
    )(flags, b_conv2, hidden_in, state, w1_one, w_conv2.transpose(0, 1, 3, 2).reshape(9, 2 * nvar, ch), b1)
    lon_a = swap(lon_a, "lon", 0, True)
    lon_b = swap(lon_b, "lon", 1, True)

    hbm = pl.BlockSpec(memory_space=pltpu.HBM)
    g_pair = (lev, 2, cols, ch)
    st8_shape = (lev, rows, VG, WIDE)
    cut = (lev, rows * SIDE, ch)
    ps_shape = (lev, rows, 2 * VG, WIDE)
    own_shape = (lev, 2, VG, WIDE)
    shapes = [(g_pair, bf16), (g_pair, bf16), (cut, bf16), (cut, bf16), (st8_shape, f32), (own_shape, f32), (ps_shape, f32)]
    g_lo, g_hi, first, last, st8, own, ps = call(
        main_kernel,
        lev,
        [per_level(hidden_in.shape), var_level(state.shape), full(w1_pair.shape), full(w2_pair.shape), full((1, 2 * ch))],
        [sds(*x) for x in shapes],
        [per_level(x[0]) for x in shapes],
        [
            pltpu.VMEM((ch * rows, cols), f32),
            pltpu.VMEM((rows * (cols + SLOT), ch), f32),
            pltpu.VMEM((rows, cols, 3 * ch), bf16),
            pltpu.VMEM((rows + 2, cols, ch), bf16),
        ],
        (hidden_in, state, w1_pair, w2_pair, b1_pair),
        pl.CostEstimate(flops=2 * lev * rows * ext * 9 * ch * ch, bytes_accessed=8 * 2**20, transcendentals=0),
    )

    lat_wire = (lev, (rows + 2) * SIDE + 8 * VG, WIDE)
    pair_shape = (lev, 2, cols, ch)
    halo_shape = (lev, 2 * REACH, VG, WIDE)
    own4_shape = (lev, 4, VG, WIDE)
    shapes = [(pair_shape, bf16), (halo_shape, f32), (own4_shape, f32), (lat_wire, bf16), (lat_wire, bf16)]
    row_pair, halo, own4, lat_a, lat_b = call(
        pack_kernel,
        lev,
        [smem, per_level(lon_wire), per_level(lon_wire), per_level(cut), per_level(cut), per_level(own_shape)],
        [sds(*x) for x in shapes],
        [per_level(x[0]) for x in shapes],
        [],
        (flags, lon_a, lon_b, first, last, own),
    )
    lat_a = swap(lat_a, "lat", 0, False)
    lat_b = swap(lat_b, "lat", 1, False)

    block = EDGE_LEVELS
    four = (4, 2 * VG, WIDE)
    pe_shape = (lev, 6, 2 * VG, WIDE)
    here = functools.partial(levels_of, block=block)
    (pe,) = call(
        edge_kernel,
        lev // block,
        [here(pair_shape), here(g_pair), here(g_pair), full(w1_one.shape), full(w2_one.shape), full((1, ch)),
         level_part(four, 0, block), level_part(four, rows // 4 - 1, block)],
        [sds(pe_shape, f32)],
        [here(pe_shape)],
        [
            pltpu.VMEM((6 * block * (cols + SLOT), ch), f32),
            pltpu.VMEM((2 * block, cols, 9 * ch), bf16),
            pltpu.VMEM((2 * block * cols, ch), bf16),
        ],
        (row_pair, g_lo, g_hi, w1_one, w2_one, b1, ps, ps),
        pl.CostEstimate(flops=lev * 2 * 2 * ext * 9 * ch * ch, bytes_accessed=4 * 2**20, transcendentals=0),
    )

    block = SIDE_LEVELS
    parts = PARTS
    count = lev // parts
    wire = (count, 2 * VG * (REACH + 2), WIDE)
    pec_shape = (count,) + pe_shape[1:]
    pm4_shape = (count, 4, 2 * VG, WIDE)
    sst_shape = (count, 4, VG, WIDE)
    shapes = [(sst_shape, f32), (pm4_shape, f32), (pm4_shape, f32), (pec_shape, f32), (wire, bf16), (wire, bf16)]
    sent = []
    for part in range(parts):
        off = part * count // block
        here = functools.partial(levels_of, block=block, offset=off)
        sst, pm, cm, pec, out_a, out_b = call(
            side_kernel,
            count // block,
            [smem, here(cut), here(cut), here(pair_shape), here(lat_wire), here(lat_wire), here(own4_shape),
             full(w1_pair.shape), full(w2_pair.shape), full(w2_ends.shape), full((1, 2 * ch)), full((2 * SLOT, 2 * ch)),
             here(pe_shape), level_part(four, 0, block, off), level_part(four, rows // 4 - 1, block, off)],
            [sds(*x) for x in shapes],
            [levels_of(x[0], block) for x in shapes],
            [
                pltpu.VMEM((block, (rows + 2) * 2 * SLOT + 2 * SIDE, ch), f32),
                pltpu.VMEM(((rows + 2) * 2 * SLOT, 3 * ch), bf16),
                pltpu.VMEM((block, 2, 2, (half + 1) * SLOT, ch), bf16),
                pltpu.VMEM((block, WIDE, ch), bf16),
            ],
            (flags, first, last, row_pair, lat_a, lat_b, own4, w1_pair, w2_pair, w2_ends, b1_pair, keep, pe, ps, ps),
            pl.CostEstimate(flops=count * 512 * 12 * ch * ch, bytes_accessed=4 * 2**20, transcendentals=0),
        )
        sent.append((pec, pm, cm, sst, swap(out_a, "lon", 0, True), swap(out_b, "lon", 1, True)))

    outs = [sds((2 * nvar, lev, rows, cols), f32), sds(state.shape, f32)]
    done = ()
    for part, (pec, pm, cm, sst, out_a, out_b) in enumerate(sent):
        off = part * count
        here = functools.partial(levels_of, offset=off)
        var = functools.partial(var_level, offset=off)
        done = call(
            advect_kernel,
            count,
            [smem, here(ps_shape), per_level(pec_shape), per_level(pm4_shape), per_level(pm4_shape), per_level(wire),
             per_level(wire), here(st8.shape), here(halo_shape), per_level(sst_shape),
             full(b2.shape), full(lat_main.shape), full(lat_side.shape)] + [hbm] * len(done),
            outs,
            [var(o.shape) for o in outs],
            [pltpu.VMEM((2, rows * VG, WIDE), f32)],
            (flags, ps, pec, pm, cm, out_a, out_b, st8, halo, sst, b2, lat_main, lat_side) + tuple(done),
            pl.CostEstimate(flops=count * 2**24, bytes_accessed=2 * 2**20, transcendentals=0),
            {13: 0, 14: 1} if done else {},
        )
    return tuple(done)


def solution(mesh):
    placed = (P(None, None, "lon", "lat"), P(), P(), P(), P(), P(None, None, "lon", "lat"))
    return jax.shard_map(
        body,
        mesh=mesh,
        in_specs=placed,
        out_specs=(P(None, None, "lon", "lat"), P(None, None, "lon", "lat")),
        check_vma=False,
    )
```

time: 252 us -> 67.2 us (0.27)
  local copies, waits for them, and re-layouts: 120 us -> 6.23 us
  Pallas kernels: 0 us -> 38.7 us
  waiting for transfers between devices: 39 us -> 7.58 us
  matrix products: 31.2 us -> 0 us
  other arithmetic: 26.1 us -> 0.08 us
  starting transfers between devices: 32 us -> 13.6 us
    dynamic_update_slice x16 -> x0, local copies, waits for them, and re-layouts: 47 us -> none  [body(): wide = jnp.transpose(lax.map(level, padded), (1, 0, 2, 3))]
    pallas_call x0 -> x6, Pallas kernels: none -> 38.7 us  [the longest x5 37 us: call(): pl.pallas_call(kernel, grid=(steps,), in_specs=ins, out_specs=out_specs,...]
    ppermute x20 -> x6, waiting for transfers between devices: 39 us -> 7.58 us  [swap(): lax.ppermute(block, axis, swap_pairs(lax.axis_size(axis), first, closed))]
    dot_general x16 -> x0, matrix products: 31.2 us -> none  [conv_block(): jnp.einsum('tcxy,tco->oxy', taps, stacked, preferred_element_type=jnp.flo...]
    while x128 -> x0, local copies, waits for them, and re-layouts: 20.9 us -> none
    ppermute x20 -> x6, starting transfers between devices: 32 us -> 13.6 us  [swap(): lax.ppermute(block, axis, swap_pairs(lax.axis_size(axis), first, closed))]
    mul x14 -> x0, other arithmetic: 11.9 us -> none  [the longest x1 6.47 us: body(): padded = padded * lat_profile(in_width, lat_dev)[0].astype(jnp.bfloat16)]
    unnamed x30 -> x18, local copies, waits for them, and re-layouts: 18 us -> 6.23 us
  transfers between devices with their start and end apart: 20 -> 6, of which waited for: 9 -> 3; matrix products, arithmetic and copies ran while one was open for 10% -> 0% of each run, Pallas kernels for 0% -> 26%
where the time goes in v3:
time: 67.2 us; the launch traced here: 66.9 us
  Pallas kernels  38.7 us (58%)
  starting transfers between devices  13.6 us (20%)
  waiting for transfers between devices  7.58 us (11%)
  local copies, waits for them, and re-layouts  6.23 us (9%)
  between operations  0.74 us (1%)
    pallas_call x5, Pallas kernels, call(): pl.pallas_call(kernel, grid=(steps,), in_specs=ins, out_specs=out_specs,...  37 us
    ppermute x6, starting transfers between devices, swap(): lax.ppermute(block, axis, swap_pairs(lax.axis_size(axis), first, closed))  13.6 us
    ppermute x6, waiting for transfers between devices, swap(): lax.ppermute(block, axis, swap_pairs(lax.axis_size(axis), first, closed))  7.58 us
    unnamed x18, local copies, waits for them, and re-layouts  6.23 us
    pallas_call x1, Pallas kernels, body(): pl.pallas_call(lambda flag_ref, *refs: prep_kernel(flag_ref, n_lat, *refs...  1.72 us
  transfers between devices with their start and end apart: 6, of which 3 were waited for; matrix products, arithmetic and copies ran while one was open for 0% of the time, Pallas kernels for 26%

profile of v3, /device:TPU:1, one launch (start us, length us, event | category | flops | bytes accessed | tf_op | source)
XLA Modules:
  0.0 66.9 jit_solution(5254842315500019746)
XLA Ops:
  0.6 0.1 pad_add_fusion.flag_ref
  0.7 0.0 copy-start
  0.7 2.2 %copy-done = bf16[8,128,16,128]{3,2,1,0:T(8,128)(2,1)S(1)} copy-done((bf16[8,128,16,128]{3,2,1,0:T(8,128)(2,1)S(1)}, bf16[8,128,16,128]{3,2,1,0:T(8,128)(2,1)}, u32[]{:S(2)}) %copy-start) | copy-done | bytes 4194328
  2.9 0.0 copy-start.2
  2.9 1.0 %copy-done.2 = bf16[3,3,128,128]{3,2,1,0:T(8,128)(2,1)S(1)} copy-done((bf16[3,3,128,128]{3,2,1,0:T(8,128)(2,1)S(1)}, bf16[3,3,128,128]{3,2,1,0:T(8,128)(2,1)}, u32[]{:S(2)}) %copy-start.2) | copy-done | bytes 294936
  3.9 0.0 copy-start.4
  3.9 1.0 %copy-done.4 = f32[6,8,16,128]{3,2,1,0:T(8,128)S(1)} copy-done((f32[6,8,16,128]{3,2,1,0:T(8,128)S(1)}, f32[6,8,16,128]{3,2,1,0:T(8,128)}, u32[]{:S(2)}) %copy-start.4) | copy-done | bytes 393240
  4.9 0.0 copy-start.6
  4.9 0.8 %copy-done.6 = bf16[3,3,128,12]{2,3,1,0:T(8,128)(2,1)S(1)} copy-done((bf16[3,3,128,12]{2,3,1,0:T(8,128)(2,1)S(1)}, bf16[3,3,128,12]{2,3,1,0:T(8,128)(2,1)}, u32[]{:S(2)}) %copy-start.6) | copy-done | bytes 27672
  5.6 0.0 copy-start.7
  5.6 0.7 copy-done.7
  6.3 0.0 copy-start.8
  6.3 0.7 copy-done.8
  7.0 0.0 copy-start.1
  7.0 0.0 copy-start.5
  7.0 1.7 %shard_map.77 = (bf16[8,192,128]{2,1,0:T(8,128)(2,1)S(1)}, bf16[8,192,128]{2,1,0:T(8,128)(2,1)S(1)}, bf16[1536,256]{1,0:T(8,128)(2,1)S(1)}, bf16[96,512]{1,0:T(8...) custom-call(s32[3]{0:T(128)S(1)} %pad_add_fusion.flag_ref, ...), custom_call_target="tpu_custom_call" | custom-call | tf_op jit(solution)/shard_map/pallas_call | solution.py:562
  8.7 2.1 %collective-permute-start = (bf16[8,192,128]{2,1,0:T(8,128)(2,1)S(1)}, bf16[8,192,128]{2,1,0:T(8,128)(2,1)S(1)}, u32[]{:S(2)}, u32[]{:S(2)}) collective-permute-start(bf16[8,192,128]{2,1,0:T(8,128)(2,1)S(1)} %get-tuple-element.37), channel_id=1, source_target_pairs={{0,4},{4,0},{8,12},{12,8},{16,20},{20,16},{24,28},{28,24},{1,5},{5... | collective-permute-start | bytes 1179656 | tf_op jit(solution)/shard_map/ppermute | solution.py:39
  10.8 3.3 %collective-permute-start.1 = (bf16[8,192,128]{2,1,0:T(8,128)(2,1)S(1)}, bf16[8,192,128]{2,1,0:T(8,128)(2,1)S(1)}, u32[]{:S(2)}, u32[]{:S(2)}) collective-permute-start(bf16[8,192,128]{2,1,0:T(8,128)(2,1)S(1)} %get-tuple-element.38), channel_id=1, source_target_pairs={{4,8},{8,4},{12,16},{16,12},{20,24},{24,20},{28,0},{0,28},{5,9},{9... | collective-permute-start | bytes 1179656 | tf_op jit(solution)/shard_map/ppermute | solution.py:39
  14.1 0.0 copy-done.1
  14.1 0.0 copy-done.5
  14.1 0.0 copy-start.3
  14.1 14.9 %shard_map.78 = (bf16[8,2,128,128]{3,2,1,0:T(8,128)(2,1)S(1)}, bf16[8,2,128,128]{3,2,1,0:T(8,128)(2,1)S(1)}, bf16[8,128,128]{2,1,0:T(8,128)(2,1)S(1)}, bf16[8,12...) custom-call(bf16[8,128,16,128]{3,2,1,0:T(8,128)(2,1)S(1)} %copy-done, ...), custom_call_target="tpu_custom_call" | custom-call | flops 5435817984 | bytes 8388608 | tf_op jit(solution)/shard_map/pallas_call | solution.py:541
  29.0 0.0 collective-permute-done.a_ref
  29.0 0.0 collective-permute-done.1.b_ref
  29.0 1.6 %shard_map.79 = (bf16[8,2,128,128]{3,2,1,0:T(8,128)(2,1)S(1)}, f32[8,8,8,128]{3,2,1,0:T(8,128)S(1)}, f32[8,4,8,128]{3,2,1,0:T(8,128)S(1)}, bf16[8,208,128]{2,1,0:T(8,128)(2,1)S(1)}, bf16[8,208,128]{2,1,0:T(8,128)(2,1)S(1)}) custom-call(s32[3]{0:T(128)S(1)} %pad_add_fusion.flag_ref, bf16[8,192,128]{2,1,0:T(8,128)(2,1)S(1)} %collective-permute-done.a_ref, ...), custom_call_target="tpu_custom_call" | custom-call | tf_op jit(solution)/shard_map/pallas_call | solution.py:541
  30.6 1.3 %collective-permute-start.2 = (bf16[8,208,128]{2,1,0:T(8,128)(2,1)S(1)}, bf16[8,208,128]{2,1,0:T(8,128)(2,1)S(1)}, u32[]{:S(2)}, u32[]{:S(2)}) collective-permute-start(bf16[8,208,128]{2,1,0:T(8,128)(2,1)S(1)} %get-tuple-element.41), channel_id=1, source_target_pairs={{0,1},{1,0},{2,3},{3,2},{4,5},{5,4},{6,7},{7,6},{8,9},{9,8},{10,11... | collective-permute-start | bytes 1277960 | tf_op jit(solution)/shard_map/ppermute | solution.py:39
  31.9 3.0 %collective-permute-start.3 = (bf16[8,208,128]{2,1,0:T(8,128)(2,1)S(1)}, bf16[8,208,128]{2,1,0:T(8,128)(2,1)S(1)}, u32[]{:S(2)}, u32[]{:S(2)}) collective-permute-start(bf16[8,208,128]{2,1,0:T(8,128)(2,1)S(1)} %get-tuple-element.42), channel_id=1, source_target_pairs={{1,2},{2,1},{5,6},{6,5},{9,10},{10,9},{13,14},{14,13},{17,18},{18,... | collective-permute-start | bytes 1277960 | tf_op jit(solution)/shard_map/ppermute | solution.py:39
  34.9 0.0 copy-done.3
  34.9 2.8 %shard_map.80.pe_ref = f32[8,6,16,128]{3,2,1,0:T(8,128)S(1)} custom-call(bf16[8,2,128,128]{3,2,1,0:T(8,128)(2,1)S(1)} %get-tuple-element.40.row_ref, bf16[8,2,128,128]{3,2,1,0:T(8,128)(2,1)S(1)} %get-tuple-element.46.g0_ref, bf16[8,2,128,128]{3,2,1,0:T(8,128)(2,1)S(1)} %get-tuple-element.47.g1_ref, bf16[1152,128]{1,0:T(8,128)(2,1)S(1)} %bitcast.9, ...), custom_call_target="tpu_custom_call" | custom-call | flops 679477248 | bytes 4194304 | tf_op jit(solution)/shard_map/pallas_call | solution.py:541
  37.7 0.0 collective-permute-done.2.la_ref
  37.7 3.6 %collective-permute-done.3.lb_ref = bf16[8,208,128]{2,1,0:T(8,128)(2,1)S(1)} collective-permute-done((bf16[8,208,128]{2,1,0:T(8,128)(2,1)S(1)}, bf16[8,208,128]{2,1,0:T(8,128)(2,1)S(1)}, u32[]{:S(2)}, u32[]{:S(2)}) %collective-permute-start.3) | collective-permute-done | bytes 426016 | tf_op jit(solution)/shard_map/ppermute | solution.py:39
  41.3 8.3 %shard_map.81 = (f32[8,4,8,128]{3,2,1,0:T(8,128)S(1)}, f32[8,4,16,128]{3,2,1,0:T(8,128)S(1)}, f32[8,4,16,128]{3,2,1,0:T(8,128)S(1)}, f32[8,6,16,128]{3,2,1,0:T(8...) custom-call(s32[3]{0:T(128)S(1)} %pad_add_fusion.flag_ref, ...), custom_call_target="tpu_custom_call" | custom-call | flops 805306368 | bytes 4194304 | tf_op jit(solution)/shard_map/pallas_call | solution.py:541
  49.6 0.6 collective-permute-start.4
  50.2 3.3 %collective-permute-start.5 = (bf16[8,96,128]{2,1,0:T(8,128)(2,1)S(1)}, bf16[8,96,128]{2,1,0:T(8,128)(2,1)S(1)}, u32[]{:S(2)}, u32[]{:S(2)}) collective-permute-start(bf16[8,96,128]{2,1,0:T(8,128)(2,1)S(1)} %get-tuple-element.53), channel_id=1, source_target_pairs={{4,8},{8,4},{12,16},{16,12},{20,24},{24,20},{28,0},{0,28},{5,9},{9... | collective-permute-start | bytes 589832 | tf_op jit(solution)/shard_map/ppermute | solution.py:39
  53.5 0.9 %collective-permute-done.4.a_ref = bf16[8,96,128]{2,1,0:T(8,128)(2,1)S(1)} collective-permute-done((bf16[8,96,128]{2,1,0:T(8,128)(2,1)S(1)}, bf16[8,96,128]{2,1,0:T(8,128)(2,1)S(1)}, u32[]{:S(2)}, u32[]{:S(2)}) %collective-permute-start.4) | collective-permute-done | bytes 196640 | tf_op jit(solution)/shard_map/ppermute | solution.py:39
  54.4 3.0 %collective-permute-done.5.b_ref = bf16[8,96,128]{2,1,0:T(8,128)(2,1)S(1)} collective-permute-done((bf16[8,96,128]{2,1,0:T(8,128)(2,1)S(1)}, bf16[8,96,128]{2,1,0:T(8,128)(2,1)S(1)}, u32[]{:S(2)}, u32[]{:S(2)}) %collective-permute-start.5) | collective-permute-done | bytes 196640 | tf_op jit(solution)/shard_map/ppermute | solution.py:39
  57.4 9.4 %shard_map.82 = (f32[12,8,16,128]{3,2,1,0:T(8,128)}, f32[6,8,16,128]{3,2,1,0:T(8,128)}) custom-call(s32[3]{0:T(128)S(1)} %pad_add_fusion.flag_ref, f32[8,16,16,128]{3,2,1,0:T(8,128)S(1)} %get-tuple-element.34.ps0_ref.ps1_ref.ps_ref, f32[8,6,16,128]{3,2,1,0:T(8,128)S(1)} %get-tuple-element.49.pe_ref, f32[8,4,16,128]{3,2,1,0:T(8,128)S(1)} %get-tuple-element.50.pm_ref, ...), custom_call_target="tpu_custom_call" | custom-call | flops 134217728 | bytes 2097152 | tf_op jit(solution)/shard_map/pallas_call | solution.py:541
Async XLA Ops:
  0.7 2.2 %copy-start = (bf16[8,128,16,128]{3,2,1,0:T(8,128)(2,1)S(1)}, bf16[8,128,16,128]{3,2,1,0:T(8,128)(2,1)}, u32[]{:S(2)}) copy-start(bf16[8,128,16,128]{3,2,1,0:T(8,128)(2,1)} %x_ref.1) | copy-start | bytes 12582916
  2.9 1.0 %copy-start.2 = (bf16[3,3,128,128]{3,2,1,0:T(8,128)(2,1)S(1)}, bf16[3,3,128,128]{3,2,1,0:T(8,128)(2,1)}, u32[]{:S(2)}) copy-start(bf16[3,3,128,128]{3,2,1,0:T(8,128)(2,1)} %param.7) | copy-start | bytes 884740
  3.9 1.0 %copy-start.4 = (f32[6,8,16,128]{3,2,1,0:T(8,128)S(1)}, f32[6,8,16,128]{3,2,1,0:T(8,128)}, u32[]{:S(2)}) copy-start(f32[6,8,16,128]{3,2,1,0:T(8,128)} %st_ref.1) | copy-start | bytes 1179652
  4.9 0.8 %copy-start.6 = (bf16[3,3,128,12]{2,3,1,0:T(8,128)(2,1)S(1)}, bf16[3,3,128,12]{2,3,1,0:T(8,128)(2,1)}, u32[]{:S(2)}) copy-start(bf16[3,3,128,12]{2,3,1,0:T(8,128)(2,1)} %param.9) | copy-start | bytes 82948
  5.6 0.7 copy-start.7
  6.3 0.7 copy-start.8
  7.0 7.1 %copy-start.1 = (bf16[8,128,16,128]{3,2,1,0:T(8,128)(2,1)S(1)}, bf16[8,128,16,128]{3,2,1,0:T(8,128)(2,1)}, u32[]{:S(2)}) copy-start(bf16[8,128,16,128]{3,2,1,0:T(8,128)(2,1)} %x_ref.1) | copy-start | bytes 12582916
  7.0 7.1 %copy-start.5 = (f32[6,8,16,128]{3,2,1,0:T(8,128)S(1)}, f32[6,8,16,128]{3,2,1,0:T(8,128)}, u32[]{:S(2)}) copy-start(f32[6,8,16,128]{3,2,1,0:T(8,128)} %st_ref.1) | copy-start | bytes 1179652
  8.7 20.3 %collective-permute-start = (bf16[8,192,128]{2,1,0:T(8,128)(2,1)S(1)}, bf16[8,192,128]{2,1,0:T(8,128)(2,1)S(1)}, u32[]{:S(2)}, u32[]{:S(2)}) collective-permute-start(bf16[8,192,128]{2,1,0:T(8,128)(2,1)S(1)} %get-tuple-element.37), channel_id=1, source_target_pairs={{0,4},{4,0},{8,12},{12,8},{16,20},{20,16},{24,28},{28,24},{1,5},{5... | collective-permute-start | bytes 1179656 | tf_op jit(solution)/shard_map/ppermute | solution.py:39
  10.8 18.2 %collective-permute-start.1 = (bf16[8,192,128]{2,1,0:T(8,128)(2,1)S(1)}, bf16[8,192,128]{2,1,0:T(8,128)(2,1)S(1)}, u32[]{:S(2)}, u32[]{:S(2)}) collective-permute-start(bf16[8,192,128]{2,1,0:T(8,128)(2,1)S(1)} %get-tuple-element.38), channel_id=1, source_target_pairs={{4,8},{8,4},{12,16},{16,12},{20,24},{24,20},{28,0},{0,28},{5,9},{9... | collective-permute-start | bytes 1179656 | tf_op jit(solution)/shard_map/ppermute | solution.py:39
  14.1 20.8 %copy-start.3 = (bf16[3,3,128,128]{3,2,1,0:T(8,128)(2,1)S(1)}, bf16[3,3,128,128]{3,2,1,0:T(8,128)(2,1)}, u32[]{:S(2)}) copy-start(bf16[3,3,128,128]{3,2,1,0:T(8,128)(2,1)} %param.7) | copy-start | bytes 884740
  30.6 7.1 %collective-permute-start.2 = (bf16[8,208,128]{2,1,0:T(8,128)(2,1)S(1)}, bf16[8,208,128]{2,1,0:T(8,128)(2,1)S(1)}, u32[]{:S(2)}, u32[]{:S(2)}) collective-permute-start(bf16[8,208,128]{2,1,0:T(8,128)(2,1)S(1)} %get-tuple-element.41), channel_id=1, source_target_pairs={{0,1},{1,0},{2,3},{3,2},{4,5},{5,4},{6,7},{7,6},{8,9},{9,8},{10,11... | collective-permute-start | bytes 1277960 | tf_op jit(solution)/shard_map/ppermute | solution.py:39
  31.9 9.4 %collective-permute-start.3 = (bf16[8,208,128]{2,1,0:T(8,128)(2,1)S(1)}, bf16[8,208,128]{2,1,0:T(8,128)(2,1)S(1)}, u32[]{:S(2)}, u32[]{:S(2)}) collective-permute-start(bf16[8,208,128]{2,1,0:T(8,128)(2,1)S(1)} %get-tuple-element.42), channel_id=1, source_target_pairs={{1,2},{2,1},{5,6},{6,5},{9,10},{10,9},{13,14},{14,13},{17,18},{18,... | collective-permute-start | bytes 1277960 | tf_op jit(solution)/shard_map/ppermute | solution.py:39
  49.6 4.8 %collective-permute-start.4 = (bf16[8,96,128]{2,1,0:T(8,128)(2,1)S(1)}, bf16[8,96,128]{2,1,0:T(8,128)(2,1)S(1)}, u32[]{:S(2)}, u32[]{:S(2)}) collective-permute-start(bf16[8,96,128]{2,1,0:T(8,128)(2,1)S(1)} %get-tuple-element.52), channel_id=1, source_target_pairs={{0,4},{4,0},{8,12},{12,8},{16,20},{20,16},{24,28},{28,24},{1,5},{5... | collective-permute-start | bytes 589832 | tf_op jit(solution)/shard_map/ppermute | solution.py:39
  50.2 7.2 %collective-permute-start.5 = (bf16[8,96,128]{2,1,0:T(8,128)(2,1)S(1)}, bf16[8,96,128]{2,1,0:T(8,128)(2,1)S(1)}, u32[]{:S(2)}, u32[]{:S(2)}) collective-permute-start(bf16[8,96,128]{2,1,0:T(8,128)(2,1)S(1)} %get-tuple-element.53), channel_id=1, source_target_pairs={{4,8},{8,4},{12,16},{16,12},{20,24},{24,20},{28,0},{0,28},{5,9},{9... | collective-permute-start | bytes 589832 | tf_op jit(solution)/shard_map/ppermute | solution.py:39

commit v4 on v3

--- a/solution.py
+++ b/solution.py
@@ -18,9 +18,10 @@
 REACH = 4
 VG = 8
 VMEM_LIMIT = 24 * 2**20
+ROWS_LIMIT = 50 * 2**20
 EDGE_LEVELS = 4
-SIDE_LEVELS = 2
-PARTS = 1
+SIDE_LEVELS = 4
+PARTS = 2
 f32 = jnp.float32
 bf16 = jnp.bfloat16
 
@@ -109,30 +110,43 @@
         s_ref[to, :, lane0 : lane0 + ch] = e_ref[pl.ds(start - 1 + b, count), :].astype(bf16)
 
 
-def prep_kernel(flag_ref, n_lat, b2_ref, x_ref, st_ref, w1_ref, w2_ref, b1_ref,
-                outa_ref, outb_ref, w1p_ref, w2p_ref, w2o_ref, w2e_ref, b1p_ref, b2o_ref, lat_ref, lats_ref, keep_ref,
-                x32_ref, w2s_ref):
-    levels, ch, rows, cols = x_ref.shape
-    nvar = st_ref.shape[0]
+def rows_kernel(flag_ref, x_hbm, st_hbm, outa_ref, outb_ref, x32_ref, x_ref, st_ref, sem):
+    levels, ch, rows, cols = x_hbm.shape
+    nvar = st_hbm.shape[0]
+    size = nvar * REACH
     even = flag_ref[0] == 0
 
+    def level_copy(lv):
+        return pltpu.make_async_copy(x_hbm.at[lv], x_ref.at[lv], sem.at[lv])
+
+    state_copy = pltpu.make_async_copy(st_hbm, st_ref, sem.at[levels])
+    level_copy(0).start()
+    state_copy.start()
+    for lv in range(1, levels):
+        level_copy(lv).start()
+    state_copy.wait()
+
     def one(lv, carry):
+        level_copy(lv).wait()
         x32_ref[...] = x_ref[lv].astype(f32).reshape(ch * rows, cols)
         lo, hi = (x32_ref[pl.ds(row, ch, stride=rows), :].astype(bf16) for row in (0, rows - 1))
         outa_ref[lv, 0:ch] = jnp.where(even, hi, lo)
         outb_ref[lv, 0:ch] = jnp.where(even, lo, hi)
-        x32_ref[0 : 2 * REACH * VG] = jnp.zeros((2 * REACH * VG, WIDE), f32)
         for n in range(nvar):
-            x32_ref[pl.ds(n, REACH, stride=VG), :] = st_ref[n, lv, 0:REACH]
-            x32_ref[pl.ds(REACH * VG + n, REACH, stride=VG), :] = st_ref[n, lv, rows - REACH :]
-        lo = x32_ref[0 : REACH * VG]
-        hi = x32_ref[REACH * VG : 2 * REACH * VG]
+            x32_ref[n * REACH : (n + 1) * REACH] = st_ref[n, lv, 0:REACH]
+            x32_ref[size + n * REACH : size + (n + 1) * REACH] = st_ref[n, lv, rows - REACH :]
+        lo, hi = x32_ref[0:size], x32_ref[size : 2 * size]
         outa_ref[lv, ch:] = jnp.concatenate(two_terms(jnp.where(even, hi, lo)), axis=0)
         outb_ref[lv, ch:] = jnp.concatenate(two_terms(jnp.where(even, lo, hi)), axis=0)
         return carry
 
     lax.fori_loop(0, levels, one, 0)
-    size = w1_ref.shape[0]
+
+
+def prep_kernel(flag_ref, n_lat, cols, b2_ref, w1_ref, w2_ref, b1_ref,
+                w1p_ref, w2p_ref, w2o_ref, w2e_ref, b1p_ref, b2o_ref, lat_ref, lats_ref, keep_ref, w2s_ref):
+    size, ch = w1_ref.shape
+    nvar = w2_ref.shape[1] // 2
     w1p_ref[0:size, 0:ch] = w1_ref[...]
     w1p_ref[size:, 0:ch] = jnp.zeros((3 * ch, ch), bf16)
     w1p_ref[0 : 3 * ch, ch:] = jnp.zeros((3 * ch, ch), bf16)
@@ -169,9 +183,11 @@
 
     lane = lanes((VG, WIDE))
     slot = lane % SLOT
-    for ref, place_in in ((lat_ref, lane), (lats_ref, jnp.where(slot < SIDE, slot - SIDE, cols + slot - SIDE))):
+    beyond = jnp.where(slot < SIDE, slot - SIDE, cols + slot - SIDE)
+    ends = jnp.where(slot < SIDE, cols - SIDE + slot, slot - SIDE)
+    for ref, first, place_in in ((lat_ref, 0, lane), (lats_ref, 0, beyond), (lats_ref, 3, ends)):
         for k, x in enumerate(table(place_in)):
-            ref[k] = x
+            ref[first + k] = x
     spot = lax.broadcasted_iota(jnp.int32, keep_ref.shape, 0)
     counts = ((spot > 0) & (spot <= SIDE)) | ((spot >= 3 * SIDE - 1) & (spot < 4 * SIDE - 1))
     place_in = jnp.where(spot < SLOT, spot - SIDE, cols - SIDE + spot - SLOT) + flag_ref[2] * cols
@@ -184,7 +200,8 @@
     nvar = st_ref.shape[0]
     half = rows // 2
     pitch = cols + SLOT
-    x32_ref[...] = x_ref[0].astype(f32).reshape(chans * rows, cols)
+    step = rows + VG
+    x32_ref.reshape(chans, step, cols)[:, 0:rows] = x_ref[0].astype(f32)
 
     @pl.when(pl.program_id(0) == 0)
     def _():
@@ -193,7 +210,7 @@
 
     sides = [[], []]
     for row in range(rows):
-        block = x32_ref[pl.ds(row, chans, stride=rows), :].T
+        block = x32_ref[pl.ds(row, chans, stride=step), :].T
         start = row * pitch + SIDE
         e_ref[start : start + cols] = block
         for k, part in enumerate((block[0:SIDE], block[cols - SIDE :])):
@@ -230,32 +247,24 @@
     own_ref[0, 0], own_ref[0, 1] = own
 
 
-def pack_kernel(flag_ref, a_ref, b_ref, first_ref, last_ref, own_ref, row_ref, halo_ref, own4_ref, outa_ref, outb_ref):
+def pack_kernel(flag_ref, a_ref, b_ref, first_ref, last_ref, own_ref, row_ref, halo_ref, outa_ref, outb_ref, x_ref):
     cols = a_ref.shape[2]
     ch = row_ref.shape[3]
+    size = (a_ref.shape[1] - ch) // 2
+    nvar = size // REACH
     even = flag_ref[0] == 0
     lat_even = flag_ref[1] == 0
     got_a, got_b = a_ref[0].astype(f32), b_ref[0].astype(f32)
     low, high = jnp.where(even, got_b, got_a), jnp.where(even, got_a, got_b)
-    size = REACH * VG
-    states = [x[ch : ch + size] + x[ch + size : ch + 2 * size] for x in (low, high)]
+    halo_ref[...] = jnp.zeros_like(halo_ref)
+    for k, x in enumerate((low, high)):
+        x_ref[...] = x[ch : ch + size] + x[ch + size :]
+        for r in range(REACH):
+            halo_ref[0, k * REACH + r, 0:nvar] = x_ref[pl.ds(r, nvar, stride=REACH), :]
     low, high = low[0:ch].T, high[0:ch].T
     row_ref[0, 0] = low.astype(bf16)
     row_ref[0, 1] = high.astype(bf16)
-    rows = first_ref.shape[1] // SIDE
-    lane = lanes((VG, WIDE))
-    own = [jnp.zeros((VG, WIDE), f32)] * 2
-    for k in range(2 * REACH):
-        row = k - REACH if k < REACH else rows + k - REACH
-        block = states[k // REACH][(k % REACH) * VG : (k % REACH + 1) * VG]
-        halo_ref[0, k] = block
-        at, base = place(row, rows)
-        own[at - 2] = jnp.where(lane // SLOT == base // SLOT, roll(block, base + SIDE), own[at - 2])
-    own = [own_ref[0, 0], own_ref[0, 1]] + own
-    terms = []
-    for k in range(4):
-        own4_ref[0, k] = own[k]
-        terms += two_terms(own[k])
+    terms = two_terms(own_ref[0, 0]) + two_terms(own_ref[0, 1])
     first = [low[0:SIDE].astype(bf16), first_ref[0], high[0:SIDE].astype(bf16)]
     last = [low[cols - SIDE :].astype(bf16), last_ref[0], high[cols - SIDE :].astype(bf16)]
     first, last = jnp.concatenate(first, axis=0), jnp.concatenate(last, axis=0)
@@ -298,7 +307,7 @@
                 pe_ref[lv, 3 * k + 2 - a] = x
 
 
-def side_kernel(flag_ref, first_ref, last_ref, row_ref, la_ref, lb_ref, own_ref, w1_ref, w2_ref, w2e_ref, b1_ref, keep_ref,
+def side_kernel(flag_ref, first_ref, last_ref, row_ref, la_ref, lb_ref, w1_ref, w2_ref, w2e_ref, b1_ref, keep_ref,
                 pe_ref, ps0_ref, ps1_ref, sst_ref, pm_ref, cm_ref, pec_ref, outa_ref, outb_ref, e_ref, s_ref, hs_ref, z_ref):
     levels = row_ref.shape[0]
     cols, ch = row_ref.shape[2:]
@@ -317,7 +326,7 @@
         a, b = la_ref[lv], lb_ref[lv]
         right, left = jnp.where(lat_even, a, b), jnp.where(lat_even, b, a)
         count = (rows + 2) * SIDE
-        for k in range(4):
+        for k in range(2):
             st = []
             for x in (left, right):
                 x = x[count + 2 * k * VG : count + (2 * k + 2) * VG].astype(f32)
@@ -338,29 +347,38 @@
             for k, part in enumerate((left[side], mine[0], mine[1], right[side])):
                 e_ref[lv, start + k * SIDE : start + (k + 1) * SIDE] = part
         for b in range(3):
-            s_ref[:, b * ch : (b + 1) * ch] = e_ref[lv, pl.ds(SIDE - 1 + b, total), :].astype(bf16)
-        s = s_ref[...].reshape(half + 1, 2, wide, 3 * ch)
-        part = [s[0:half, 0], s[0:half, 1], s[1:, 0], s[1:, 1]]
-        lhs = jnp.concatenate([p.reshape(half * wide, 3 * ch) for p in part], axis=1)
-        acc = jnp.dot(lhs, w1_ref[...], preferred_element_type=f32) + b1_ref[...]
-        hid = silu(acc).reshape(half, wide, 2 * ch) * keep_ref[...]
+            s_ref[lv, :, b * ch : (b + 1) * ch] = e_ref[lv, pl.ds(SIDE - 1 + b, total), :].astype(bf16)
+    s = s_ref[...].reshape(levels, half + 1, 2, wide, 3 * ch)
+    part = [s[:, 0:half, 0], s[:, 0:half, 1], s[:, 1:, 0], s[:, 1:, 1]]
+    lhs = jnp.concatenate([p.reshape(levels * half * wide, 3 * ch) for p in part], axis=1)
+    acc = jnp.dot(lhs, w1_ref[...], preferred_element_type=f32) + b1_ref[...]
+    hid = silu(acc).reshape(levels, half, wide, 2 * ch) * keep_ref[...]
+    for lv in range(levels):
         for m in range(half):
             for side in range(2):
-                here = hid[m, side * SLOT : (side + 1) * SLOT].astype(bf16)
+                here = hid[lv, m, side * SLOT : (side + 1) * SLOT].astype(bf16)
                 hs_ref[lv, side, 0, m * SLOT : (m + 1) * SLOT] = here[:, 0:ch]
                 hs_ref[lv, side, 1, (m + 1) * SLOT : (m + 2) * SLOT] = here[:, ch:]
+                at = (4 * lv + side) * SLOT
                 if m == 0:
-                    z_ref[lv, side * SLOT : (side + 1) * SLOT] = here[:, 0:ch]
+                    z_ref[at : at + SLOT] = here[:, 0:ch]
                 if m == half - 1:
-                    z_ref[lv, (2 + side) * SLOT : (3 + side) * SLOT] = here[:, ch:]
+                    z_ref[at + 2 * SLOT : at + 3 * SLOT] = here[:, ch:]
+    size = half * SLOT
+    rhs = []
+    for lv in range(levels):
+        for side in range(2):
+            odd, ev = hs_ref.at[lv, side, 1], hs_ref.at[lv, side, 0]
+            rhs.append(jnp.concatenate([odd[0:size], ev[0:size], odd[SLOT : size + SLOT], ev[SLOT : size + SLOT]], axis=1))
+    q_side = nt(w2_ref[...], jnp.concatenate(rhs, axis=0))
+    q_ends = nt(w2e_ref[...], z_ref[...])
+    for lv in range(levels):
         tiles = []
         for side in range(2):
-            odd, ev = hs_ref.at[lv, side, 1], hs_ref.at[lv, side, 0]
-            size = half * SLOT
-            rhs = [odd[0:size], ev[0:size], odd[SLOT : size + SLOT], ev[SLOT : size + SLOT]]
-            q = nt(w2_ref[...], jnp.concatenate(rhs, axis=1))
+            q = q_side[:, (2 * lv + side) * size : (2 * lv + side + 1) * size]
             tiles.append([join_taps(q[k * 3 * SLOT : (k + 1) * 3 * SLOT]) for k in range(2)])
-        q = nt(w2e_ref[...], z_ref[lv])
+        per = WIDE // (4 * SLOT)
+        q = roll(q_ends[:, (lv // per) * WIDE : (lv // per + 1) * WIDE], -(lv % per) * 4 * SLOT)
         prev = join_taps(q[3 * SLOT : 6 * SLOT])
         nxt = join_taps(q[0 : 3 * SLOT])
         out, inn = {}, {}
@@ -386,16 +404,23 @@
             mains[row] = add_columns(mains[row], inn[k], base)
         for k, row in enumerate((-1, 0, 1, rows - 2, rows - 1, rows)):
             pec_ref[lv, k] = mains[row]
+        lane8 = lanes((VG, WIDE))
+        st = sst_ref[lv, 0], sst_ref[lv, 1]
+        st_lo = two_terms(jnp.where(lane8 < 2 * SLOT, st[0], roll(st[1], 2 * SLOT)))
+        st_hi = two_terms(jnp.where(lane8 >= WIDE - 2 * SLOT, st[0], roll(st[1], -2 * SLOT)))
         side_lo = jnp.where(lane < 2 * SLOT, out[0], jnp.where(lane < 4 * SLOT, roll(out[1], 2 * SLOT), out[3]))
         side_hi = jnp.where(lane >= WIDE - 2 * SLOT, out[0],
                             jnp.where(lane >= WIDE - 4 * SLOT, roll(out[1], -2 * SLOT), out[2]))
         out_lo = jnp.concatenate([mains[-1], mains[0], mains[1], mains[2], side_lo, mains[3]], axis=0)
         out_hi = jnp.concatenate([mains[rows - k] for k in range(4)] + [side_hi, mains[rows - 4]], axis=0)
-        outa_ref[lv] = jnp.where(even, out_hi, out_lo).astype(bf16)
-        outb_ref[lv] = jnp.where(even, out_lo, out_hi).astype(bf16)
-
-
-def advect_kernel(flag_ref, ps_ref, pe_ref, pm_ref, cm_ref, a_ref, b_ref, st8_ref, halo_ref, sst_ref,
+        main_rows = out_lo.shape[0]
+        outa_ref[lv, 0:main_rows] = jnp.where(even, out_hi, out_lo).astype(bf16)
+        outb_ref[lv, 0:main_rows] = jnp.where(even, out_lo, out_hi).astype(bf16)
+        outa_ref[lv, main_rows:] = jnp.concatenate([jnp.where(even, h, l) for h, l in zip(st_hi, st_lo)], axis=0)
+        outb_ref[lv, main_rows:] = jnp.concatenate([jnp.where(even, l, h) for h, l in zip(st_hi, st_lo)], axis=0)
+
+
+def advect_kernel(flag_ref, ps_ref, pe_ref, pm_ref, cm_ref, a_ref, b_ref, st8_ref, halo_ref, sst_ref, own_ref,
                   b2_ref, lat_ref, lats_ref, *rest):
     vel_ref, ten_ref, out_ref = rest[-3:]
     rows = st8_ref.shape[1]
@@ -439,36 +464,60 @@
 
     q0 = {row: st8_ref[0, row] for row in range(rows)}
     for k in range(REACH):
-        q0[k - REACH] = halo_ref[0, k]
-        q0[rows + k] = halo_ref[0, REACH + k]
-    s0 = {k: sst_ref[0, k] for k in range(4)}
-
-    def at(row):
-        return place(row, rows)
-
-    def side_rows(s):
+        q0[k - REACH], q0[rows + k] = halo_ref[0, k], halo_ref[0, REACH + k]
+    hlo, hhi = (x[(REACH + 1) * pair + pair :] for x in (lo, hi))
+    hlo, hhi = hlo[0:VG] + hlo[VG:], hhi[0:VG] + hhi[VG:]
+    last, front = lane >= WIDE - 2 * SLOT, lane < 2 * SLOT
+    nil = jnp.zeros((VG, WIDE), f32)
+    out_q = {
+        0: sst_ref[0, 0],
+        1: sst_ref[0, 1],
+        2: jnp.where(last, hlo, jnp.where(front, hhi, nil)),
+        3: jnp.where(last, roll(hlo, 2 * SLOT), jnp.where(front, roll(hhi, -2 * SLOT), nil)),
+    }
+    own_q = {0: own_ref[0, 0], 1: own_ref[0, 1], 2: nil, 3: nil}
+    for row in list(range(-REACH, 0)) + list(range(rows, rows + REACH)):
+        k, base = place(row, rows)
+        own_q[k] = jnp.where(lane // SLOT == base // SLOT, roll(q0[row], base + SIDE), own_q[k])
+
+    everywhere = range(-REACH, rows + REACH)
+    own = {k: jnp.zeros((pair, WIDE), f32) for k in range(4)}
+    for row in everywhere:
+        k, base = place(row, rows)
+        own[k] = jnp.where(lane16 // SLOT == base // SLOT, roll(main[row], base + SIDE), own[k])
+
+    def tiles(out, inner):
+        return {**{k: mix(out[k], inner[k]) for k in range(4)}, **{4 + k: mix(inner[k], out[k]) for k in range(4)}}
+
+    s0 = tiles(out_q, own_q)
+    vel_s = tiles(side, own)
+
+    def tile_rows(s):
         def turned(own, halo, by, first):
             own, halo = roll(own, by), roll(halo, by)
             return jnp.where(first, halo, own), jnp.where(first, own, halo)
 
-        odd_back = turned(s[1], s[3], SLOT, lane < SLOT)
-        even_on = turned(s[0], s[2], -SLOT, lane >= WIDE - SLOT)
-        before = {0: odd_back[0], 2: odd_back[1], 1: s[0], 3: s[2]}
-        after = {0: s[1], 2: s[3], 1: even_on[0], 3: even_on[1]}
+        before, after = {}, {}
+        for t in (0, 4):
+            before[t + 1], before[t + 3], after[t], after[t + 2] = s[t], s[t + 2], s[t + 1], s[t + 3]
+            before[t], before[t + 2] = turned(s[t + 1], s[t + 3], SLOT, lane < SLOT)
+            after[t + 1], after[t + 3] = turned(s[t], s[t + 2], -SLOT, lane >= WIDE - SLOT)
         return before, after
 
     u = {r: x[0:VG] for r, x in main.items()}
-    us = {k: x[0:VG] for k, x in side.items()}
+    us = {k: x[0:VG] for k, x in vel_s.items()}
     inside = range(1 - REACH, rows + REACH - 1)
     v = {r: main[r][VG:] for r in inside}
-    vs = {k: x[VG:] for k, x in side.items()}
+    vs = {k: x[VG:] for k, x in vel_s.items()}
     cosine, metric = lat_ref[0], lat_ref[1]
-    cosine_s, metric_s = lats_ref[0], lats_ref[1]
+
+    def side_table(n, k):
+        return mix(lats_ref[n], lats_ref[n + 3]) if k < 4 else mix(lats_ref[n + 3], lats_ref[n])
+
+    cosine_s, metric_s = ([side_table(n, k) for k in range(8)] for n in range(2))
     flux = {r: x * cosine for r, x in v.items()}
-    flux_s = {k: x * cosine_s for k, x in vs.items()}
-    fb, fbs = col_before(flux, flux_s, at)
-    fa, fas = col_after(flux, flux_s, at)
-    ub, ua = side_rows(us)
+    flux_s = {k: x * cosine_s[k] for k, x in vs.items()}
+    ub, ua = tile_rows(us)
 
     def coefs(m, uu, vv, udiff, vdiff):
         div = m * (udiff * 0.5 + vdiff * 0.5)
@@ -478,21 +527,18 @@
         cu = -jnp.minimum(vv, 0.0)
         return -(cl + cr + cd + cu + div), cl, cr, cd, cu
 
-    cm = {r: coefs(metric, u[r], v[r], u[r + 1] - u[r - 1], fa[r] - fb[r]) for r in inside}
-    cs = {k: coefs(metric_s, us[k], vs[k], ua[k] - ub[k], fas[k] - fbs[k]) for k in range(4)}
-
-    def stencil(c, x, left, right, down, up):
-        return c[0] * x + c[1] * left + c[2] * right + c[3] * down + c[4] * up
+    cm = {r: coefs(metric, u[r], v[r], u[r + 1] - u[r - 1], roll(flux[r], -1) - roll(flux[r], 1)) for r in inside}
+    cs = {k: coefs(metric_s[k], us[k], vs[k], ua[k] - ub[k], roll(flux_s[k], -1) - roll(flux_s[k], 1)) for k in range(8)}
+
+    def stencil(c, x, left, right):
+        return c[0] * x + c[1] * left + c[2] * right + c[3] * roll(x, 1) + c[4] * roll(x, -1)
 
     def rate(q, s, depth):
-        centre = {r: q[r] for r in range(depth - REACH, rows + REACH - depth)}
-        qb, sb = col_before(centre, s, at)
-        qa, sa = col_after(centre, s, at)
-        rb, ra = side_rows(s)
-        out = {r: stencil(cm[r], q[r], q[r - 1], q[r + 1], qb[r], qa[r]) for r in centre}
-        if depth == REACH:
-            return out, None
-        return out, {k: stencil(cs[k], s[k], rb[k], ra[k], sb[k], sa[k]) for k in range(4)}
+        rb, ra = tile_rows(s)
+        inner = range(depth - REACH, rows + REACH - depth)
+        wanted = [k for k in range(8) if depth < REACH or k % 4 < 2]
+        return ({r: stencil(cm[r], q[r], q[r - 1], q[r + 1]) for r in inner},
+                {k: stencil(cs[k], s[k], rb[k], ra[k]) for k in wanted})
 
     def moved(rates, by):
         return {r: q0[r] + by * x for r, x in rates[0].items()}, {k: s0[k] + by * x for k, x in rates[1].items()}
@@ -501,9 +547,15 @@
     two = rate(*moved(one, 0.5 * time_step), 2)
     three = rate(*moved(two, 0.5 * time_step), 3)
     four = rate(*moved(three, time_step), 4)
+
+    def mean(n, k):
+        return (one[n][k] + 2.0 * two[n][k] + 2.0 * three[n][k] + four[n][k]) / 6.0
+
+    ends = {k: mix(mean(1, 4 + k), mean(1, k)) for k in range(2)}
     for row in range(rows):
-        ten = (one[0][row] + 2.0 * two[0][row] + 2.0 * three[0][row] + four[0][row]) / 6.0
-        out_ref[0, row * VG : (row + 1) * VG] = ten
+        k, base = place(row, rows)
+        at_end = (lane < REACH) | (lane >= WIDE - REACH)
+        out_ref[0, row * VG : (row + 1) * VG] = jnp.where(at_end, roll(ends[k], -(base + SIDE)), mean(0, row))
     for n in range(nvar):
         ten_ref[n, 0] = out_ref[0, pl.ds(n, rows, stride=VG), :]
 
@@ -551,22 +603,35 @@
         )(*args)
 
     flags = jnp.stack([lax.axis_index("lon") % 2, lax.axis_index("lat") % 2, lax.axis_index("lat")]).astype(jnp.int32)
-    lon_wire = (lev, ch + 2 * REACH * VG, WIDE)
-    shapes = [(lon_wire, bf16), (lon_wire, bf16), ((12 * ch, 2 * ch), bf16), ((6 * SLOT, 4 * ch), bf16), ((9 * SLOT, ch), bf16),
-              ((6 * SLOT, ch), bf16), ((1, 2 * ch), f32), ((2 * VG, WIDE), f32), ((3, VG, WIDE), f32), ((3, VG, WIDE), f32),
+    lon_wire = (lev, ch + 2 * nvar * REACH, cols)
+    vmem = pl.BlockSpec(memory_space=pltpu.VMEM)
+    lon_a, lon_b = pl.pallas_call(
+        rows_kernel,
+        in_specs=[smem] + [pl.BlockSpec(memory_space=pltpu.HBM)] * 2,
+        out_specs=[vmem] * 2,
+        out_shape=[sds(lon_wire, bf16)] * 2,
+        scratch_shapes=[
+            pltpu.VMEM((ch * rows, cols), f32),
+            pltpu.VMEM(hidden_in.shape, bf16),
+            pltpu.VMEM(state.shape, f32),
+            pltpu.SemaphoreType.DMA((lev + 1,)),
+        ],
+        compiler_params=pltpu.CompilerParams(vmem_limit_bytes=ROWS_LIMIT),
+    )(flags, hidden_in, state)
+    shapes = [((12 * ch, 2 * ch), bf16), ((6 * SLOT, 4 * ch), bf16), ((9 * SLOT, ch), bf16),
+              ((6 * SLOT, ch), bf16), ((1, 2 * ch), f32), ((2 * VG, WIDE), f32), ((3, VG, WIDE), f32), ((6, VG, WIDE), f32),
               ((2 * SLOT, 2 * ch), f32)]
-    vmem = pl.BlockSpec(memory_space=pltpu.VMEM)
     w1_one = w_conv1.reshape(9 * ch, ch)
     b1 = b_conv1.reshape(1, ch)
     n_lat = cols * lax.axis_size("lat")
-    lon_a, lon_b, w1_pair, w2_pair, w2_one, w2_ends, b1_pair, b2, lat_main, lat_side, keep = pl.pallas_call(
-        lambda flag_ref, *refs: prep_kernel(flag_ref, n_lat, *refs),
-        in_specs=[smem, smem] + [vmem] * 5,
+    w1_pair, w2_pair, w2_one, w2_ends, b1_pair, b2, lat_main, lat_side, keep = pl.pallas_call(
+        lambda flag_ref, *refs: prep_kernel(flag_ref, n_lat, cols, *refs),
+        in_specs=[smem, smem] + [vmem] * 3,
         out_specs=[vmem] * len(shapes),
         out_shape=[sds(*x) for x in shapes],
-        scratch_shapes=[pltpu.VMEM((ch * rows, cols), f32), pltpu.VMEM((4 * VG, ch), f32)],
+        scratch_shapes=[pltpu.VMEM((4 * VG, ch), f32)],
         compiler_params=params,
-    )(flags, b_conv2, hidden_in, state, w1_one, w_conv2.transpose(0, 1, 3, 2).reshape(9, 2 * nvar, ch), b1)
+    )(flags, b_conv2, w1_one, w_conv2.transpose(0, 1, 3, 2).reshape(9, 2 * nvar, ch), b1)
     lon_a = swap(lon_a, "lon", 0, True)
     lon_b = swap(lon_b, "lon", 1, True)
 
@@ -576,6 +641,7 @@
     cut = (lev, rows * SIDE, ch)
     ps_shape = (lev, rows, 2 * VG, WIDE)
     own_shape = (lev, 2, VG, WIDE)
+    halo_shape = (lev, 2 * REACH, VG, WIDE)
     shapes = [(g_pair, bf16), (g_pair, bf16), (cut, bf16), (cut, bf16), (st8_shape, f32), (own_shape, f32), (ps_shape, f32)]
     g_lo, g_hi, first, last, st8, own, ps = call(
         main_kernel,
@@ -584,7 +650,7 @@
         [sds(*x) for x in shapes],
         [per_level(x[0]) for x in shapes],
         [
-            pltpu.VMEM((ch * rows, cols), f32),
+            pltpu.VMEM((ch * (rows + VG), cols), f32),
             pltpu.VMEM((rows * (cols + SLOT), ch), f32),
             pltpu.VMEM((rows, cols, 3 * ch), bf16),
             pltpu.VMEM((rows + 2, cols, ch), bf16),
@@ -593,18 +659,16 @@
         pl.CostEstimate(flops=2 * lev * rows * ext * 9 * ch * ch, bytes_accessed=8 * 2**20, transcendentals=0),
     )
 
-    lat_wire = (lev, (rows + 2) * SIDE + 8 * VG, WIDE)
+    lat_wire = (lev, (rows + 2) * SIDE + 4 * VG, WIDE)
     pair_shape = (lev, 2, cols, ch)
-    halo_shape = (lev, 2 * REACH, VG, WIDE)
-    own4_shape = (lev, 4, VG, WIDE)
-    shapes = [(pair_shape, bf16), (halo_shape, f32), (own4_shape, f32), (lat_wire, bf16), (lat_wire, bf16)]
-    row_pair, halo, own4, lat_a, lat_b = call(
+    shapes = [(pair_shape, bf16), (halo_shape, f32), (lat_wire, bf16), (lat_wire, bf16)]
+    row_pair, halo, lat_a, lat_b = call(
         pack_kernel,
         lev,
         [smem, per_level(lon_wire), per_level(lon_wire), per_level(cut), per_level(cut), per_level(own_shape)],
         [sds(*x) for x in shapes],
         [per_level(x[0]) for x in shapes],
-        [],
+        [pltpu.VMEM((nvar * REACH, WIDE), f32)],
         (flags, lon_a, lon_b, first, last, own),
     )
     lat_a = swap(lat_a, "lat", 0, False)
@@ -633,10 +697,10 @@
     block = SIDE_LEVELS
     parts = PARTS
     count = lev // parts
-    wire = (count, 2 * VG * (REACH + 2), WIDE)
+    wire = (count, 2 * VG * (REACH + 3), WIDE)
     pec_shape = (count,) + pe_shape[1:]
     pm4_shape = (count, 4, 2 * VG, WIDE)
-    sst_shape = (count, 4, VG, WIDE)
+    sst_shape = (count, 2, VG, WIDE)
     shapes = [(sst_shape, f32), (pm4_shape, f32), (pm4_shape, f32), (pec_shape, f32), (wire, bf16), (wire, bf16)]
     sent = []
     for part in range(parts):
@@ -645,18 +709,18 @@
         sst, pm, cm, pec, out_a, out_b = call(
             side_kernel,
             count // block,
-            [smem, here(cut), here(cut), here(pair_shape), here(lat_wire), here(lat_wire), here(own4_shape),
+            [smem, here(cut), here(cut), here(pair_shape), here(lat_wire), here(lat_wire),
              full(w1_pair.shape), full(w2_pair.shape), full(w2_ends.shape), full((1, 2 * ch)), full((2 * SLOT, 2 * ch)),
              here(pe_shape), level_part(four, 0, block, off), level_part(four, rows // 4 - 1, block, off)],
             [sds(*x) for x in shapes],
             [levels_of(x[0], block) for x in shapes],
             [
                 pltpu.VMEM((block, (rows + 2) * 2 * SLOT + 2 * SIDE, ch), f32),
-                pltpu.VMEM(((rows + 2) * 2 * SLOT, 3 * ch), bf16),
+                pltpu.VMEM((block, (rows + 2) * 2 * SLOT, 3 * ch), bf16),
                 pltpu.VMEM((block, 2, 2, (half + 1) * SLOT, ch), bf16),
-                pltpu.VMEM((block, WIDE, ch), bf16),
+                pltpu.VMEM((max(WIDE, block * 4 * SLOT), ch), bf16),
             ],
-            (flags, first, last, row_pair, lat_a, lat_b, own4, w1_pair, w2_pair, w2_ends, b1_pair, keep, pe, ps, ps),
+            (flags, first, last, row_pair, lat_a, lat_b, w1_pair, w2_pair, w2_ends, b1_pair, keep, pe, ps, ps),
             pl.CostEstimate(flops=count * 512 * 12 * ch * ch, bytes_accessed=4 * 2**20, transcendentals=0),
         )
         sent.append((pec, pm, cm, sst, swap(out_a, "lon", 0, True), swap(out_b, "lon", 1, True)))
@@ -671,14 +735,14 @@
             advect_kernel,
             count,
             [smem, here(ps_shape), per_level(pec_shape), per_level(pm4_shape), per_level(pm4_shape), per_level(wire),
-             per_level(wire), here(st8.shape), here(halo_shape), per_level(sst_shape),
+             per_level(wire), here(st8.shape), here(halo_shape), per_level(sst_shape), here(own_shape),
              full(b2.shape), full(lat_main.shape), full(lat_side.shape)] + [hbm] * len(done),
             outs,
             [var(o.shape) for o in outs],
             [pltpu.VMEM((2, rows * VG, WIDE), f32)],
-            (flags, ps, pec, pm, cm, out_a, out_b, st8, halo, sst, b2, lat_main, lat_side) + tuple(done),
+            (flags, ps, pec, pm, cm, out_a, out_b, st8, halo, sst, own, b2, lat_main, lat_side) + tuple(done),
             pl.CostEstimate(flops=count * 2**24, bytes_accessed=2 * 2**20, transcendentals=0),
-            {13: 0, 14: 1} if done else {},
+            {14: 0, 15: 1} if done else {},
         )
     return tuple(done)
 

time: 67.2 us -> 56.4 us (0.84)
  local copies, waits for them, and re-layouts: 6.23 us -> 1.17 us
  waiting for transfers between devices: 7.58 us -> 3.02 us
  Pallas kernels: 38.7 us -> 36.9 us
    unnamed x18 -> x12, local copies, waits for them, and re-layouts: 6.23 us -> 1.17 us
    ppermute x6 -> x8, waiting for transfers between devices: 7.58 us -> 3.02 us  [swap(): lax.ppermute(block, axis, swap_pairs(lax.axis_size(axis), first, closed))]
    pallas_call x5 -> x7, Pallas kernels: 37 us -> 33.2 us  [call(): pl.pallas_call(kernel, grid=(steps,), in_specs=ins, out_specs=out_specs,...]
    pallas_call x1 -> x2, Pallas kernels: 1.72 us -> 3.71 us  [the longest x1 2.95 us: body(): pl.pallas_call(rows_kernel, in_specs=[smem] + [pl.BlockSpec(memory_space=...]
    ppermute x6 -> x8, starting transfers between devices: 13.6 us -> 14.2 us  [swap(): lax.ppermute(block, axis, swap_pairs(lax.axis_size(axis), first, closed))]
  transfers between devices with their start and end apart: 6 -> 8, of which waited for: 3 -> 2; matrix products, arithmetic and copies ran while one was open for 0% -> 0% of each run, Pallas kernels for 26% -> 44%
where the time goes in v4:
time: 56.4 us; the launch traced here: 56.1 us
  Pallas kernels  36.9 us (65%)
  starting transfers between devices  14.2 us (25%)
  waiting for transfers between devices  3.02 us (5%)
  local copies, waits for them, and re-layouts  1.17 us (2%)
  between operations  0.78 us (1%)
    pallas_call x7, Pallas kernels, call(): pl.pallas_call(kernel, grid=(steps,), in_specs=ins, out_specs=out_specs,...  33.2 us
    ppermute x8, starting transfers between devices, swap(): lax.ppermute(block, axis, swap_pairs(lax.axis_size(axis), first, closed))  14.2 us
    ppermute x8, waiting for transfers between devices, swap(): lax.ppermute(block, axis, swap_pairs(lax.axis_size(axis), first, closed))  3.02 us
    pallas_call x1, Pallas kernels, body(): pl.pallas_call(rows_kernel, in_specs=[smem] + [pl.BlockSpec(memory_space=...  2.95 us
    unnamed x12, local copies, waits for them, and re-layouts  1.17 us
  transfers between devices with their start and end apart: 8, of which 2 were waited for; matrix products, arithmetic and copies ran while one was open for 0% of the time, Pallas kernels for 44%

profile of v4, /device:TPU:1, one launch (start us, length us, event | category | flops | bytes accessed | tf_op | source)
XLA Modules:
  0.0 56.1 jit_solution(6700609256855072158)
XLA Ops:
  0.6 0.0 copy-start.1
  0.7 0.0 copy-start
  0.7 0.1 pad_add_fusion.flag_ref
  0.7 0.0 copy-start.2
  0.7 1.1 %copy-done.2 = f32[6,8,16,128]{3,2,1,0:T(8,128)S(1)} copy-done((f32[6,8,16,128]{3,2,1,0:T(8,128)S(1)}, f32[6,8,16,128]{3,2,1,0:T(8,128)}, u32[]{:S(2)}) %copy-start.2) | copy-done | bytes 393240
  1.9 0.0 copy-start.3
  1.9 0.0 copy-start.4
  1.9 0.0 copy-start.5
  1.9 3.0 %shard_map.79 = (bf16[8,176,128]{2,1,0:T(8,128)(2,1)S(1)}, bf16[8,176,128]{2,1,0:T(8,128)(2,1)S(1)}) custom-call(s32[3]{0:T(128)S(1)} %pad_add_fusion.flag_ref, bf16[8,128,16,128]{3,2,1,0:T(8,128)(2,1)} %x_hbm.1, f32[6,8,16,128]{3,2,1,0:T(8,128)S(1)} %copy-done.2), custom_call_target="tpu_custom_call" | custom-call | tf_op jit(solution)/shard_map/pallas_call | solution.py:608
  4.9 2.1 %collective-permute-start = (bf16[8,176,128]{2,1,0:T(8,128)(2,1)S(1)}, bf16[8,176,128]{2,1,0:T(8,128)(2,1)S(1)}, u32[]{:S(2)}, u32[]{:S(2)}) collective-permute-start(bf16[8,176,128]{2,1,0:T(8,128)(2,1)S(1)} %get-tuple-element.44), channel_id=1, source_target_pairs={{0,4},{4,0},{8,12},{12,8},{16,20},{20,16},{24,28},{28,24},{1,5},{5... | collective-permute-start | bytes 1081352 | tf_op jit(solution)/shard_map/ppermute | solution.py:40
  7.0 3.3 %collective-permute-start.1 = (bf16[8,176,128]{2,1,0:T(8,128)(2,1)S(1)}, bf16[8,176,128]{2,1,0:T(8,128)(2,1)S(1)}, u32[]{:S(2)}, u32[]{:S(2)}) collective-permute-start(bf16[8,176,128]{2,1,0:T(8,128)(2,1)S(1)} %get-tuple-element.45), channel_id=1, source_target_pairs={{4,8},{8,4},{12,16},{16,12},{20,24},{24,20},{28,0},{0,28},{5,9},{9... | collective-permute-start | bytes 1081352 | tf_op jit(solution)/shard_map/ppermute | solution.py:40
  10.3 0.0 copy-done.1
  10.3 0.0 copy-done.3
  10.3 0.0 copy-done.4
  10.3 0.0 copy-done.5
  10.3 0.8 %shard_map.77 = (bf16[1536,256]{1,0:T(8,128)(2,1)S(1)}, bf16[96,512]{1,0:T(8,128)(2,1)S(1)}, bf16[144,128]{1,0:T(8,128)(2,1)S(1)}, bf16[96,128]{1,0:T(8,128)(2,1...) custom-call(s32[3]{0:T(128)S(1)} %pad_add_fusion.flag_ref, ...), custom_call_target="tpu_custom_call" | custom-call | tf_op jit(solution)/shard_map/pallas_call | solution.py:627
  11.0 0.0 copy-done
  11.0 13.9 %shard_map.78 = (bf16[8,2,128,128]{3,2,1,0:T(8,128)(2,1)S(1)}, bf16[8,2,128,128]{3,2,1,0:T(8,128)(2,1)S(1)}, bf16[8,128,128]{2,1,0:T(8,128)(2,1)S(1)}, bf16[8,12...) custom-call(bf16[8,128,16,128]{3,2,1,0:T(8,128)(2,1)S(1)} %copy-done, ...), custom_call_target="tpu_custom_call" | custom-call | flops 5435817984 | bytes 8388608 | tf_op jit(solution)/shard_map/pallas_call | solution.py:593
  25.0 0.0 collective-permute-done.a_ref
  25.0 0.0 collective-permute-done.1.b_ref
  25.0 1.6 %shard_map.80 = (bf16[8,2,128,128]{3,2,1,0:T(8,128)(2,1)S(1)}, f32[8,8,8,128]{3,2,1,0:T(8,128)S(1)}, bf16[8,176,128]{2,1,0:T(8,128)(2,1)S(1)}, bf16[8,176,128]{2,1,0:T(8,128)(2,1)S(1)}) custom-call(s32[3]{0:T(128)S(1)} %pad_add_fusion.flag_ref, bf16[8,176,128]{2,1,0:T(8,128)(2,1)S(1)} %collective-permute-done.a_ref, ...), custom_call_target="tpu_custom_call" | custom-call | tf_op jit(solution)/shard_map/pallas_call | solution.py:593
  26.6 1.3 %collective-permute-start.2 = (bf16[8,176,128]{2,1,0:T(8,128)(2,1)S(1)}, bf16[8,176,128]{2,1,0:T(8,128)(2,1)S(1)}, u32[]{:S(2)}, u32[]{:S(2)}) collective-permute-start(bf16[8,176,128]{2,1,0:T(8,128)(2,1)S(1)} %get-tuple-element.48), channel_id=1, source_target_pairs={{0,1},{1,0},{2,3},{3,2},{4,5},{5,4},{6,7},{7,6},{8,9},{9,8},{10,11... | collective-permute-start | bytes 1081352 | tf_op jit(solution)/shard_map/ppermute | solution.py:40
  27.9 3.0 %collective-permute-start.3 = (bf16[8,176,128]{2,1,0:T(8,128)(2,1)S(1)}, bf16[8,176,128]{2,1,0:T(8,128)(2,1)S(1)}, u32[]{:S(2)}, u32[]{:S(2)}) collective-permute-start(bf16[8,176,128]{2,1,0:T(8,128)(2,1)S(1)} %get-tuple-element.49), channel_id=1, source_target_pairs={{1,2},{2,1},{5,6},{6,5},{9,10},{10,9},{13,14},{14,13},{17,18},{18,... | collective-permute-start | bytes 1081352 | tf_op jit(solution)/shard_map/ppermute | solution.py:40
  30.9 2.8 %shard_map.81.pe_ref = f32[8,6,16,128]{3,2,1,0:T(8,128)S(1)} custom-call(bf16[8,2,128,128]{3,2,1,0:T(8,128)(2,1)S(1)} %get-tuple-element.47.row_ref, bf16[8,2,128,128]{3,2,1,0:T(8,128)(2,1)S(1)} %get-tuple-element.52.g0_ref, bf16[8,2,128,128]{3,2,1,0:T(8,128)(2,1)S(1)} %get-tuple-element.53.g1_ref, bf16[1152,128]{1,0:T(8,128)(2,1)S(1)} %bitcast.9, ...), custom_call_target="tpu_custom_call" | custom-call | flops 679477248 | bytes 4194304 | tf_op jit(solution)/shard_map/pallas_call | solution.py:593
  33.7 0.0 collective-permute-done.2.la_ref
  33.7 2.9 %collective-permute-done.3.lb_ref = bf16[8,176,128]{2,1,0:T(8,128)(2,1)S(1)} collective-permute-done((bf16[8,176,128]{2,1,0:T(8,128)(2,1)S(1)}, bf16[8,176,128]{2,1,0:T(8,128)(2,1)S(1)}, u32[]{:S(2)}, u32[]{:S(2)}) %collective-permute-start.3) | collective-permute-done | bytes 360480 | tf_op jit(solution)/shard_map/ppermute | solution.py:40
  36.6 2.9 %shard_map.83 = (f32[4,2,8,128]{3,2,1,0:T(8,128)S(1)}, f32[4,4,16,128]{3,2,1,0:T(8,128)S(1)}, f32[4,4,16,128]{3,2,1,0:T(8,128)S(1)}, f32[4,6,16,128]{3,2,1,0:T(8...) custom-call(s32[3]{0:T(128)S(1)} %pad_add_fusion.flag_ref, ...), custom_call_target="tpu_custom_call" | custom-call | flops 402653184 | bytes 4194304 | tf_op jit(solution)/shard_map/pallas_call | solution.py:593
  39.5 0.1 collective-permute-start.6
  39.6 2.5 %collective-permute-start.7 = (bf16[4,112,128]{2,1,0:T(8,128)(2,1)S(1)}, bf16[4,112,128]{2,1,0:T(8,128)(2,1)S(1)}, u32[]{:S(2)}, u32[]{:S(2)}) collective-permute-start(bf16[4,112,128]{2,1,0:T(8,128)(2,1)S(1)} %get-tuple-element.70), channel_id=1, source_target_pairs={{4,8},{8,4},{12,16},{16,12},{20,24},{24,20},{28,0},{0,28},{5,9},{9... | collective-permute-start | bytes 344072 | tf_op jit(solution)/shard_map/ppermute | solution.py:40
  42.2 2.9 %shard_map.82 = (f32[4,2,8,128]{3,2,1,0:T(8,128)S(1)}, f32[4,4,16,128]{3,2,1,0:T(8,128)S(1)}, f32[4,4,16,128]{3,2,1,0:T(8,128)S(1)}, f32[4,6,16,128]{3,2,1,0:T(8...) custom-call(s32[3]{0:T(128)S(1)} %pad_add_fusion.flag_ref, ...), custom_call_target="tpu_custom_call" | custom-call | flops 402653184 | bytes 4194304 | tf_op jit(solution)/shard_map/pallas_call | solution.py:593
  45.0 0.1 collective-permute-start.4
  45.1 1.7 %collective-permute-start.5 = (bf16[4,112,128]{2,1,0:T(8,128)(2,1)S(1)}, bf16[4,112,128]{2,1,0:T(8,128)(2,1)S(1)}, u32[]{:S(2)}, u32[]{:S(2)}) collective-permute-start(bf16[4,112,128]{2,1,0:T(8,128)(2,1)S(1)} %get-tuple-element.59), channel_id=1, source_target_pairs={{4,8},{8,4},{12,16},{16,12},{20,24},{24,20},{28,0},{0,28},{5,9},{9... | collective-permute-start | bytes 344072 | tf_op jit(solution)/shard_map/ppermute | solution.py:40
  46.9 0.0 collective-permute-done.6.a_ref
  46.9 0.0 collective-permute-done.7.b_ref
  46.9 4.6 %shard_map.84 = (f32[12,8,16,128]{3,2,1,0:T(8,128)}, f32[6,8,16,128]{3,2,1,0:T(8,128)}) custom-call(s32[3]{0:T(128)S(1)} %pad_add_fusion.flag_ref, f32[8,16,16,128]{3,2,1,0:T(8,128)S(1)} %get-tuple-element.41.ps0_ref.ps1_ref.ps_ref, f32[4,6,16,128]{3,2,1,0:T(8,128)S(1)} %get-tuple-element.66.pe_ref, f32[4,4,16,128]{3,2,1,0:T(8,128)S(1)} %get-tuple-element.67.pm_ref, ...), custom_call_target="tpu_custom_call" | custom-call | flops 67108864 | bytes 2097152 | tf_op jit(solution)/shard_map/pallas_call | solution.py:593
  51.4 0.0 collective-permute-done.4.a_ref
  51.4 0.1 collective-permute-done.5.b_ref
  51.5 4.5 %shard_map.85 = (f32[12,8,16,128]{3,2,1,0:T(8,128)}, f32[6,8,16,128]{3,2,1,0:T(8,128)}) custom-call(s32[3]{0:T(128)S(1)} %pad_add_fusion.flag_ref, f32[8,16,16,128]{3,2,1,0:T(8,128)S(1)} %get-tuple-element.41.ps0_ref.ps1_ref.ps_ref, f32[4,6,16,128]{3,2,1,0:T(8,128)S(1)} %get-tuple-element.55.pe_ref, ...), custom_call_target="tpu_custom_call", output_to_operand_aliasing={{0}: (14, {}), {1}: (15, {})} | custom-call | flops 67108864 | bytes 2097152 | tf_op jit(solution)/shard_map/pallas_call | solution.py:593
Async XLA Ops:
  0.6 9.6 %copy-start.1 = (bf16[3,3,128,128]{3,2,1,0:T(8,128)(2,1)S(1)}, bf16[3,3,128,128]{3,2,1,0:T(8,128)(2,1)}, u32[]{:S(2)}) copy-start(bf16[3,3,128,128]{3,2,1,0:T(8,128)(2,1)} %param.7) | copy-start | bytes 884740
  0.7 10.4 %copy-start = (bf16[8,128,16,128]{3,2,1,0:T(8,128)(2,1)S(1)}, bf16[8,128,16,128]{3,2,1,0:T(8,128)(2,1)}, u32[]{:S(2)}) copy-start(bf16[8,128,16,128]{3,2,1,0:T(8,128)(2,1)} %x_hbm.1) | copy-start | bytes 12582916
  0.7 1.1 %copy-start.2 = (f32[6,8,16,128]{3,2,1,0:T(8,128)S(1)}, f32[6,8,16,128]{3,2,1,0:T(8,128)}, u32[]{:S(2)}) copy-start(f32[6,8,16,128]{3,2,1,0:T(8,128)} %st_hbm.1) | copy-start | bytes 1179652
  1.9 8.4 %copy-start.3 = (bf16[3,3,128,12]{2,3,1,0:T(8,128)(2,1)S(1)}, bf16[3,3,128,12]{2,3,1,0:T(8,128)(2,1)}, u32[]{:S(2)}) copy-start(bf16[3,3,128,12]{2,3,1,0:T(8,128)(2,1)} %param.9) | copy-start | bytes 82948
  1.9 8.4 %copy-start.4 = (f32[128]{0:T(128)S(1)}, f32[128]{0:T(128)}, u32[]{:S(2)}) copy-start(f32[128]{0:T(128)} %param.8) | copy-start | bytes 1540
  1.9 8.4 %copy-start.5 = (f32[12]{0:T(128)S(1)}, f32[12]{0:T(128)}, u32[]{:S(2)}) copy-start(f32[12]{0:T(128)} %refs_0_.1) | copy-start | bytes 148
  4.9 20.1 %collective-permute-start = (bf16[8,176,128]{2,1,0:T(8,128)(2,1)S(1)}, bf16[8,176,128]{2,1,0:T(8,128)(2,1)S(1)}, u32[]{:S(2)}, u32[]{:S(2)}) collective-permute-start(bf16[8,176,128]{2,1,0:T(8,128)(2,1)S(1)} %get-tuple-element.44), channel_id=1, source_target_pairs={{0,4},{4,0},{8,12},{12,8},{16,20},{20,16},{24,28},{28,24},{1,5},{5... | collective-permute-start | bytes 1081352 | tf_op jit(solution)/shard_map/ppermute | solution.py:40
  7.0 18.0 %collective-permute-start.1 = (bf16[8,176,128]{2,1,0:T(8,128)(2,1)S(1)}, bf16[8,176,128]{2,1,0:T(8,128)(2,1)S(1)}, u32[]{:S(2)}, u32[]{:S(2)}) collective-permute-start(bf16[8,176,128]{2,1,0:T(8,128)(2,1)S(1)} %get-tuple-element.45), channel_id=1, source_target_pairs={{4,8},{8,4},{12,16},{16,12},{20,24},{24,20},{28,0},{0,28},{5,9},{9... | collective-permute-start | bytes 1081352 | tf_op jit(solution)/shard_map/ppermute | solution.py:40
  26.6 7.1 %collective-permute-start.2 = (bf16[8,176,128]{2,1,0:T(8,128)(2,1)S(1)}, bf16[8,176,128]{2,1,0:T(8,128)(2,1)S(1)}, u32[]{:S(2)}, u32[]{:S(2)}) collective-permute-start(bf16[8,176,128]{2,1,0:T(8,128)(2,1)S(1)} %get-tuple-element.48), channel_id=1, source_target_pairs={{0,1},{1,0},{2,3},{3,2},{4,5},{5,4},{6,7},{7,6},{8,9},{9,8},{10,11... | collective-permute-start | bytes 1081352 | tf_op jit(solution)/shard_map/ppermute | solution.py:40
  27.9 8.7 %collective-permute-start.3 = (bf16[8,176,128]{2,1,0:T(8,128)(2,1)S(1)}, bf16[8,176,128]{2,1,0:T(8,128)(2,1)S(1)}, u32[]{:S(2)}, u32[]{:S(2)}) collective-permute-start(bf16[8,176,128]{2,1,0:T(8,128)(2,1)S(1)} %get-tuple-element.49), channel_id=1, source_target_pairs={{1,2},{2,1},{5,6},{6,5},{9,10},{10,9},{13,14},{14,13},{17,18},{18,... | collective-permute-start | bytes 1081352 | tf_op jit(solution)/shard_map/ppermute | solution.py:40
  39.5 7.3 %collective-permute-start.6 = (bf16[4,112,128]{2,1,0:T(8,128)(2,1)S(1)}, bf16[4,112,128]{2,1,0:T(8,128)(2,1)S(1)}, u32[]{:S(2)}, u32[]{:S(2)}) collective-permute-start(bf16[4,112,128]{2,1,0:T(8,128)(2,1)S(1)} %get-tuple-element.69), channel_id=1, source_target_pairs={{0,4},{4,0},{8,12},{12,8},{16,20},{20,16},{24,28},{28,24},{1,5},{5... | collective-permute-start | bytes 344072 | tf_op jit(solution)/shard_map/ppermute | solution.py:40
  39.6 7.3 %collective-permute-start.7 = (bf16[4,112,128]{2,1,0:T(8,128)(2,1)S(1)}, bf16[4,112,128]{2,1,0:T(8,128)(2,1)S(1)}, u32[]{:S(2)}, u32[]{:S(2)}) collective-permute-start(bf16[4,112,128]{2,1,0:T(8,128)(2,1)S(1)} %get-tuple-element.70), channel_id=1, source_target_pairs={{4,8},{8,4},{12,16},{16,12},{20,24},{24,20},{28,0},{0,28},{5,9},{9... | collective-permute-start | bytes 344072 | tf_op jit(solution)/shard_map/ppermute | solution.py:40
  45.0 6.4 %collective-permute-start.4 = (bf16[4,112,128]{2,1,0:T(8,128)(2,1)S(1)}, bf16[4,112,128]{2,1,0:T(8,128)(2,1)S(1)}, u32[]{:S(2)}, u32[]{:S(2)}) collective-permute-start(bf16[4,112,128]{2,1,0:T(8,128)(2,1)S(1)} %get-tuple-element.58), channel_id=1, source_target_pairs={{0,4},{4,0},{8,12},{12,8},{16,20},{20,16},{24,28},{28,24},{1,5},{5... | collective-permute-start | bytes 344072 | tf_op jit(solution)/shard_map/ppermute | solution.py:40
  45.1 6.4 %collective-permute-start.5 = (bf16[4,112,128]{2,1,0:T(8,128)(2,1)S(1)}, bf16[4,112,128]{2,1,0:T(8,128)(2,1)S(1)}, u32[]{:S(2)}, u32[]{:S(2)}) collective-permute-start(bf16[4,112,128]{2,1,0:T(8,128)(2,1)S(1)} %get-tuple-element.59), channel_id=1, source_target_pairs={{4,8},{8,4},{12,16},{16,12},{20,24},{24,20},{28,0},{0,28},{5,9},{9... | collective-permute-start | bytes 344072 | tf_op jit(solution)/shard_map/ppermute | solution.py:40

commit v5 on v4

--- a/solution.py
+++ b/solution.py
@@ -19,9 +19,11 @@
 VG = 8
 VMEM_LIMIT = 24 * 2**20
 ROWS_LIMIT = 50 * 2**20
-EDGE_LEVELS = 4
+EDGE_LEVELS = 8
+ADVECT_UNROLL = 2
 SIDE_LEVELS = 4
 PARTS = 2
+PACK_UNROLL = 4
 f32 = jnp.float32
 bf16 = jnp.bfloat16
 
@@ -189,9 +191,8 @@
         for k, x in enumerate(table(place_in)):
             ref[first + k] = x
     spot = lax.broadcasted_iota(jnp.int32, keep_ref.shape, 0)
-    counts = ((spot > 0) & (spot <= SIDE)) | ((spot >= 3 * SIDE - 1) & (spot < 4 * SIDE - 1))
-    place_in = jnp.where(spot < SLOT, spot - SIDE, cols - SIDE + spot - SLOT) + flag_ref[2] * cols
-    keep_ref[...] = (counts & (place_in >= 0) & (place_in < n_lat)).astype(f32)
+    place_in = jnp.where(spot < SIDE, spot - SIDE + 1, cols - SIDE - 1 + spot) + flag_ref[2] * cols
+    keep_ref[...] = ((place_in >= 0) & (place_in < n_lat)).astype(f32)
 
 
 def main_kernel(x_ref, st_ref, w1_ref, w2_ref, b1_ref, glo_ref, ghi_ref, first_ref, last_ref, st8_ref, own_ref, ps_ref,
@@ -207,6 +208,21 @@
     def _():
         e_ref[...] = jnp.zeros_like(e_ref)
         h_ref[...] = jnp.zeros_like(h_ref)
+
+    place_in = lax.broadcasted_iota(jnp.int32, (cols, 2 * chans), 0)
+    within = (place_in > 0) & (place_in < cols - 1)
+
+    def hidden_pair(m):
+        lhs = jnp.concatenate([s_ref[2 * m + r] for r in range(4)], axis=1)
+        acc = jnp.dot(lhs, w1_ref[...], preferred_element_type=f32) + b1_ref[...]
+        hid = jnp.where(within, silu(acc), 0.0).astype(bf16)
+        for k in range(2):
+            h_ref[2 * m + 2 + k] = hid[:, k * chans : (k + 1) * chans]
+
+    def sum_pair(m):
+        q = nt(w2_ref[...], jnp.concatenate([h_ref[2 * m + r] for r in range(4)], axis=1))
+        for k in range(2):
+            ps_ref[0, 2 * m + k] = join_taps(q[k * 3 * SLOT : (k + 1) * 3 * SLOT])
 
     sides = [[], []]
     for row in range(rows):
@@ -222,18 +238,10 @@
         shifted(e_ref, start, s_ref, row, cols)
     first_ref[0] = jnp.concatenate(sides[0], axis=0).astype(bf16)
     last_ref[0] = jnp.concatenate(sides[1], axis=0).astype(bf16)
-    place_in = lax.broadcasted_iota(jnp.int32, (cols, 2 * chans), 0)
-    within = (place_in > 0) & (place_in < cols - 1)
     for m in range(half - 1):
-        lhs = jnp.concatenate([s_ref[2 * m + r] for r in range(4)], axis=1)
-        acc = jnp.dot(lhs, w1_ref[...], preferred_element_type=f32) + b1_ref[...]
-        hid = jnp.where(within, silu(acc), 0.0).astype(bf16)
-        for k in range(2):
-            h_ref[2 * m + 2 + k] = hid[:, k * chans : (k + 1) * chans]
+        hidden_pair(m)
     for m in range(half):
-        q = nt(w2_ref[...], jnp.concatenate([h_ref[2 * m + r] for r in range(4)], axis=1))
-        for k in range(2):
-            ps_ref[0, 2 * m + k] = join_taps(q[k * 3 * SLOT : (k + 1) * 3 * SLOT])
+        sum_pair(m)
     for n in range(nvar):
         x32_ref[pl.ds(n, rows, stride=VG), :] = st_ref[n, 0]
     lane = lanes((VG, WIDE))
@@ -316,7 +324,6 @@
     even = flag_ref[0] == 0
     lat_even = flag_ref[1] == 0
     wide = 2 * SLOT
-    total = (rows + 2) * wide
     lane = lanes((2 * VG, WIDE))
     begin, end = lane < SLOT, lane >= WIDE - SLOT
     e_ref[...] = jnp.zeros_like(e_ref)
@@ -346,51 +353,54 @@
             start = SIDE + (row + 1) * wide
             for k, part in enumerate((left[side], mine[0], mine[1], right[side])):
                 e_ref[lv, start + k * SIDE : start + (k + 1) * SIDE] = part
-        for b in range(3):
-            s_ref[lv, :, b * ch : (b + 1) * ch] = e_ref[lv, pl.ds(SIDE - 1 + b, total), :].astype(bf16)
-    s = s_ref[...].reshape(levels, half + 1, 2, wide, 3 * ch)
+        for row in range(rows + 2):
+            for b in range(3):
+                start = SIDE + row * wide + b
+                x = [e_ref[lv, pl.ds(start, SIDE), :], e_ref[lv, pl.ds(start + 3 * SIDE - 2, SIDE), :]]
+                x = jnp.concatenate(x, axis=0).astype(bf16)
+                s_ref[lv, row * SLOT : (row + 1) * SLOT, b * ch : (b + 1) * ch] = x
+    s = s_ref[...].reshape(levels, half + 1, 2, SLOT, 3 * ch)
     part = [s[:, 0:half, 0], s[:, 0:half, 1], s[:, 1:, 0], s[:, 1:, 1]]
-    lhs = jnp.concatenate([p.reshape(levels * half * wide, 3 * ch) for p in part], axis=1)
+    lhs = jnp.concatenate([p.reshape(levels * half * SLOT, 3 * ch) for p in part], axis=1)
     acc = jnp.dot(lhs, w1_ref[...], preferred_element_type=f32) + b1_ref[...]
-    hid = silu(acc).reshape(levels, half, wide, 2 * ch) * keep_ref[...]
+    hid = silu(acc).reshape(levels, half, SLOT, 2 * ch) * keep_ref[...]
     for lv in range(levels):
         for m in range(half):
-            for side in range(2):
-                here = hid[lv, m, side * SLOT : (side + 1) * SLOT].astype(bf16)
-                hs_ref[lv, side, 0, m * SLOT : (m + 1) * SLOT] = here[:, 0:ch]
-                hs_ref[lv, side, 1, (m + 1) * SLOT : (m + 2) * SLOT] = here[:, ch:]
-                at = (4 * lv + side) * SLOT
-                if m == 0:
-                    z_ref[at : at + SLOT] = here[:, 0:ch]
-                if m == half - 1:
-                    z_ref[at + 2 * SLOT : at + 3 * SLOT] = here[:, ch:]
+            here = hid[lv, m].astype(bf16)
+            hs_ref[lv, 0, m * SLOT : (m + 1) * SLOT] = here[:, 0:ch]
+            hs_ref[lv, 1, (m + 1) * SLOT : (m + 2) * SLOT] = here[:, ch:]
+            if m == 0:
+                z_ref[2 * lv * SLOT : (2 * lv + 1) * SLOT] = here[:, 0:ch]
+            if m == half - 1:
+                z_ref[(2 * lv + 1) * SLOT : (2 * lv + 2) * SLOT] = here[:, ch:]
     size = half * SLOT
     rhs = []
     for lv in range(levels):
-        for side in range(2):
-            odd, ev = hs_ref.at[lv, side, 1], hs_ref.at[lv, side, 0]
-            rhs.append(jnp.concatenate([odd[0:size], ev[0:size], odd[SLOT : size + SLOT], ev[SLOT : size + SLOT]], axis=1))
+        odd, ev = hs_ref.at[lv, 1], hs_ref.at[lv, 0]
+        rhs.append(jnp.concatenate([odd[0:size], ev[0:size], odd[SLOT : size + SLOT], ev[SLOT : size + SLOT]], axis=1))
     q_side = nt(w2_ref[...], jnp.concatenate(rhs, axis=0))
     q_ends = nt(w2e_ref[...], z_ref[...])
+    in_left = lanes((SLOT, WIDE)) % SLOT < SIDE
+
+    def join_sides(q):
+        taps = [q[b * SLOT : (b + 1) * SLOT] for b in range(3)]
+        l = [jnp.where(in_left, x, 0.0) for x in taps]
+        r = [jnp.where(in_left, 0.0, x) for x in taps]
+        l = roll(l[0], 2) + roll(l[1], 1) + l[2]
+        r = r[0] + roll(r[1], -1) + roll(r[2], -2)
+        return mix(l, r), mix(r, l)
+
     for lv in range(levels):
-        tiles = []
-        for side in range(2):
-            q = q_side[:, (2 * lv + side) * size : (2 * lv + side + 1) * size]
-            tiles.append([join_taps(q[k * 3 * SLOT : (k + 1) * 3 * SLOT]) for k in range(2)])
-        per = WIDE // (4 * SLOT)
-        q = roll(q_ends[:, (lv // per) * WIDE : (lv // per + 1) * WIDE], -(lv % per) * 4 * SLOT)
-        prev = join_taps(q[3 * SLOT : 6 * SLOT])
-        nxt = join_taps(q[0 : 3 * SLOT])
         out, inn = {}, {}
+        q = q_side[:, lv * size : (lv + 1) * size]
         for k in range(2):
-            out[k] = mix(tiles[0][k], tiles[1][k])
-            inn[k] = mix(tiles[1][k], tiles[0][k])
-        for k, x, s0 in ((3, prev, 0), (2, nxt, 2)):
-            spot = end if k == 3 else begin
-            to = WIDE - SLOT if k == 3 else 0
-            at_l, at_r = roll(x, to - s0 * SLOT), roll(x, to - (s0 + 1) * SLOT)
-            out[k] = jnp.where(spot, mix(at_l, at_r), 0.0)
-            inn[k] = jnp.where(spot, mix(at_r, at_l), 0.0)
+            out[k], inn[k] = join_sides(q[k * 3 * SLOT : (k + 1) * 3 * SLOT])
+        per = WIDE // (2 * SLOT)
+        q = roll(q_ends[:, (lv // per) * WIDE : (lv // per + 1) * WIDE], -(lv % per) * 2 * SLOT)
+        prev = join_sides(q[3 * SLOT : 6 * SLOT])
+        nxt = join_sides(q[0 : 3 * SLOT])
+        for k, x, spot, by in ((3, prev, end, WIDE - SLOT), (2, nxt, begin, -SLOT)):
+            out[k], inn[k] = (jnp.where(spot, roll(y, by), 0.0) for y in x)
         for k in range(4):
             pm_ref[lv, k] = out[k]
             cm_ref[lv, k] = inn[k]
@@ -520,12 +530,13 @@
     ub, ua = tile_rows(us)
 
     def coefs(m, uu, vv, udiff, vdiff):
-        div = m * (udiff * 0.5 + vdiff * 0.5)
-        cl = m * jnp.maximum(uu, 0.0)
-        cr = -(m * jnp.minimum(uu, 0.0))
+        flow = m * uu
+        cl = jnp.maximum(flow, 0.0)
+        cr = cl - flow
         cd = jnp.maximum(vv, 0.0)
-        cu = -jnp.minimum(vv, 0.0)
-        return -(cl + cr + cd + cu + div), cl, cr, cd, cu
+        cu = cd - vv
+        div = (0.5 * m) * (udiff + vdiff)
+        return -((cl + cr) + (cd + cu) + div), cl, cr, cd, cu
 
     cm = {r: coefs(metric, u[r], v[r], u[r + 1] - u[r - 1], roll(flux[r], -1) - roll(flux[r], 1)) for r in inside}
     cs = {k: coefs(metric_s[k], us[k], vs[k], ua[k] - ub[k], roll(flux_s[k], -1) - roll(flux_s[k], 1)) for k in range(8)}
@@ -549,7 +560,7 @@
     four = rate(*moved(three, time_step), 4)
 
     def mean(n, k):
-        return (one[n][k] + 2.0 * two[n][k] + 2.0 * three[n][k] + four[n][k]) / 6.0
+        return (one[n][k] + four[n][k] + 2.0 * (two[n][k] + three[n][k])) * (1.0 / 6.0)
 
     ends = {k: mix(mean(1, 4 + k), mean(1, k)) for k in range(2)}
     for row in range(rows):
@@ -602,9 +613,40 @@
             input_output_aliases=aliases,
         )(*args)
 
+    vmem = pl.BlockSpec(memory_space=pltpu.VMEM)
+
+    def levels(block=1, off=0, first=None, size=None):
+        def view(ref, i):
+            here = pl.ds(off + i * block, block)
+            return ref.at[here] if first is None else ref.at[here, first : first + size]
+
+        return view
+
+    def whole(kernel, steps, ins, outs, scratch, cost, unroll=1):
+        views = [v for _, v in ins] + [v for _, v in outs]
+
+        def run(*refs):
+            def one(i, carry):
+                kernel(*[v(r, i) if v else r for v, r in zip(views, refs)], *refs[len(views) :])
+                return carry
+
+            if steps == 1:
+                one(0, 0)
+            else:
+                lax.fori_loop(0, steps, one, 0, unroll=unroll)
+
+        return pl.pallas_call(
+            run,
+            in_specs=[smem if x is flags else vmem for x, _ in ins],
+            out_specs=[vmem] * len(outs),
+            out_shape=[x for x, _ in outs],
+            scratch_shapes=scratch,
+            compiler_params=params,
+            cost_estimate=pl.CostEstimate(flops=cost, bytes_accessed=2**20, transcendentals=0),
+        )(*[x for x, _ in ins])
+
     flags = jnp.stack([lax.axis_index("lon") % 2, lax.axis_index("lat") % 2, lax.axis_index("lat")]).astype(jnp.int32)
     lon_wire = (lev, ch + 2 * nvar * REACH, cols)
-    vmem = pl.BlockSpec(memory_space=pltpu.VMEM)
     lon_a, lon_b = pl.pallas_call(
         rows_kernel,
         in_specs=[smem] + [pl.BlockSpec(memory_space=pltpu.HBM)] * 2,
@@ -620,7 +662,7 @@
     )(flags, hidden_in, state)
     shapes = [((12 * ch, 2 * ch), bf16), ((6 * SLOT, 4 * ch), bf16), ((9 * SLOT, ch), bf16),
               ((6 * SLOT, ch), bf16), ((1, 2 * ch), f32), ((2 * VG, WIDE), f32), ((3, VG, WIDE), f32), ((6, VG, WIDE), f32),
-              ((2 * SLOT, 2 * ch), f32)]
+              ((SLOT, 2 * ch), f32)]
     w1_one = w_conv1.reshape(9 * ch, ch)
     b1 = b_conv1.reshape(1, ch)
     n_lat = cols * lax.axis_size("lat")
@@ -662,36 +704,34 @@
     lat_wire = (lev, (rows + 2) * SIDE + 4 * VG, WIDE)
     pair_shape = (lev, 2, cols, ch)
     shapes = [(pair_shape, bf16), (halo_shape, f32), (lat_wire, bf16), (lat_wire, bf16)]
-    row_pair, halo, lat_a, lat_b = call(
+    each = levels()
+    row_pair, halo, lat_a, lat_b = whole(
         pack_kernel,
         lev,
-        [smem, per_level(lon_wire), per_level(lon_wire), per_level(cut), per_level(cut), per_level(own_shape)],
-        [sds(*x) for x in shapes],
-        [per_level(x[0]) for x in shapes],
+        [(flags, None)] + [(x, each) for x in (lon_a, lon_b, first, last, own)],
+        [(sds(*x), each) for x in shapes],
         [pltpu.VMEM((nvar * REACH, WIDE), f32)],
-        (flags, lon_a, lon_b, first, last, own),
+        2**22,
+        PACK_UNROLL,
     )
     lat_a = swap(lat_a, "lat", 0, False)
     lat_b = swap(lat_b, "lat", 1, False)
 
     block = EDGE_LEVELS
-    four = (4, 2 * VG, WIDE)
     pe_shape = (lev, 6, 2 * VG, WIDE)
-    here = functools.partial(levels_of, block=block)
-    (pe,) = call(
+    each = levels(block)
+    (pe,) = whole(
         edge_kernel,
         lev // block,
-        [here(pair_shape), here(g_pair), here(g_pair), full(w1_one.shape), full(w2_one.shape), full((1, ch)),
-         level_part(four, 0, block), level_part(four, rows // 4 - 1, block)],
-        [sds(pe_shape, f32)],
-        [here(pe_shape)],
+        [(row_pair, each), (g_lo, each), (g_hi, each), (w1_one, None), (w2_one, None), (b1, None),
+         (ps, levels(block, 0, 0, 4)), (ps, levels(block, 0, rows - 4, 4))],
+        [(sds(pe_shape, f32), each)],
         [
             pltpu.VMEM((6 * block * (cols + SLOT), ch), f32),
             pltpu.VMEM((2 * block, cols, 9 * ch), bf16),
             pltpu.VMEM((2 * block * cols, ch), bf16),
         ],
-        (row_pair, g_lo, g_hi, w1_one, w2_one, b1, ps, ps),
-        pl.CostEstimate(flops=lev * 2 * 2 * ext * 9 * ch * ch, bytes_accessed=4 * 2**20, transcendentals=0),
+        lev * 4 * ext * 9 * ch * ch,
     )
 
     block = SIDE_LEVELS
@@ -704,24 +744,22 @@
     shapes = [(sst_shape, f32), (pm4_shape, f32), (pm4_shape, f32), (pec_shape, f32), (wire, bf16), (wire, bf16)]
     sent = []
     for part in range(parts):
-        off = part * count // block
-        here = functools.partial(levels_of, block=block, offset=off)
-        sst, pm, cm, pec, out_a, out_b = call(
+        here = levels(block, part * count)
+        each = levels(block)
+        sst, pm, cm, pec, out_a, out_b = whole(
             side_kernel,
             count // block,
-            [smem, here(cut), here(cut), here(pair_shape), here(lat_wire), here(lat_wire),
-             full(w1_pair.shape), full(w2_pair.shape), full(w2_ends.shape), full((1, 2 * ch)), full((2 * SLOT, 2 * ch)),
-             here(pe_shape), level_part(four, 0, block, off), level_part(four, rows // 4 - 1, block, off)],
-            [sds(*x) for x in shapes],
-            [levels_of(x[0], block) for x in shapes],
+            [(flags, None)] + [(x, here) for x in (first, last, row_pair, lat_a, lat_b)]
+            + [(x, None) for x in (w1_pair, w2_pair, w2_ends, b1_pair, keep)]
+            + [(pe, here), (ps, levels(block, part * count, 0, 4)), (ps, levels(block, part * count, rows - 4, 4))],
+            [(sds(*x), each) for x in shapes],
             [
                 pltpu.VMEM((block, (rows + 2) * 2 * SLOT + 2 * SIDE, ch), f32),
-                pltpu.VMEM((block, (rows + 2) * 2 * SLOT, 3 * ch), bf16),
-                pltpu.VMEM((block, 2, 2, (half + 1) * SLOT, ch), bf16),
-                pltpu.VMEM((max(WIDE, block * 4 * SLOT), ch), bf16),
+                pltpu.VMEM((block, (rows + 2) * SLOT, 3 * ch), bf16),
+                pltpu.VMEM((block, 2, (half + 1) * SLOT, ch), bf16),
+                pltpu.VMEM((max(WIDE, block * 2 * SLOT), ch), bf16),
             ],
-            (flags, first, last, row_pair, lat_a, lat_b, w1_pair, w2_pair, w2_ends, b1_pair, keep, pe, ps, ps),
-            pl.CostEstimate(flops=count * 512 * 12 * ch * ch, bytes_accessed=4 * 2**20, transcendentals=0),
+            count * 512 * 12 * ch * ch,
         )
         sent.append((pec, pm, cm, sst, swap(out_a, "lon", 0, True), swap(out_b, "lon", 1, True)))
 
@@ -729,21 +767,48 @@
     done = ()
     for part, (pec, pm, cm, sst, out_a, out_b) in enumerate(sent):
         off = part * count
-        here = functools.partial(levels_of, offset=off)
-        var = functools.partial(var_level, offset=off)
-        done = call(
-            advect_kernel,
-            count,
-            [smem, here(ps_shape), per_level(pec_shape), per_level(pm4_shape), per_level(pm4_shape), per_level(wire),
-             per_level(wire), here(st8.shape), here(halo_shape), per_level(sst_shape), here(own_shape),
-             full(b2.shape), full(lat_main.shape), full(lat_side.shape)] + [hbm] * len(done),
-            outs,
-            [var(o.shape) for o in outs],
-            [pltpu.VMEM((2, rows * VG, WIDE), f32)],
-            (flags, ps, pec, pm, cm, out_a, out_b, st8, halo, sst, own, b2, lat_main, lat_side) + tuple(done),
-            pl.CostEstimate(flops=count * 2**24, bytes_accessed=2 * 2**20, transcendentals=0),
-            {14: 0, 15: 1} if done else {},
-        )
+        here, each = levels(1, off), levels()
+        ins = [(flags, None), (ps, here)] + [(x, each) for x in (pec, pm, cm, out_a, out_b)]
+        ins += [(st8, here), (halo, here), (sst, each), (own, here)] + [(x, None) for x in (b2, lat_main, lat_side)]
+
+        def run(*refs, off=off, ins=ins, given=len(done)):
+            sources = [functools.partial(v, r) if v else (lambda i, r=r: r) for (_, v), r in zip(ins, refs)]
+            vel_hbm, ten_hbm, vel_ref, ten_ref, out_ref, sem = refs[len(ins) + given :]
+
+            def copies(i):
+                at, to = pl.ds(i, 1), pl.ds(off + i, 1)
+                return [
+                    pltpu.make_async_copy(src.at[:, at], dst.at[:, to], sem.at[i, k])
+                    for k, (src, dst) in enumerate(((vel_ref, vel_hbm), (ten_ref, ten_hbm)))
+                ]
+
+            def one(i, carry):
+                at = pl.ds(i, 1)
+                advect_kernel(*[f(i) for f in sources], vel_ref.at[:, at], ten_ref.at[:, at], out_ref.at[i])
+                for copy in copies(i):
+                    copy.start()
+                return carry
+
+            lax.fori_loop(0, count, one, 0, unroll=ADVECT_UNROLL)
+            for i in range(count):
+                for copy in copies(i):
+                    copy.wait()
+
+        done = pl.pallas_call(
+            run,
+            in_specs=[smem if x is flags else vmem for x, _ in ins] + [hbm] * len(done),
+            out_specs=[hbm] * 2,
+            out_shape=outs,
+            scratch_shapes=[
+                pltpu.VMEM((2 * nvar, count, rows, cols), f32),
+                pltpu.VMEM((nvar, count, rows, cols), f32),
+                pltpu.VMEM((count, 2, rows * VG, WIDE), f32),
+                pltpu.SemaphoreType.DMA((count, 2)),
+            ],
+            compiler_params=params,
+            cost_estimate=pl.CostEstimate(flops=count * 2**24, bytes_accessed=2 * 2**20, transcendentals=0),
+            input_output_aliases={len(ins): 0, len(ins) + 1: 1} if done else {},
+        )(*[x for x, _ in ins], *done)
     return tuple(done)
 
 

time: 56.4 us -> 54.7 us (0.970)
  Pallas kernels: 36.9 us -> 33.7 us
  waiting for transfers between devices: 3.02 us -> 4.66 us
    pallas_call x7 -> x1, Pallas kernels: 33.2 us -> 13.9 us  [call(): pl.pallas_call(kernel, grid=(steps,), in_specs=ins, out_specs=out_specs,...]
    pallas_call x0 -> x6, Pallas kernels: none -> 16.1 us  [the longest x2 8.74 us: body(): pl.pallas_call(run, in_specs=[smem if x is flags else vmem for x, _ in in...]
    ppermute x8, waiting for transfers between devices: 3.02 us -> 4.66 us  [swap(): lax.ppermute(block, axis, swap_pairs(lax.axis_size(axis), first, closed))]
  transfers between devices with their start and end apart: 8 -> 8, of which waited for: 2 -> 2; matrix products, arithmetic and copies ran while one was open for 0% -> 0% of each run, Pallas kernels for 44% -> 43%
where the time goes in v5:
time: 54.7 us; the launch traced here: 54.6 us
  Pallas kernels  33.7 us (62%)
  starting transfers between devices  14.2 us (26%)
  waiting for transfers between devices  4.66 us (9%)
  local copies, waits for them, and re-layouts  1.17 us (2%)
  between operations  0.8 us (1%)
    ppermute x8, starting transfers between devices, swap(): lax.ppermute(block, axis, swap_pairs(lax.axis_size(axis), first, closed))  14.2 us
    pallas_call x1, Pallas kernels, call(): pl.pallas_call(kernel, grid=(steps,), in_specs=ins, out_specs=out_specs,...  13.9 us
    pallas_call x2, Pallas kernels, body(): pl.pallas_call(run, in_specs=[smem if x is flags else vmem for x, _ in in...  8.74 us
    pallas_call x4, Pallas kernels, whole(): pl.pallas_call(run, in_specs=[smem if x is flags else vmem for x, _ in in...  7.33 us
    ppermute x8, waiting for transfers between devices, swap(): lax.ppermute(block, axis, swap_pairs(lax.axis_size(axis), first, closed))  4.66 us
    pallas_call x1, Pallas kernels, body(): pl.pallas_call(rows_kernel, in_specs=[smem] + [pl.BlockSpec(memory_space=...  2.95 us
    unnamed x12, local copies, waits for them, and re-layouts  1.17 us
  transfers between devices with their start and end apart: 8, of which 2 were waited for; matrix products, arithmetic and copies ran while one was open for 0% of the time, Pallas kernels for 43%

profile of v5, /device:TPU:1, one launch (start us, length us, event | category | flops | bytes accessed | tf_op | source)
XLA Modules:
  0.0 54.6 jit_solution(4270145014810580491)
XLA Ops:
  0.6 0.0 copy-start.1
  0.7 0.0 copy-start
  0.7 0.1 pad_add_fusion.flag_ref.refs_0_
  0.7 0.0 copy-start.2
  0.7 1.1 %copy-done.2 = f32[6,8,16,128]{3,2,1,0:T(8,128)S(1)} copy-done((f32[6,8,16,128]{3,2,1,0:T(8,128)S(1)}, f32[6,8,16,128]{3,2,1,0:T(8,128)}, u32[]{:S(2)}) %copy-start.2) | copy-done | bytes 393240
  1.9 0.0 copy-start.3
  1.9 0.0 copy-start.4
  1.9 0.0 copy-start.5
  1.9 3.0 %shard_map.79 = (bf16[8,176,128]{2,1,0:T(8,128)(2,1)S(1)}, bf16[8,176,128]{2,1,0:T(8,128)(2,1)S(1)}) custom-call(s32[3]{0:T(128)S(1)} %pad_add_fusion.flag_ref.refs_0_, bf16[8,128,16,128]{3,2,1,0:T(8,128)(2,1)} %x_hbm.1, f32[6,8,16,128]{3,2,1,0:T(8,128)S(1)} %copy-done.2), custom_call_target="tpu_custom_call" | custom-call | tf_op jit(solution)/shard_map/pallas_call | solution.py:650
  4.9 2.1 %collective-permute-start = (bf16[8,176,128]{2,1,0:T(8,128)(2,1)S(1)}, bf16[8,176,128]{2,1,0:T(8,128)(2,1)S(1)}, u32[]{:S(2)}, u32[]{:S(2)}) collective-permute-start(bf16[8,176,128]{2,1,0:T(8,128)(2,1)S(1)} %get-tuple-element.44), channel_id=1, source_target_pairs={{0,4},{4,0},{8,12},{12,8},{16,20},{20,16},{24,28},{28,24},{1,5},{5... | collective-permute-start | bytes 1081352 | tf_op jit(solution)/shard_map/ppermute | solution.py:42
  7.0 3.3 %collective-permute-start.1 = (bf16[8,176,128]{2,1,0:T(8,128)(2,1)S(1)}, bf16[8,176,128]{2,1,0:T(8,128)(2,1)S(1)}, u32[]{:S(2)}, u32[]{:S(2)}) collective-permute-start(bf16[8,176,128]{2,1,0:T(8,128)(2,1)S(1)} %get-tuple-element.45), channel_id=1, source_target_pairs={{4,8},{8,4},{12,16},{16,12},{20,24},{24,20},{28,0},{0,28},{5,9},{9... | collective-permute-start | bytes 1081352 | tf_op jit(solution)/shard_map/ppermute | solution.py:42
  10.3 0.0 copy-done.1
  10.3 0.0 copy-done.3
  10.3 0.0 copy-done.4
  10.3 0.0 copy-done.5
  10.3 0.7 %shard_map.77 = (bf16[1536,256]{1,0:T(8,128)(2,1)S(1)}, bf16[96,512]{1,0:T(8,128)(2,1)S(1)}, bf16[144,128]{1,0:T(8,128)(2,1)S(1)}, bf16[96,128]{1,0:T(8,128)(2,1...) custom-call(s32[3]{0:T(128)S(1)} %pad_add_fusion.flag_ref.refs_0_, ...), custom_call_target="tpu_custom_call" | custom-call | tf_op jit(solution)/shard_map/pallas_call | solution.py:669
  11.0 0.0 copy-done
  11.0 13.9 %shard_map.78 = (bf16[8,2,128,128]{3,2,1,0:T(8,128)(2,1)S(1)}, bf16[8,2,128,128]{3,2,1,0:T(8,128)(2,1)S(1)}, bf16[8,128,128]{2,1,0:T(8,128)(2,1)S(1)}, bf16[8,12...) custom-call(bf16[8,128,16,128]{3,2,1,0:T(8,128)(2,1)S(1)} %copy-done, ...), custom_call_target="tpu_custom_call" | custom-call | flops 5435817984 | bytes 8388608 | tf_op jit(solution)/shard_map/pallas_call | solution.py:604
  25.0 0.0 collective-permute-done.refs_1_
  25.0 0.0 collective-permute-done.1.refs_2_
  25.0 0.9 %shard_map.80 = (bf16[8,2,128,128]{3,2,1,0:T(8,128)(2,1)S(1)}, f32[8,8,8,128]{3,2,1,0:T(8,128)S(1)}, bf16[8,176,128]{2,1,0:T(8,128)(2,1)S(1)}, bf16[8,176,128]{2,1,0:T(8,128)(2,1)S(1)}) custom-call(s32[3]{0:T(128)S(1)} %pad_add_fusion.flag_ref.refs_0_, bf16[8,176,128]{2,1,0:T(8,128)(2,1)S(1)} %collective-permute-done.refs_1_, ...), custom_call_target="tpu_custom_call" | custom-call | flops 4194304 | bytes 1048576 | tf_op jit(solution)/shard_map/pallas_call | solution.py:638
  25.9 1.3 %collective-permute-start.2 = (bf16[8,176,128]{2,1,0:T(8,128)(2,1)S(1)}, bf16[8,176,128]{2,1,0:T(8,128)(2,1)S(1)}, u32[]{:S(2)}, u32[]{:S(2)}) collective-permute-start(bf16[8,176,128]{2,1,0:T(8,128)(2,1)S(1)} %get-tuple-element.48), channel_id=1, source_target_pairs={{0,1},{1,0},{2,3},{3,2},{4,5},{5,4},{6,7},{7,6},{8,9},{9,8},{10,11... | collective-permute-start | bytes 1081352 | tf_op jit(solution)/shard_map/ppermute | solution.py:42
  27.2 3.0 %collective-permute-start.3 = (bf16[8,176,128]{2,1,0:T(8,128)(2,1)S(1)}, bf16[8,176,128]{2,1,0:T(8,128)(2,1)S(1)}, u32[]{:S(2)}, u32[]{:S(2)}) collective-permute-start(bf16[8,176,128]{2,1,0:T(8,128)(2,1)S(1)} %get-tuple-element.49), channel_id=1, source_target_pairs={{1,2},{2,1},{5,6},{6,5},{9,10},{10,9},{13,14},{14,13},{17,18},{18,... | collective-permute-start | bytes 1081352 | tf_op jit(solution)/shard_map/ppermute | solution.py:42
  30.3 2.3 %shard_map.81.refs_11_ = f32[8,6,16,128]{3,2,1,0:T(8,128)S(1)} custom-call(bf16[8,2,128,128]{3,2,1,0:T(8,128)(2,1)S(1)} %get-tuple-element.47.refs_0_.refs_3_, bf16[8,2,128,128]{3,2,1,0:T(8,128)(2,1)S(1)} %get-tuple-element.52.refs_1_, bf16[8,2,128,128]{3,2,1,0:T(8,128)(2,1)S(1)} %get-tuple-element.53.refs_2_, bf16[1152,128]{1,0:T(8,128)(2,1)S(1)} %bitcast.9, ...), custom_call_target="tpu_custom_call" | custom-call | flops 679477248 | bytes 1048576 | tf_op jit(solution)/shard_map/pallas_call | solution.py:638
  32.6 0.0 collective-permute-done.2.refs_4_
  32.6 3.7 %collective-permute-done.3.refs_5_ = bf16[8,176,128]{2,1,0:T(8,128)(2,1)S(1)} collective-permute-done((bf16[8,176,128]{2,1,0:T(8,128)(2,1)S(1)}, bf16[8,176,128]{2,1,0:T(8,128)(2,1)S(1)}, u32[]{:S(2)}, u32[]{:S(2)}) %collective-permute-start.3) | collective-permute-done | bytes 360480 | tf_op jit(solution)/shard_map/ppermute | solution.py:42
  36.3 2.1 %shard_map.83 = (f32[4,2,8,128]{3,2,1,0:T(8,128)S(1)}, f32[4,4,16,128]{3,2,1,0:T(8,128)S(1)}, f32[4,4,16,128]{3,2,1,0:T(8,128)S(1)}, f32[4,6,16,128]{3,2,1,0:T(8...) custom-call(s32[3]{0:T(128)S(1)} %pad_add_fusion.flag_ref.refs_0_, ...), custom_call_target="tpu_custom_call" | custom-call | flops 402653184 | bytes 1048576 | tf_op jit(solution)/shard_map/pallas_call | solution.py:638
  38.3 0.1 collective-permute-start.6
  38.4 2.6 %collective-permute-start.7 = (bf16[4,112,128]{2,1,0:T(8,128)(2,1)S(1)}, bf16[4,112,128]{2,1,0:T(8,128)(2,1)S(1)}, u32[]{:S(2)}, u32[]{:S(2)}) collective-permute-start(bf16[4,112,128]{2,1,0:T(8,128)(2,1)S(1)} %get-tuple-element.70), channel_id=1, source_target_pairs={{4,8},{8,4},{12,16},{16,12},{20,24},{24,20},{28,0},{0,28},{5,9},{9... | collective-permute-start | bytes 344072 | tf_op jit(solution)/shard_map/ppermute | solution.py:42
  41.0 2.1 %shard_map.82 = (f32[4,2,8,128]{3,2,1,0:T(8,128)S(1)}, f32[4,4,16,128]{3,2,1,0:T(8,128)S(1)}, f32[4,4,16,128]{3,2,1,0:T(8,128)S(1)}, f32[4,6,16,128]{3,2,1,0:T(8...) custom-call(s32[3]{0:T(128)S(1)} %pad_add_fusion.flag_ref.refs_0_, ...), custom_call_target="tpu_custom_call" | custom-call | flops 402653184 | bytes 1048576 | tf_op jit(solution)/shard_map/pallas_call | solution.py:638
  43.0 0.1 collective-permute-start.4
  43.1 1.7 %collective-permute-start.5 = (bf16[4,112,128]{2,1,0:T(8,128)(2,1)S(1)}, bf16[4,112,128]{2,1,0:T(8,128)(2,1)S(1)}, u32[]{:S(2)}, u32[]{:S(2)}) collective-permute-start(bf16[4,112,128]{2,1,0:T(8,128)(2,1)S(1)} %get-tuple-element.59), channel_id=1, source_target_pairs={{4,8},{8,4},{12,16},{16,12},{20,24},{24,20},{28,0},{0,28},{5,9},{9... | collective-permute-start | bytes 344072 | tf_op jit(solution)/shard_map/ppermute | solution.py:42
  44.8 0.0 collective-permute-done.6.refs_5_
  44.8 0.9 %collective-permute-done.7.refs_6_ = bf16[4,112,128]{2,1,0:T(8,128)(2,1)S(1)} collective-permute-done((bf16[4,112,128]{2,1,0:T(8,128)(2,1)S(1)}, bf16[4,112,128]{2,1,0:T(8,128)(2,1)S(1)}, u32[]{:S(2)}, u32[]{:S(2)}) %collective-permute-start.7) | collective-permute-done | bytes 114720 | tf_op jit(solution)/shard_map/ppermute | solution.py:42
  45.8 4.4 %shard_map.84 = (f32[12,8,16,128]{3,2,1,0:T(8,128)}, f32[6,8,16,128]{3,2,1,0:T(8,128)}) custom-call(s32[3]{0:T(128)S(1)} %pad_add_fusion.flag_ref.refs_0_, f32[8,16,16,128]{3,2,1,0:T(8,128)S(1)} %get-tuple-element.41.refs_6_.refs_7_.refs_12_.refs_13_.refs_1_, f32[4,6,16,128]{3,2,1,0:T(8,128)S(1)} %get-tuple-element.66.refs_2_, ...), custom_call_target="tpu_custom_call" | custom-call | flops 67108864 | bytes 2097152 | tf_op jit(solution)/shard_map/pallas_call | solution.py:797
  50.2 0.0 collective-permute-done.4.refs_5_
  50.2 0.0 collective-permute-done.5.refs_6_
  50.2 4.4 %shard_map.85 = (f32[12,8,16,128]{3,2,1,0:T(8,128)}, f32[6,8,16,128]{3,2,1,0:T(8,128)}) custom-call(s32[3]{0:T(128)S(1)} %pad_add_fusion.flag_ref.refs_0_, f32[8,16,16,128]{3,2,1,0:T(8,128)S(1)} %get-tuple-element.41.refs_6_.refs_7_.refs_12_.refs_13_.refs_1_, ...), custom_call_target="tpu_custom_call", output_to_operand_aliasing={{0}: (14, {}), {1}: (15, {})} | custom-call | flops 67108864 | bytes 2097152 | tf_op jit(solution)/shard_map/pallas_call | solution.py:797
Async XLA Ops:
  0.6 9.6 %copy-start.1 = (bf16[3,3,128,128]{3,2,1,0:T(8,128)(2,1)S(1)}, bf16[3,3,128,128]{3,2,1,0:T(8,128)(2,1)}, u32[]{:S(2)}) copy-start(bf16[3,3,128,128]{3,2,1,0:T(8,128)(2,1)} %param.7) | copy-start | bytes 884740
  0.7 10.4 %copy-start = (bf16[8,128,16,128]{3,2,1,0:T(8,128)(2,1)S(1)}, bf16[8,128,16,128]{3,2,1,0:T(8,128)(2,1)}, u32[]{:S(2)}) copy-start(bf16[8,128,16,128]{3,2,1,0:T(8,128)(2,1)} %x_hbm.1) | copy-start | bytes 12582916
  0.7 1.1 %copy-start.2 = (f32[6,8,16,128]{3,2,1,0:T(8,128)S(1)}, f32[6,8,16,128]{3,2,1,0:T(8,128)}, u32[]{:S(2)}) copy-start(f32[6,8,16,128]{3,2,1,0:T(8,128)} %st_hbm.1) | copy-start | bytes 1179652
  1.9 8.4 %copy-start.3 = (bf16[3,3,128,12]{2,3,1,0:T(8,128)(2,1)S(1)}, bf16[3,3,128,12]{2,3,1,0:T(8,128)(2,1)}, u32[]{:S(2)}) copy-start(bf16[3,3,128,12]{2,3,1,0:T(8,128)(2,1)} %param.9) | copy-start | bytes 82948
  1.9 8.4 %copy-start.4 = (f32[128]{0:T(128)S(1)}, f32[128]{0:T(128)}, u32[]{:S(2)}) copy-start(f32[128]{0:T(128)} %param.8) | copy-start | bytes 1540
  1.9 8.4 %copy-start.5 = (f32[12]{0:T(128)S(1)}, f32[12]{0:T(128)}, u32[]{:S(2)}) copy-start(f32[12]{0:T(128)} %refs_0_.1) | copy-start | bytes 148
  4.9 20.1 %collective-permute-start = (bf16[8,176,128]{2,1,0:T(8,128)(2,1)S(1)}, bf16[8,176,128]{2,1,0:T(8,128)(2,1)S(1)}, u32[]{:S(2)}, u32[]{:S(2)}) collective-permute-start(bf16[8,176,128]{2,1,0:T(8,128)(2,1)S(1)} %get-tuple-element.44), channel_id=1, source_target_pairs={{0,4},{4,0},{8,12},{12,8},{16,20},{20,16},{24,28},{28,24},{1,5},{5... | collective-permute-start | bytes 1081352 | tf_op jit(solution)/shard_map/ppermute | solution.py:42
  7.0 18.0 %collective-permute-start.1 = (bf16[8,176,128]{2,1,0:T(8,128)(2,1)S(1)}, bf16[8,176,128]{2,1,0:T(8,128)(2,1)S(1)}, u32[]{:S(2)}, u32[]{:S(2)}) collective-permute-start(bf16[8,176,128]{2,1,0:T(8,128)(2,1)S(1)} %get-tuple-element.45), channel_id=1, source_target_pairs={{4,8},{8,4},{12,16},{16,12},{20,24},{24,20},{28,0},{0,28},{5,9},{9... | collective-permute-start | bytes 1081352 | tf_op jit(solution)/shard_map/ppermute | solution.py:42
  25.9 6.6 %collective-permute-start.2 = (bf16[8,176,128]{2,1,0:T(8,128)(2,1)S(1)}, bf16[8,176,128]{2,1,0:T(8,128)(2,1)S(1)}, u32[]{:S(2)}, u32[]{:S(2)}) collective-permute-start(bf16[8,176,128]{2,1,0:T(8,128)(2,1)S(1)} %get-tuple-element.48), channel_id=1, source_target_pairs={{0,1},{1,0},{2,3},{3,2},{4,5},{5,4},{6,7},{7,6},{8,9},{9,8},{10,11... | collective-permute-start | bytes 1081352 | tf_op jit(solution)/shard_map/ppermute | solution.py:42
  27.2 9.0 %collective-permute-start.3 = (bf16[8,176,128]{2,1,0:T(8,128)(2,1)S(1)}, bf16[8,176,128]{2,1,0:T(8,128)(2,1)S(1)}, u32[]{:S(2)}, u32[]{:S(2)}) collective-permute-start(bf16[8,176,128]{2,1,0:T(8,128)(2,1)S(1)} %get-tuple-element.49), channel_id=1, source_target_pairs={{1,2},{2,1},{5,6},{6,5},{9,10},{10,9},{13,14},{14,13},{17,18},{18,... | collective-permute-start | bytes 1081352 | tf_op jit(solution)/shard_map/ppermute | solution.py:42
  38.3 6.5 %collective-permute-start.6 = (bf16[4,112,128]{2,1,0:T(8,128)(2,1)S(1)}, bf16[4,112,128]{2,1,0:T(8,128)(2,1)S(1)}, u32[]{:S(2)}, u32[]{:S(2)}) collective-permute-start(bf16[4,112,128]{2,1,0:T(8,128)(2,1)S(1)} %get-tuple-element.69), channel_id=1, source_target_pairs={{0,4},{4,0},{8,12},{12,8},{16,20},{20,16},{24,28},{28,24},{1,5},{5... | collective-permute-start | bytes 344072 | tf_op jit(solution)/shard_map/ppermute | solution.py:42
  38.4 7.4 %collective-permute-start.7 = (bf16[4,112,128]{2,1,0:T(8,128)(2,1)S(1)}, bf16[4,112,128]{2,1,0:T(8,128)(2,1)S(1)}, u32[]{:S(2)}, u32[]{:S(2)}) collective-permute-start(bf16[4,112,128]{2,1,0:T(8,128)(2,1)S(1)} %get-tuple-element.70), channel_id=1, source_target_pairs={{4,8},{8,4},{12,16},{16,12},{20,24},{24,20},{28,0},{0,28},{5,9},{9... | collective-permute-start | bytes 344072 | tf_op jit(solution)/shard_map/ppermute | solution.py:42
  43.0 7.1 %collective-permute-start.4 = (bf16[4,112,128]{2,1,0:T(8,128)(2,1)S(1)}, bf16[4,112,128]{2,1,0:T(8,128)(2,1)S(1)}, u32[]{:S(2)}, u32[]{:S(2)}) collective-permute-start(bf16[4,112,128]{2,1,0:T(8,128)(2,1)S(1)} %get-tuple-element.58), channel_id=1, source_target_pairs={{0,4},{4,0},{8,12},{12,8},{16,20},{20,16},{24,28},{28,24},{1,5},{5... | collective-permute-start | bytes 344072 | tf_op jit(solution)/shard_map/ppermute | solution.py:42
  43.1 7.1 %collective-permute-start.5 = (bf16[4,112,128]{2,1,0:T(8,128)(2,1)S(1)}, bf16[4,112,128]{2,1,0:T(8,128)(2,1)S(1)}, u32[]{:S(2)}, u32[]{:S(2)}) collective-permute-start(bf16[4,112,128]{2,1,0:T(8,128)(2,1)S(1)} %get-tuple-element.59), channel_id=1, source_target_pairs={{4,8},{8,4},{12,16},{16,12},{20,24},{24,20},{28,0},{0,28},{5,9},{9... | collective-permute-start | bytes 344072 | tf_op jit(solution)/shard_map/ppermute | solution.py:42

commit v6 on v5

--- a/solution.py
+++ b/solution.py
@@ -14,6 +14,7 @@
 
 SIDE = 8
 SLOT = 2 * SIDE
+SENT = 6
 WIDE = 128
 REACH = 4
 VG = 8
@@ -255,8 +256,9 @@
     own_ref[0, 0], own_ref[0, 1] = own
 
 
-def pack_kernel(flag_ref, a_ref, b_ref, first_ref, last_ref, own_ref, row_ref, halo_ref, outa_ref, outb_ref, x_ref):
+def pack_kernel(flag_ref, a_ref, b_ref, first_ref, last_ref, own_ref, row_ref, halo_ref, outa_ref, outb_ref, w_ref, x_ref):
     cols = a_ref.shape[2]
+    rows = first_ref.shape[1] // SIDE
     ch = row_ref.shape[3]
     size = (a_ref.shape[1] - ch) // 2
     nvar = size // REACH
@@ -272,11 +274,18 @@
     low, high = low[0:ch].T, high[0:ch].T
     row_ref[0, 0] = low.astype(bf16)
     row_ref[0, 1] = high.astype(bf16)
-    terms = two_terms(own_ref[0, 0]) + two_terms(own_ref[0, 1])
-    first = [low[0:SIDE].astype(bf16), first_ref[0], high[0:SIDE].astype(bf16)]
-    last = [low[cols - SIDE :].astype(bf16), last_ref[0], high[cols - SIDE :].astype(bf16)]
-    first, last = jnp.concatenate(first, axis=0), jnp.concatenate(last, axis=0)
-    count = first.shape[0]
+    spot = lanes((VG, WIDE)) % SLOT
+    near = (spot >= SIDE - REACH) & (spot < SIDE + REACH)
+    terms = two_terms(jnp.where(near, own_ref[0, 0], roll(own_ref[0, 1], SIDE)))
+    firsts = [low[0:SIDE]] + [first_ref[0, r * SIDE : (r + 1) * SIDE].astype(f32) for r in range(rows)] + [high[0:SIDE]]
+    lasts = [low[cols - SIDE :]] + [last_ref[0, r * SIDE : (r + 1) * SIDE].astype(f32) for r in range(rows)]
+    lasts += [high[cols - SIDE :]]
+    for r in range(rows + 2):
+        w_ref[0, 0, r * SENT : r * SENT + SIDE] = firsts[r]
+    for r in reversed(range(rows + 2)):
+        w_ref[0, 1, r * SENT : r * SENT + SIDE] = lasts[r]
+    count = w_ref.shape[2]
+    first, last = w_ref[0, 0].astype(bf16), w_ref[0, 1].astype(bf16)
     for out, pick in ((outa_ref, jnp.where(lat_even, last, first)), (outb_ref, jnp.where(lat_even, first, last))):
         out[0, 0:count] = pick
         out[0, count:] = jnp.concatenate(terms, axis=0)
@@ -316,7 +325,7 @@
 
 
 def side_kernel(flag_ref, first_ref, last_ref, row_ref, la_ref, lb_ref, w1_ref, w2_ref, w2e_ref, b1_ref, keep_ref,
-                pe_ref, ps0_ref, ps1_ref, sst_ref, pm_ref, cm_ref, pec_ref, outa_ref, outb_ref, e_ref, s_ref, hs_ref, z_ref):
+                pe_ref, ps0_ref, ps1_ref, sst_ref, pm_ref, cm_ref, pec_ref, outa_ref, outb_ref, e_ref, s_ref, hs_ref, z_ref, w_ref):
     levels = row_ref.shape[0]
     cols, ch = row_ref.shape[2:]
     rows = first_ref.shape[1] // SIDE
@@ -332,18 +341,18 @@
     for lv in range(levels):
         a, b = la_ref[lv], lb_ref[lv]
         right, left = jnp.where(lat_even, a, b), jnp.where(lat_even, b, a)
-        count = (rows + 2) * SIDE
-        for k in range(2):
-            st = []
-            for x in (left, right):
-                x = x[count + 2 * k * VG : count + (2 * k + 2) * VG].astype(f32)
-                st.append(x[0:VG] + x[VG:])
-            sst_ref[lv, k] = mix(st[0], st[1])
-        right, left = right[0:count].astype(f32), left[0:count].astype(f32)
+        count = la_ref.shape[1] - 2 * VG
+        st = []
+        for x in (left, right):
+            x = x[count:].astype(f32)
+            st.append(x[0:VG] + x[VG:])
+        sst_ref[lv, 0] = mix(st[0], st[1])
+        sst_ref[lv, 1] = mix(roll(st[0], -SIDE), roll(st[1], -SIDE))
+        w_ref[lv, 0], w_ref[lv, 1] = left[0:count].astype(f32), right[0:count].astype(f32)
         first, last = first_ref[lv].astype(f32), last_ref[lv].astype(f32)
         low, high = row_ref[lv, 0].astype(f32), row_ref[lv, 1].astype(f32)
         for row in range(-1, rows + 1):
-            side = slice((row + 1) * SIDE, (row + 2) * SIDE)
+            far = [w_ref[lv, k, pl.ds((row + 1) * SENT, SIDE), :] for k in range(2)]
             if 0 <= row < rows:
                 own = slice(row * SIDE, (row + 1) * SIDE)
                 mine = first[own], last[own]
@@ -351,7 +360,7 @@
                 x = low if row < 0 else high
                 mine = x[0:SIDE], x[cols - SIDE :]
             start = SIDE + (row + 1) * wide
-            for k, part in enumerate((left[side], mine[0], mine[1], right[side])):
+            for k, part in enumerate((far[0], mine[0], mine[1], far[1])):
                 e_ref[lv, start + k * SIDE : start + (k + 1) * SIDE] = part
         for row in range(rows + 2):
             for b in range(3):
@@ -416,18 +425,20 @@
             pec_ref[lv, k] = mains[row]
         lane8 = lanes((VG, WIDE))
         st = sst_ref[lv, 0], sst_ref[lv, 1]
-        st_lo = two_terms(jnp.where(lane8 < 2 * SLOT, st[0], roll(st[1], 2 * SLOT)))
-        st_hi = two_terms(jnp.where(lane8 >= WIDE - 2 * SLOT, st[0], roll(st[1], -2 * SLOT)))
+
+        def terms_of(x, here):
+            first = x.astype(bf16).astype(f32)
+            return jnp.where(here, first, roll(x - first, WIDE // 2))
+
+        st_lo = terms_of(jnp.where(lane8 < 2 * SLOT, st[0], roll(st[1], 2 * SLOT)), lane8 < WIDE // 2)
+        st_hi = terms_of(jnp.where(lane8 >= WIDE - 2 * SLOT, st[0], roll(st[1], -2 * SLOT)), lane8 >= WIDE // 2)
         side_lo = jnp.where(lane < 2 * SLOT, out[0], jnp.where(lane < 4 * SLOT, roll(out[1], 2 * SLOT), out[3]))
         side_hi = jnp.where(lane >= WIDE - 2 * SLOT, out[0],
                             jnp.where(lane >= WIDE - 4 * SLOT, roll(out[1], -2 * SLOT), out[2]))
-        out_lo = jnp.concatenate([mains[-1], mains[0], mains[1], mains[2], side_lo, mains[3]], axis=0)
-        out_hi = jnp.concatenate([mains[rows - k] for k in range(4)] + [side_hi, mains[rows - 4]], axis=0)
-        main_rows = out_lo.shape[0]
-        outa_ref[lv, 0:main_rows] = jnp.where(even, out_hi, out_lo).astype(bf16)
-        outb_ref[lv, 0:main_rows] = jnp.where(even, out_lo, out_hi).astype(bf16)
-        outa_ref[lv, main_rows:] = jnp.concatenate([jnp.where(even, h, l) for h, l in zip(st_hi, st_lo)], axis=0)
-        outb_ref[lv, main_rows:] = jnp.concatenate([jnp.where(even, l, h) for h, l in zip(st_hi, st_lo)], axis=0)
+        out_lo = jnp.concatenate([mains[k - 1] for k in range(4)] + [side_lo, mains[3][0:VG], st_lo], axis=0)
+        out_hi = jnp.concatenate([mains[rows - k] for k in range(4)] + [side_hi, mains[rows - 4][0:VG], st_hi], axis=0)
+        outa_ref[lv] = jnp.where(even, out_hi, out_lo).astype(bf16)
+        outb_ref[lv] = jnp.where(even, out_lo, out_hi).astype(bf16)
 
 
 def advect_kernel(flag_ref, ps_ref, pe_ref, pm_ref, cm_ref, a_ref, b_ref, st8_ref, halo_ref, sst_ref, own_ref,
@@ -475,8 +486,8 @@
     q0 = {row: st8_ref[0, row] for row in range(rows)}
     for k in range(REACH):
         q0[k - REACH], q0[rows + k] = halo_ref[0, k], halo_ref[0, REACH + k]
-    hlo, hhi = (x[(REACH + 1) * pair + pair :] for x in (lo, hi))
-    hlo, hhi = hlo[0:VG] + hlo[VG:], hhi[0:VG] + hhi[VG:]
+    hlo, hhi = (x[(REACH + 1) * pair + VG :] for x in (lo, hi))
+    hlo, hhi = hlo + roll(hlo, WIDE // 2), hhi + roll(hhi, WIDE // 2)
     last, front = lane >= WIDE - 2 * SLOT, lane < 2 * SLOT
     nil = jnp.zeros((VG, WIDE), f32)
     out_q = {
@@ -622,8 +633,8 @@
 
         return view
 
-    def whole(kernel, steps, ins, outs, scratch, cost, unroll=1):
-        views = [v for _, v in ins] + [v for _, v in outs]
+    def whole(kernel, steps, ins, outs, scratch, cost, unroll=1, scratch_views=()):
+        views = [v for _, v in ins] + [v for _, v in outs] + list(scratch_views)
 
         def run(*refs):
             def one(i, carry):
@@ -701,7 +712,8 @@
         pl.CostEstimate(flops=2 * lev * rows * ext * 9 * ch * ch, bytes_accessed=8 * 2**20, transcendentals=0),
     )
 
-    lat_wire = (lev, (rows + 2) * SIDE + 4 * VG, WIDE)
+    sent_rows = -(-((rows + 1) * SENT + SIDE) // SLOT) * SLOT
+    lat_wire = (lev, sent_rows + 2 * VG, WIDE)
     pair_shape = (lev, 2, cols, ch)
     shapes = [(pair_shape, bf16), (halo_shape, f32), (lat_wire, bf16), (lat_wire, bf16)]
     each = levels()
@@ -710,9 +722,10 @@
         lev,
         [(flags, None)] + [(x, each) for x in (lon_a, lon_b, first, last, own)],
         [(sds(*x), each) for x in shapes],
-        [pltpu.VMEM((nvar * REACH, WIDE), f32)],
+        [pltpu.VMEM((lev, 2, sent_rows, ch), f32), pltpu.VMEM((nvar * REACH, WIDE), f32)],
         2**22,
         PACK_UNROLL,
+        [each],
     )
     lat_a = swap(lat_a, "lat", 0, False)
     lat_b = swap(lat_b, "lat", 1, False)
@@ -737,7 +750,7 @@
     block = SIDE_LEVELS
     parts = PARTS
     count = lev // parts
-    wire = (count, 2 * VG * (REACH + 3), WIDE)
+    wire = (count, 2 * VG * (REACH + 2), WIDE)
     pec_shape = (count,) + pe_shape[1:]
     pm4_shape = (count, 4, 2 * VG, WIDE)
     sst_shape = (count, 2, VG, WIDE)
@@ -758,6 +771,7 @@
                 pltpu.VMEM((block, (rows + 2) * SLOT, 3 * ch), bf16),
                 pltpu.VMEM((block, 2, (half + 1) * SLOT, ch), bf16),
                 pltpu.VMEM((max(WIDE, block * 2 * SLOT), ch), bf16),
+                pltpu.VMEM((block, 2, sent_rows, ch), f32),
             ],
             count * 512 * 12 * ch * ch,
         )

time: 54.7 us -> 53 us (0.969)
  waiting for transfers between devices: 4.66 us -> 2.43 us
    ppermute x8, waiting for transfers between devices: 4.66 us -> 2.43 us  [swap(): lax.ppermute(block, axis, swap_pairs(lax.axis_size(axis), first, closed))]
  transfers between devices with their start and end apart: 8 -> 8, of which waited for: 2 -> 2; matrix products, arithmetic and copies ran while one was open for 0% -> 0% of each run, Pallas kernels for 43% -> 45%
where the time goes in v6:
time: 53 us; the launch traced here: 52.6 us
  Pallas kernels  34 us (64%)
  starting transfers between devices  14.2 us (27%)
  waiting for transfers between devices  2.43 us (5%)
  local copies, waits for them, and re-layouts  1.17 us (2%)
  between operations  0.79 us (1%)
    ppermute x8, starting transfers between devices, swap(): lax.ppermute(block, axis, swap_pairs(lax.axis_size(axis), first, closed))  14.2 us
    pallas_call x1, Pallas kernels, call(): pl.pallas_call(kernel, grid=(steps,), in_specs=ins, out_specs=out_specs,...  13.9 us
    pallas_call x2, Pallas kernels, body(): pl.pallas_call(run, in_specs=[smem if x is flags else vmem for x, _ in in...  8.83 us
    pallas_call x4, Pallas kernels, whole(): pl.pallas_call(run, in_specs=[smem if x is flags else vmem for x, _ in in...  7.52 us
    pallas_call x1, Pallas kernels, body(): pl.pallas_call(rows_kernel, in_specs=[smem] + [pl.BlockSpec(memory_space=...  2.95 us
    ppermute x8, waiting for transfers between devices, swap(): lax.ppermute(block, axis, swap_pairs(lax.axis_size(axis), first, closed))  2.43 us
    unnamed x12, local copies, waits for them, and re-layouts  1.17 us
  transfers between devices with their start and end apart: 8, of which 2 were waited for; matrix products, arithmetic and copies ran while one was open for 0% of the time, Pallas kernels for 45%

profile of v6, /device:TPU:1, one launch (start us, length us, event | category | flops | bytes accessed | tf_op | source)
XLA Modules:
  0.0 52.6 jit_solution(6061223552248955311)
XLA Ops:
  0.6 0.0 copy-start.1
  0.7 0.0 copy-start
  0.7 0.1 pad_add_fusion.flag_ref.refs_0_
  0.7 0.0 copy-start.2
  0.7 1.1 %copy-done.2 = f32[6,8,16,128]{3,2,1,0:T(8,128)S(1)} copy-done((f32[6,8,16,128]{3,2,1,0:T(8,128)S(1)}, f32[6,8,16,128]{3,2,1,0:T(8,128)}, u32[]{:S(2)}) %copy-start.2) | copy-done | bytes 393240
  1.9 0.0 copy-start.3
  1.9 0.0 copy-start.4
  1.9 0.0 copy-start.5
  1.9 3.0 %shard_map.79 = (bf16[8,176,128]{2,1,0:T(8,128)(2,1)S(1)}, bf16[8,176,128]{2,1,0:T(8,128)(2,1)S(1)}) custom-call(s32[3]{0:T(128)S(1)} %pad_add_fusion.flag_ref.refs_0_, bf16[8,128,16,128]{3,2,1,0:T(8,128)(2,1)} %x_hbm.1, f32[6,8,16,128]{3,2,1,0:T(8,128)S(1)} %copy-done.2), custom_call_target="tpu_custom_call" | custom-call | tf_op jit(solution)/shard_map/pallas_call | solution.py:661
  4.9 2.1 %collective-permute-start = (bf16[8,176,128]{2,1,0:T(8,128)(2,1)S(1)}, bf16[8,176,128]{2,1,0:T(8,128)(2,1)S(1)}, u32[]{:S(2)}, u32[]{:S(2)}) collective-permute-start(bf16[8,176,128]{2,1,0:T(8,128)(2,1)S(1)} %get-tuple-element.44), channel_id=1, source_target_pairs={{0,4},{4,0},{8,12},{12,8},{16,20},{20,16},{24,28},{28,24},{1,5},{5... | collective-permute-start | bytes 1081352 | tf_op jit(solution)/shard_map/ppermute | solution.py:43
  7.0 3.3 %collective-permute-start.1 = (bf16[8,176,128]{2,1,0:T(8,128)(2,1)S(1)}, bf16[8,176,128]{2,1,0:T(8,128)(2,1)S(1)}, u32[]{:S(2)}, u32[]{:S(2)}) collective-permute-start(bf16[8,176,128]{2,1,0:T(8,128)(2,1)S(1)} %get-tuple-element.45), channel_id=1, source_target_pairs={{4,8},{8,4},{12,16},{16,12},{20,24},{24,20},{28,0},{0,28},{5,9},{9... | collective-permute-start | bytes 1081352 | tf_op jit(solution)/shard_map/ppermute | solution.py:43
  10.3 0.0 copy-done.1
  10.3 0.0 copy-done.3
  10.3 0.0 copy-done.4
  10.3 0.0 copy-done.5
  10.3 0.7 %shard_map.77 = (bf16[1536,256]{1,0:T(8,128)(2,1)S(1)}, bf16[96,512]{1,0:T(8,128)(2,1)S(1)}, bf16[144,128]{1,0:T(8,128)(2,1)S(1)}, bf16[96,128]{1,0:T(8,128)(2,1...) custom-call(s32[3]{0:T(128)S(1)} %pad_add_fusion.flag_ref.refs_0_, ...), custom_call_target="tpu_custom_call" | custom-call | tf_op jit(solution)/shard_map/pallas_call | solution.py:680
  11.0 0.0 copy-done
  11.0 13.9 %shard_map.78 = (bf16[8,2,128,128]{3,2,1,0:T(8,128)(2,1)S(1)}, bf16[8,2,128,128]{3,2,1,0:T(8,128)(2,1)S(1)}, bf16[8,128,128]{2,1,0:T(8,128)(2,1)S(1)}, bf16[8,12...) custom-call(bf16[8,128,16,128]{3,2,1,0:T(8,128)(2,1)S(1)} %copy-done, ...), custom_call_target="tpu_custom_call" | custom-call | flops 5435817984 | bytes 8388608 | tf_op jit(solution)/shard_map/pallas_call | solution.py:615
  25.0 0.0 collective-permute-done.refs_1_
  25.0 0.0 collective-permute-done.1.refs_2_
  25.0 1.0 %shard_map.80 = (bf16[8,2,128,128]{3,2,1,0:T(8,128)(2,1)S(1)}, f32[8,8,8,128]{3,2,1,0:T(8,128)S(1)}, bf16[8,128,128]{2,1,0:T(8,128)(2,1)S(1)}, bf16[8,128,128]{2,1,0:T(8,128)(2,1)S(1)}) custom-call(s32[3]{0:T(128)S(1)} %pad_add_fusion.flag_ref.refs_0_, bf16[8,176,128]{2,1,0:T(8,128)(2,1)S(1)} %collective-permute-done.refs_1_, ...), custom_call_target="tpu_custom_call" | custom-call | flops 4194304 | bytes 1048576 | tf_op jit(solution)/shard_map/pallas_call | solution.py:649
  26.1 1.3 %collective-permute-start.2 = (bf16[8,128,128]{2,1,0:T(8,128)(2,1)S(1)}, bf16[8,128,128]{2,1,0:T(8,128)(2,1)S(1)}, u32[]{:S(2)}, u32[]{:S(2)}) collective-permute-start(bf16[8,128,128]{2,1,0:T(8,128)(2,1)S(1)} %get-tuple-element.48), channel_id=1, source_target_pairs={{0,1},{1,0},{2,3},{3,2},{4,5},{5,4},{6,7},{7,6},{8,9},{9,8},{10,11... | collective-permute-start | bytes 786440 | tf_op jit(solution)/shard_map/ppermute | solution.py:43
  27.4 3.0 %collective-permute-start.3 = (bf16[8,128,128]{2,1,0:T(8,128)(2,1)S(1)}, bf16[8,128,128]{2,1,0:T(8,128)(2,1)S(1)}, u32[]{:S(2)}, u32[]{:S(2)}) collective-permute-start(bf16[8,128,128]{2,1,0:T(8,128)(2,1)S(1)} %get-tuple-element.49), channel_id=1, source_target_pairs={{1,2},{2,1},{5,6},{6,5},{9,10},{10,9},{13,14},{14,13},{17,18},{18,... | collective-permute-start | bytes 786440 | tf_op jit(solution)/shard_map/ppermute | solution.py:43
  30.4 2.3 %shard_map.81.refs_11_ = f32[8,6,16,128]{3,2,1,0:T(8,128)S(1)} custom-call(bf16[8,2,128,128]{3,2,1,0:T(8,128)(2,1)S(1)} %get-tuple-element.47.refs_0_.refs_3_, bf16[8,2,128,128]{3,2,1,0:T(8,128)(2,1)S(1)} %get-tuple-element.52.refs_1_, bf16[8,2,128,128]{3,2,1,0:T(8,128)(2,1)S(1)} %get-tuple-element.53.refs_2_, bf16[1152,128]{1,0:T(8,128)(2,1)S(1)} %bitcast.9, ...), custom_call_target="tpu_custom_call" | custom-call | flops 679477248 | bytes 1048576 | tf_op jit(solution)/shard_map/pallas_call | solution.py:649
  32.7 0.0 collective-permute-done.2.refs_4_
  32.7 2.4 %collective-permute-done.3.refs_5_ = bf16[8,128,128]{2,1,0:T(8,128)(2,1)S(1)} collective-permute-done((bf16[8,128,128]{2,1,0:T(8,128)(2,1)S(1)}, bf16[8,128,128]{2,1,0:T(8,128)(2,1)S(1)}, u32[]{:S(2)}, u32[]{:S(2)}) %collective-permute-start.3) | collective-permute-done | bytes 262176 | tf_op jit(solution)/shard_map/ppermute | solution.py:43
  35.0 2.1 %shard_map.83 = (f32[4,2,8,128]{3,2,1,0:T(8,128)S(1)}, f32[4,4,16,128]{3,2,1,0:T(8,128)S(1)}, f32[4,4,16,128]{3,2,1,0:T(8,128)S(1)}, f32[4,6,16,128]{3,2,1,0:T(8...) custom-call(s32[3]{0:T(128)S(1)} %pad_add_fusion.flag_ref.refs_0_, ...), custom_call_target="tpu_custom_call" | custom-call | flops 402653184 | bytes 1048576 | tf_op jit(solution)/shard_map/pallas_call | solution.py:649
  37.1 0.1 collective-permute-start.6
  37.2 2.6 %collective-permute-start.7 = (bf16[4,96,128]{2,1,0:T(8,128)(2,1)S(1)}, bf16[4,96,128]{2,1,0:T(8,128)(2,1)S(1)}, u32[]{:S(2)}, u32[]{:S(2)}) collective-permute-start(bf16[4,96,128]{2,1,0:T(8,128)(2,1)S(1)} %get-tuple-element.70), channel_id=1, source_target_pairs={{4,8},{8,4},{12,16},{16,12},{20,24},{24,20},{28,0},{0,28},{5,9},{9... | collective-permute-start | bytes 294920 | tf_op jit(solution)/shard_map/ppermute | solution.py:43
  39.8 2.1 %shard_map.82 = (f32[4,2,8,128]{3,2,1,0:T(8,128)S(1)}, f32[4,4,16,128]{3,2,1,0:T(8,128)S(1)}, f32[4,4,16,128]{3,2,1,0:T(8,128)S(1)}, f32[4,6,16,128]{3,2,1,0:T(8...) custom-call(s32[3]{0:T(128)S(1)} %pad_add_fusion.flag_ref.refs_0_, ...), custom_call_target="tpu_custom_call" | custom-call | flops 402653184 | bytes 1048576 | tf_op jit(solution)/shard_map/pallas_call | solution.py:649
  41.9 0.1 collective-permute-start.4
  42.0 1.7 %collective-permute-start.5 = (bf16[4,96,128]{2,1,0:T(8,128)(2,1)S(1)}, bf16[4,96,128]{2,1,0:T(8,128)(2,1)S(1)}, u32[]{:S(2)}, u32[]{:S(2)}) collective-permute-start(bf16[4,96,128]{2,1,0:T(8,128)(2,1)S(1)} %get-tuple-element.59), channel_id=1, source_target_pairs={{4,8},{8,4},{12,16},{16,12},{20,24},{24,20},{28,0},{0,28},{5,9},{9... | collective-permute-start | bytes 294920 | tf_op jit(solution)/shard_map/ppermute | solution.py:43
  43.7 0.0 collective-permute-done.6.refs_5_
  43.7 0.0 collective-permute-done.7.refs_6_
  43.7 4.4 %shard_map.84 = (f32[12,8,16,128]{3,2,1,0:T(8,128)}, f32[6,8,16,128]{3,2,1,0:T(8,128)}) custom-call(s32[3]{0:T(128)S(1)} %pad_add_fusion.flag_ref.refs_0_, f32[8,16,16,128]{3,2,1,0:T(8,128)S(1)} %get-tuple-element.41.refs_6_.refs_7_.refs_12_.refs_13_.refs_1_, f32[4,6,16,128]{3,2,1,0:T(8,128)S(1)} %get-tuple-element.66.refs_2_, ...), custom_call_target="tpu_custom_call" | custom-call | flops 67108864 | bytes 2097152 | tf_op jit(solution)/shard_map/pallas_call | solution.py:811
  48.1 0.0 collective-permute-done.4.refs_5_
  48.1 0.1 collective-permute-done.5.refs_6_
  48.2 4.4 %shard_map.85 = (f32[12,8,16,128]{3,2,1,0:T(8,128)}, f32[6,8,16,128]{3,2,1,0:T(8,128)}) custom-call(s32[3]{0:T(128)S(1)} %pad_add_fusion.flag_ref.refs_0_, f32[8,16,16,128]{3,2,1,0:T(8,128)S(1)} %get-tuple-element.41.refs_6_.refs_7_.refs_12_.refs_13_.refs_1_, ...), custom_call_target="tpu_custom_call", output_to_operand_aliasing={{0}: (14, {}), {1}: (15, {})} | custom-call | flops 67108864 | bytes 2097152 | tf_op jit(solution)/shard_map/pallas_call | solution.py:811
Async XLA Ops:
  0.6 9.6 %copy-start.1 = (bf16[3,3,128,128]{3,2,1,0:T(8,128)(2,1)S(1)}, bf16[3,3,128,128]{3,2,1,0:T(8,128)(2,1)}, u32[]{:S(2)}) copy-start(bf16[3,3,128,128]{3,2,1,0:T(8,128)(2,1)} %param.7) | copy-start | bytes 884740
  0.7 10.4 %copy-start = (bf16[8,128,16,128]{3,2,1,0:T(8,128)(2,1)S(1)}, bf16[8,128,16,128]{3,2,1,0:T(8,128)(2,1)}, u32[]{:S(2)}) copy-start(bf16[8,128,16,128]{3,2,1,0:T(8,128)(2,1)} %x_hbm.1) | copy-start | bytes 12582916
  0.7 1.1 %copy-start.2 = (f32[6,8,16,128]{3,2,1,0:T(8,128)S(1)}, f32[6,8,16,128]{3,2,1,0:T(8,128)}, u32[]{:S(2)}) copy-start(f32[6,8,16,128]{3,2,1,0:T(8,128)} %st_hbm.1) | copy-start | bytes 1179652
  1.9 8.4 %copy-start.3 = (bf16[3,3,128,12]{2,3,1,0:T(8,128)(2,1)S(1)}, bf16[3,3,128,12]{2,3,1,0:T(8,128)(2,1)}, u32[]{:S(2)}) copy-start(bf16[3,3,128,12]{2,3,1,0:T(8,128)(2,1)} %param.9) | copy-start | bytes 82948
  1.9 8.4 %copy-start.4 = (f32[128]{0:T(128)S(1)}, f32[128]{0:T(128)}, u32[]{:S(2)}) copy-start(f32[128]{0:T(128)} %param.8) | copy-start | bytes 1540
  1.9 8.4 %copy-start.5 = (f32[12]{0:T(128)S(1)}, f32[12]{0:T(128)}, u32[]{:S(2)}) copy-start(f32[12]{0:T(128)} %refs_0_.1) | copy-start | bytes 148
  4.9 20.1 %collective-permute-start = (bf16[8,176,128]{2,1,0:T(8,128)(2,1)S(1)}, bf16[8,176,128]{2,1,0:T(8,128)(2,1)S(1)}, u32[]{:S(2)}, u32[]{:S(2)}) collective-permute-start(bf16[8,176,128]{2,1,0:T(8,128)(2,1)S(1)} %get-tuple-element.44), channel_id=1, source_target_pairs={{0,4},{4,0},{8,12},{12,8},{16,20},{20,16},{24,28},{28,24},{1,5},{5... | collective-permute-start | bytes 1081352 | tf_op jit(solution)/shard_map/ppermute | solution.py:43
  7.0 18.0 %collective-permute-start.1 = (bf16[8,176,128]{2,1,0:T(8,128)(2,1)S(1)}, bf16[8,176,128]{2,1,0:T(8,128)(2,1)S(1)}, u32[]{:S(2)}, u32[]{:S(2)}) collective-permute-start(bf16[8,176,128]{2,1,0:T(8,128)(2,1)S(1)} %get-tuple-element.45), channel_id=1, source_target_pairs={{4,8},{8,4},{12,16},{16,12},{20,24},{24,20},{28,0},{0,28},{5,9},{9... | collective-permute-start | bytes 1081352 | tf_op jit(solution)/shard_map/ppermute | solution.py:43
  26.1 6.6 %collective-permute-start.2 = (bf16[8,128,128]{2,1,0:T(8,128)(2,1)S(1)}, bf16[8,128,128]{2,1,0:T(8,128)(2,1)S(1)}, u32[]{:S(2)}, u32[]{:S(2)}) collective-permute-start(bf16[8,128,128]{2,1,0:T(8,128)(2,1)S(1)} %get-tuple-element.48), channel_id=1, source_target_pairs={{0,1},{1,0},{2,3},{3,2},{4,5},{5,4},{6,7},{7,6},{8,9},{9,8},{10,11... | collective-permute-start | bytes 786440 | tf_op jit(solution)/shard_map/ppermute | solution.py:43
  27.4 7.7 %collective-permute-start.3 = (bf16[8,128,128]{2,1,0:T(8,128)(2,1)S(1)}, bf16[8,128,128]{2,1,0:T(8,128)(2,1)S(1)}, u32[]{:S(2)}, u32[]{:S(2)}) collective-permute-start(bf16[8,128,128]{2,1,0:T(8,128)(2,1)S(1)} %get-tuple-element.49), channel_id=1, source_target_pairs={{1,2},{2,1},{5,6},{6,5},{9,10},{10,9},{13,14},{14,13},{17,18},{18,... | collective-permute-start | bytes 786440 | tf_op jit(solution)/shard_map/ppermute | solution.py:43
  37.1 6.6 %collective-permute-start.6 = (bf16[4,96,128]{2,1,0:T(8,128)(2,1)S(1)}, bf16[4,96,128]{2,1,0:T(8,128)(2,1)S(1)}, u32[]{:S(2)}, u32[]{:S(2)}) collective-permute-start(bf16[4,96,128]{2,1,0:T(8,128)(2,1)S(1)} %get-tuple-element.69), channel_id=1, source_target_pairs={{0,4},{4,0},{8,12},{12,8},{16,20},{20,16},{24,28},{28,24},{1,5},{5... | collective-permute-start | bytes 294920 | tf_op jit(solution)/shard_map/ppermute | solution.py:43
  37.2 6.5 %collective-permute-start.7 = (bf16[4,96,128]{2,1,0:T(8,128)(2,1)S(1)}, bf16[4,96,128]{2,1,0:T(8,128)(2,1)S(1)}, u32[]{:S(2)}, u32[]{:S(2)}) collective-permute-start(bf16[4,96,128]{2,1,0:T(8,128)(2,1)S(1)} %get-tuple-element.70), channel_id=1, source_target_pairs={{4,8},{8,4},{12,16},{16,12},{20,24},{24,20},{28,0},{0,28},{5,9},{9... | collective-permute-start | bytes 294920 | tf_op jit(solution)/shard_map/ppermute | solution.py:43
  41.9 6.2 %collective-permute-start.4 = (bf16[4,96,128]{2,1,0:T(8,128)(2,1)S(1)}, bf16[4,96,128]{2,1,0:T(8,128)(2,1)S(1)}, u32[]{:S(2)}, u32[]{:S(2)}) collective-permute-start(bf16[4,96,128]{2,1,0:T(8,128)(2,1)S(1)} %get-tuple-element.58), channel_id=1, source_target_pairs={{0,4},{4,0},{8,12},{12,8},{16,20},{20,16},{24,28},{28,24},{1,5},{5... | collective-permute-start | bytes 294920 | tf_op jit(solution)/shard_map/ppermute | solution.py:43
  42.0 6.2 %collective-permute-start.5 = (bf16[4,96,128]{2,1,0:T(8,128)(2,1)S(1)}, bf16[4,96,128]{2,1,0:T(8,128)(2,1)S(1)}, u32[]{:S(2)}, u32[]{:S(2)}) collective-permute-start(bf16[4,96,128]{2,1,0:T(8,128)(2,1)S(1)} %get-tuple-element.59), channel_id=1, source_target_pairs={{4,8},{8,4},{12,16},{16,12},{20,24},{24,20},{28,0},{0,28},{5,9},{9... | collective-permute-start | bytes 294920 | tf_op jit(solution)/shard_map/ppermute | solution.py:43

commit v7 on v6

--- a/solution.py
+++ b/solution.py
@@ -15,6 +15,7 @@
 SIDE = 8
 SLOT = 2 * SIDE
 SENT = 6
+FINE = 32
 WIDE = 128
 REACH = 4
 VG = 8
@@ -205,11 +206,6 @@
     step = rows + VG
     x32_ref.reshape(chans, step, cols)[:, 0:rows] = x_ref[0].astype(f32)
 
-    @pl.when(pl.program_id(0) == 0)
-    def _():
-        e_ref[...] = jnp.zeros_like(e_ref)
-        h_ref[...] = jnp.zeros_like(h_ref)
-
     place_in = lax.broadcasted_iota(jnp.int32, (cols, 2 * chans), 0)
     within = (place_in > 0) & (place_in < cols - 1)
 
@@ -254,6 +250,11 @@
         par, base = place(row, rows)
         own[par] = jnp.where(lane // SLOT == base // SLOT, roll(block, base + SIDE), own[par])
     own_ref[0, 0], own_ref[0, 1] = own
+
+
+def main_start(x32_ref, e_ref, s_ref, h_ref):
+    e_ref[...] = jnp.zeros_like(e_ref)
+    h_ref[...] = jnp.zeros_like(h_ref)
 
 
 def pack_kernel(flag_ref, a_ref, b_ref, first_ref, last_ref, own_ref, row_ref, halo_ref, outa_ref, outb_ref, w_ref, x_ref):
@@ -335,9 +336,11 @@
     wide = 2 * SLOT
     lane = lanes((2 * VG, WIDE))
     begin, end = lane < SLOT, lane >= WIDE - SLOT
-    e_ref[...] = jnp.zeros_like(e_ref)
-    hs_ref[...] = jnp.zeros_like(hs_ref)
-    z_ref[...] = jnp.zeros_like(z_ref)
+    if z_ref.shape[0] > 2 * levels * SLOT:
+        z_ref[...] = jnp.zeros_like(z_ref)
+    for lv in range(levels):
+        hs_ref[lv, 0, half * SLOT :] = jnp.zeros((SLOT, ch), bf16)
+        hs_ref[lv, 1, 0:SLOT] = jnp.zeros((SLOT, ch), bf16)
     for lv in range(levels):
         a, b = la_ref[lv], lb_ref[lv]
         right, left = jnp.where(lat_even, a, b), jnp.where(lat_even, b, a)
@@ -435,10 +438,13 @@
         side_lo = jnp.where(lane < 2 * SLOT, out[0], jnp.where(lane < 4 * SLOT, roll(out[1], 2 * SLOT), out[3]))
         side_hi = jnp.where(lane >= WIDE - 2 * SLOT, out[0],
                             jnp.where(lane >= WIDE - 4 * SLOT, roll(out[1], -2 * SLOT), out[2]))
-        out_lo = jnp.concatenate([mains[k - 1] for k in range(4)] + [side_lo, mains[3][0:VG], st_lo], axis=0)
-        out_hi = jnp.concatenate([mains[rows - k] for k in range(4)] + [side_hi, mains[rows - 4][0:VG], st_hi], axis=0)
-        outa_ref[lv] = jnp.where(even, out_hi, out_lo).astype(bf16)
-        outb_ref[lv] = jnp.where(even, out_lo, out_hi).astype(bf16)
+        out_lo = [mains[-1], mains[0], side_lo, mains[1], mains[2], mains[3][0:VG], st_lo]
+        out_hi = [mains[rows], mains[rows - 1], side_hi, mains[rows - 2], mains[rows - 3], mains[rows - 4][0:VG], st_hi]
+        out_lo, out_hi = jnp.concatenate(out_lo, axis=0), jnp.concatenate(out_hi, axis=0)
+        for ref, x in ((outa_ref, jnp.where(even, out_hi, out_lo)), (outb_ref, jnp.where(even, out_lo, out_hi))):
+            terms = two_terms(x)
+            ref[lv, 0 : x.shape[0]] = terms[0]
+            ref[lv, x.shape[0] :] = terms[1][0:FINE]
 
 
 def advect_kernel(flag_ref, ps_ref, pe_ref, pm_ref, cm_ref, a_ref, b_ref, st8_ref, halo_ref, sst_ref, own_ref,
@@ -454,7 +460,13 @@
     def halos(xa, xb):
         return jnp.where(even, xb, xa), jnp.where(even, xa, xb)
 
-    lo, hi = halos(a_ref[0].astype(f32), b_ref[0].astype(f32))
+    coarse = a_ref.shape[1] - FINE
+
+    def both_terms(ref):
+        x = ref[0].astype(f32)
+        return jnp.concatenate([x[0:FINE] + x[coarse:], x[FINE:coarse]], axis=0)
+
+    lo, hi = halos(both_terms(a_ref), both_terms(b_ref))
     main = {}
     for row in range(2, rows - 2):
         k, base = place(row, rows)
@@ -462,10 +474,11 @@
     for k, row in enumerate((-1, 0, 1, rows - 2, rows - 1, rows)):
         main[row] = pe_ref[0, k]
     for k in range(REACH + 1):
-        there = slice(k * pair, (k + 1) * pair) if k < REACH else slice((k + 1) * pair, (k + 2) * pair)
+        first = k * pair if k < 2 else (k + 1) * pair
+        there = slice(first, first + pair)
         for got, row in ((lo, -k), (hi, rows - 1 + k)):
             main[row] = main[row] + got[there] if row in main else got[there]
-    slo, shi = (got[REACH * pair : (REACH + 1) * pair] for got in (lo, hi))
+    slo, shi = (got[2 * pair : 3 * pair] for got in (lo, hi))
     zero = jnp.zeros((pair, WIDE), f32)
     last, front = lane16 >= WIDE - 2 * SLOT, lane16 < 2 * SLOT
     side = {
@@ -633,7 +646,7 @@
 
         return view
 
-    def whole(kernel, steps, ins, outs, scratch, cost, unroll=1, scratch_views=()):
+    def whole(kernel, steps, ins, outs, scratch, cost, unroll=1, scratch_views=(), first=None):
         views = [v for _, v in ins] + [v for _, v in outs] + list(scratch_views)
 
         def run(*refs):
@@ -641,6 +654,8 @@
                 kernel(*[v(r, i) if v else r for v, r in zip(views, refs)], *refs[len(views) :])
                 return carry
 
+            if first:
+                first(*refs[len(views) :])
             if steps == 1:
                 one(0, 0)
             else:
@@ -696,20 +711,20 @@
     own_shape = (lev, 2, VG, WIDE)
     halo_shape = (lev, 2 * REACH, VG, WIDE)
     shapes = [(g_pair, bf16), (g_pair, bf16), (cut, bf16), (cut, bf16), (st8_shape, f32), (own_shape, f32), (ps_shape, f32)]
-    g_lo, g_hi, first, last, st8, own, ps = call(
+    each = levels()
+    g_lo, g_hi, first, last, st8, own, ps = whole(
         main_kernel,
         lev,
-        [per_level(hidden_in.shape), var_level(state.shape), full(w1_pair.shape), full(w2_pair.shape), full((1, 2 * ch))],
-        [sds(*x) for x in shapes],
-        [per_level(x[0]) for x in shapes],
+        [(hidden_in, each), (state, lambda ref, i: ref.at[:, pl.ds(i, 1)]), (w1_pair, None), (w2_pair, None), (b1_pair, None)],
+        [(sds(*x), each) for x in shapes],
         [
             pltpu.VMEM((ch * (rows + VG), cols), f32),
             pltpu.VMEM((rows * (cols + SLOT), ch), f32),
             pltpu.VMEM((rows, cols, 3 * ch), bf16),
             pltpu.VMEM((rows + 2, cols, ch), bf16),
         ],
-        (hidden_in, state, w1_pair, w2_pair, b1_pair),
-        pl.CostEstimate(flops=2 * lev * rows * ext * 9 * ch * ch, bytes_accessed=8 * 2**20, transcendentals=0),
+        2 * lev * rows * ext * 9 * ch * ch,
+        first=main_start,
     )
 
     sent_rows = -(-((rows + 1) * SENT + SIDE) // SLOT) * SLOT
@@ -750,7 +765,7 @@
     block = SIDE_LEVELS
     parts = PARTS
     count = lev // parts
-    wire = (count, 2 * VG * (REACH + 2), WIDE)
+    wire = (count, 2 * VG * (REACH + 2) + FINE, WIDE)
     pec_shape = (count,) + pe_shape[1:]
     pm4_shape = (count, 4, 2 * VG, WIDE)
     sst_shape = (count, 2, VG, WIDE)

time: 53 us -> 53.4 us (level)
  waiting for transfers between devices: 2.43 us -> 3.07 us
    pallas_call x1 -> x0, Pallas kernels: 13.9 us -> none  [call(): pl.pallas_call(kernel, grid=(steps,), in_specs=ins, out_specs=out_specs,...]
    pallas_call x4 -> x5, Pallas kernels: 7.52 us -> 21.3 us  [whole(): pl.pallas_call(run, in_specs=[smem if x is flags else vmem for x, _ in in...]
    ppermute x8, waiting for transfers between devices: 2.43 us -> 3.07 us  [swap(): lax.ppermute(block, axis, swap_pairs(lax.axis_size(axis), first, closed))]
  transfers between devices with their start and end apart: 8 -> 8, of which waited for: 2 -> 2; matrix products, arithmetic and copies ran while one was open for 0% -> 0% of each run, Pallas kernels for 45% -> 44%
where the time goes in v7:
time: 53.4 us; the launch traced here: 53.1 us
  Pallas kernels  33.9 us (63%)
  starting transfers between devices  14.2 us (27%)
  waiting for transfers between devices  3.07 us (6%)
  local copies, waits for them, and re-layouts  1.17 us (2%)
  between operations  0.79 us (1%)
    pallas_call x5, Pallas kernels, whole(): pl.pallas_call(run, in_specs=[smem if x is flags else vmem for x, _ in in...  21.3 us
    ppermute x8, starting transfers between devices, swap(): lax.ppermute(block, axis, swap_pairs(lax.axis_size(axis), first, closed))  14.2 us
    pallas_call x2, Pallas kernels, body(): pl.pallas_call(run, in_specs=[smem if x is flags else vmem for x, _ in in...  8.86 us
    ppermute x8, waiting for transfers between devices, swap(): lax.ppermute(block, axis, swap_pairs(lax.axis_size(axis), first, closed))  3.07 us
    pallas_call x1, Pallas kernels, body(): pl.pallas_call(rows_kernel, in_specs=[smem] + [pl.BlockSpec(memory_space=...  2.95 us
    unnamed x12, local copies, waits for them, and re-layouts  1.17 us
  transfers between devices with their start and end apart: 8, of which 2 were waited for; matrix products, arithmetic and copies ran while one was open for 0% of the time, Pallas kernels for 44%

profile of v7, /device:TPU:1, one launch (start us, length us, event | category | flops | bytes accessed | tf_op | source)
XLA Modules:
  0.0 53.1 jit_solution(8327629297952132688)
XLA Ops:
  0.6 0.0 copy-start.1
  0.7 0.0 copy-start
  0.7 0.1 pad_add_fusion.flag_ref.refs_0_
  0.7 0.0 copy-start.2
  0.7 1.1 %copy-done.2 = f32[6,8,16,128]{3,2,1,0:T(8,128)S(1)} copy-done((f32[6,8,16,128]{3,2,1,0:T(8,128)S(1)}, f32[6,8,16,128]{3,2,1,0:T(8,128)}, u32[]{:S(2)}) %copy-start.2) | copy-done | bytes 393240
  1.9 0.0 copy-start.3
  1.9 0.0 copy-start.4
  1.9 0.0 copy-start.5
  1.9 3.0 %shard_map.79 = (bf16[8,176,128]{2,1,0:T(8,128)(2,1)S(1)}, bf16[8,176,128]{2,1,0:T(8,128)(2,1)S(1)}) custom-call(s32[3]{0:T(128)S(1)} %pad_add_fusion.flag_ref.refs_0_, bf16[8,128,16,128]{3,2,1,0:T(8,128)(2,1)} %x_hbm.1, f32[6,8,16,128]{3,2,1,0:T(8,128)S(1)} %copy-done.2), custom_call_target="tpu_custom_call" | custom-call | tf_op jit(solution)/shard_map/pallas_call | solution.py:676
  4.9 2.1 %collective-permute-start = (bf16[8,176,128]{2,1,0:T(8,128)(2,1)S(1)}, bf16[8,176,128]{2,1,0:T(8,128)(2,1)S(1)}, u32[]{:S(2)}, u32[]{:S(2)}) collective-permute-start(bf16[8,176,128]{2,1,0:T(8,128)(2,1)S(1)} %get-tuple-element.44), channel_id=1, source_target_pairs={{0,4},{4,0},{8,12},{12,8},{16,20},{20,16},{24,28},{28,24},{1,5},{5... | collective-permute-start | bytes 1081352 | tf_op jit(solution)/shard_map/ppermute | solution.py:44
  7.0 3.3 %collective-permute-start.1 = (bf16[8,176,128]{2,1,0:T(8,128)(2,1)S(1)}, bf16[8,176,128]{2,1,0:T(8,128)(2,1)S(1)}, u32[]{:S(2)}, u32[]{:S(2)}) collective-permute-start(bf16[8,176,128]{2,1,0:T(8,128)(2,1)S(1)} %get-tuple-element.45), channel_id=1, source_target_pairs={{4,8},{8,4},{12,16},{16,12},{20,24},{24,20},{28,0},{0,28},{5,9},{9... | collective-permute-start | bytes 1081352 | tf_op jit(solution)/shard_map/ppermute | solution.py:44
  10.3 0.0 copy-done.1
  10.3 0.0 copy-done.3
  10.3 0.0 copy-done.4
  10.3 0.0 copy-done.5
  10.3 0.7 %shard_map.77 = (bf16[1536,256]{1,0:T(8,128)(2,1)S(1)}, bf16[96,512]{1,0:T(8,128)(2,1)S(1)}, bf16[144,128]{1,0:T(8,128)(2,1)S(1)}, bf16[96,128]{1,0:T(8,128)(2,1...) custom-call(s32[3]{0:T(128)S(1)} %pad_add_fusion.flag_ref.refs_0_, ...), custom_call_target="tpu_custom_call" | custom-call | tf_op jit(solution)/shard_map/pallas_call | solution.py:695
  11.0 0.0 copy-done
  11.0 13.9 %shard_map.78 = (bf16[8,2,128,128]{3,2,1,0:T(8,128)(2,1)S(1)}, bf16[8,2,128,128]{3,2,1,0:T(8,128)(2,1)S(1)}, bf16[8,128,128]{2,1,0:T(8,128)(2,1)S(1)}, bf16[8,12...) custom-call(bf16[8,128,16,128]{3,2,1,0:T(8,128)(2,1)S(1)} %copy-done, ...), custom_call_target="tpu_custom_call" | custom-call | flops 5435817984 | bytes 1048576 | tf_op jit(solution)/shard_map/pallas_call | solution.py:664
  24.9 0.0 collective-permute-done.refs_1_
  24.9 0.0 collective-permute-done.1.refs_2_
  24.9 1.0 %shard_map.80 = (bf16[8,2,128,128]{3,2,1,0:T(8,128)(2,1)S(1)}, f32[8,8,8,128]{3,2,1,0:T(8,128)S(1)}, bf16[8,128,128]{2,1,0:T(8,128)(2,1)S(1)}, bf16[8,128,128]{2,1,0:T(8,128)(2,1)S(1)}) custom-call(s32[3]{0:T(128)S(1)} %pad_add_fusion.flag_ref.refs_0_, bf16[8,176,128]{2,1,0:T(8,128)(2,1)S(1)} %collective-permute-done.refs_1_, ...), custom_call_target="tpu_custom_call" | custom-call | flops 4194304 | bytes 1048576 | tf_op jit(solution)/shard_map/pallas_call | solution.py:664
  26.0 1.3 %collective-permute-start.2 = (bf16[8,128,128]{2,1,0:T(8,128)(2,1)S(1)}, bf16[8,128,128]{2,1,0:T(8,128)(2,1)S(1)}, u32[]{:S(2)}, u32[]{:S(2)}) collective-permute-start(bf16[8,128,128]{2,1,0:T(8,128)(2,1)S(1)} %get-tuple-element.48), channel_id=1, source_target_pairs={{0,1},{1,0},{2,3},{3,2},{4,5},{5,4},{6,7},{7,6},{8,9},{9,8},{10,11... | collective-permute-start | bytes 786440 | tf_op jit(solution)/shard_map/ppermute | solution.py:44
  27.3 3.0 %collective-permute-start.3 = (bf16[8,128,128]{2,1,0:T(8,128)(2,1)S(1)}, bf16[8,128,128]{2,1,0:T(8,128)(2,1)S(1)}, u32[]{:S(2)}, u32[]{:S(2)}) collective-permute-start(bf16[8,128,128]{2,1,0:T(8,128)(2,1)S(1)} %get-tuple-element.49), channel_id=1, source_target_pairs={{1,2},{2,1},{5,6},{6,5},{9,10},{10,9},{13,14},{14,13},{17,18},{18,... | collective-permute-start | bytes 786440 | tf_op jit(solution)/shard_map/ppermute | solution.py:44
  30.3 2.3 %shard_map.81.refs_11_ = f32[8,6,16,128]{3,2,1,0:T(8,128)S(1)} custom-call(bf16[8,2,128,128]{3,2,1,0:T(8,128)(2,1)S(1)} %get-tuple-element.47.refs_0_.refs_3_, bf16[8,2,128,128]{3,2,1,0:T(8,128)(2,1)S(1)} %get-tuple-element.52.refs_1_, bf16[8,2,128,128]{3,2,1,0:T(8,128)(2,1)S(1)} %get-tuple-element.53.refs_2_, bf16[1152,128]{1,0:T(8,128)(2,1)S(1)} %bitcast.9, ...), custom_call_target="tpu_custom_call" | custom-call | flops 679477248 | bytes 1048576 | tf_op jit(solution)/shard_map/pallas_call | solution.py:664
  32.6 0.0 collective-permute-done.2.refs_4_
  32.6 2.4 %collective-permute-done.3.refs_5_ = bf16[8,128,128]{2,1,0:T(8,128)(2,1)S(1)} collective-permute-done((bf16[8,128,128]{2,1,0:T(8,128)(2,1)S(1)}, bf16[8,128,128]{2,1,0:T(8,128)(2,1)S(1)}, u32[]{:S(2)}, u32[]{:S(2)}) %collective-permute-start.3) | collective-permute-done | bytes 262176 | tf_op jit(solution)/shard_map/ppermute | solution.py:44
  35.0 2.1 %shard_map.83 = (f32[4,2,8,128]{3,2,1,0:T(8,128)S(1)}, f32[4,4,16,128]{3,2,1,0:T(8,128)S(1)}, f32[4,4,16,128]{3,2,1,0:T(8,128)S(1)}, f32[4,6,16,128]{3,2,1,0:T(8...) custom-call(s32[3]{0:T(128)S(1)} %pad_add_fusion.flag_ref.refs_0_, ...), custom_call_target="tpu_custom_call" | custom-call | flops 402653184 | bytes 1048576 | tf_op jit(solution)/shard_map/pallas_call | solution.py:664
  37.0 0.1 collective-permute-start.6
  37.1 2.6 %collective-permute-start.7 = (bf16[4,128,128]{2,1,0:T(8,128)(2,1)S(1)}, bf16[4,128,128]{2,1,0:T(8,128)(2,1)S(1)}, u32[]{:S(2)}, u32[]{:S(2)}) collective-permute-start(bf16[4,128,128]{2,1,0:T(8,128)(2,1)S(1)} %get-tuple-element.70), channel_id=1, source_target_pairs={{4,8},{8,4},{12,16},{16,12},{20,24},{24,20},{28,0},{0,28},{5,9},{9... | collective-permute-start | bytes 393224 | tf_op jit(solution)/shard_map/ppermute | solution.py:44
  39.8 2.1 %shard_map.82 = (f32[4,2,8,128]{3,2,1,0:T(8,128)S(1)}, f32[4,4,16,128]{3,2,1,0:T(8,128)S(1)}, f32[4,4,16,128]{3,2,1,0:T(8,128)S(1)}, f32[4,6,16,128]{3,2,1,0:T(8...) custom-call(s32[3]{0:T(128)S(1)} %pad_add_fusion.flag_ref.refs_0_, ...), custom_call_target="tpu_custom_call" | custom-call | flops 402653184 | bytes 1048576 | tf_op jit(solution)/shard_map/pallas_call | solution.py:664
  41.8 0.1 collective-permute-start.4
  41.9 1.7 %collective-permute-start.5 = (bf16[4,128,128]{2,1,0:T(8,128)(2,1)S(1)}, bf16[4,128,128]{2,1,0:T(8,128)(2,1)S(1)}, u32[]{:S(2)}, u32[]{:S(2)}) collective-permute-start(bf16[4,128,128]{2,1,0:T(8,128)(2,1)S(1)} %get-tuple-element.59), channel_id=1, source_target_pairs={{4,8},{8,4},{12,16},{16,12},{20,24},{24,20},{28,0},{0,28},{5,9},{9... | collective-permute-start | bytes 393224 | tf_op jit(solution)/shard_map/ppermute | solution.py:44
  43.6 0.0 collective-permute-done.6.refs_5_
  43.6 0.7 %collective-permute-done.7.refs_6_ = bf16[4,128,128]{2,1,0:T(8,128)(2,1)S(1)} collective-permute-done((bf16[4,128,128]{2,1,0:T(8,128)(2,1)S(1)}, bf16[4,128,128]{2,1,0:T(8,128)(2,1)S(1)}, u32[]{:S(2)}, u32[]{:S(2)}) %collective-permute-start.7) | collective-permute-done | bytes 131104 | tf_op jit(solution)/shard_map/ppermute | solution.py:44
  44.2 4.4 %shard_map.84 = (f32[12,8,16,128]{3,2,1,0:T(8,128)}, f32[6,8,16,128]{3,2,1,0:T(8,128)}) custom-call(s32[3]{0:T(128)S(1)} %pad_add_fusion.flag_ref.refs_0_, f32[8,16,16,128]{3,2,1,0:T(8,128)S(1)} %get-tuple-element.41.refs_6_.refs_7_.refs_12_.refs_13_.refs_1_, f32[4,6,16,128]{3,2,1,0:T(8,128)S(1)} %get-tuple-element.66.refs_2_, ...), custom_call_target="tpu_custom_call" | custom-call | flops 67108864 | bytes 2097152 | tf_op jit(solution)/shard_map/pallas_call | solution.py:826
  48.7 0.0 collective-permute-done.4.refs_5_
  48.7 0.0 collective-permute-done.5.refs_6_
  48.7 4.4 %shard_map.85 = (f32[12,8,16,128]{3,2,1,0:T(8,128)}, f32[6,8,16,128]{3,2,1,0:T(8,128)}) custom-call(s32[3]{0:T(128)S(1)} %pad_add_fusion.flag_ref.refs_0_, f32[8,16,16,128]{3,2,1,0:T(8,128)S(1)} %get-tuple-element.41.refs_6_.refs_7_.refs_12_.refs_13_.refs_1_, ...), custom_call_target="tpu_custom_call", output_to_operand_aliasing={{0}: (14, {}), {1}: (15, {})} | custom-call | flops 67108864 | bytes 2097152 | tf_op jit(solution)/shard_map/pallas_call | solution.py:826
Async XLA Ops:
  0.6 9.6 %copy-start.1 = (bf16[3,3,128,128]{3,2,1,0:T(8,128)(2,1)S(1)}, bf16[3,3,128,128]{3,2,1,0:T(8,128)(2,1)}, u32[]{:S(2)}) copy-start(bf16[3,3,128,128]{3,2,1,0:T(8,128)(2,1)} %param.7) | copy-start | bytes 884740
  0.7 10.4 %copy-start = (bf16[8,128,16,128]{3,2,1,0:T(8,128)(2,1)S(1)}, bf16[8,128,16,128]{3,2,1,0:T(8,128)(2,1)}, u32[]{:S(2)}) copy-start(bf16[8,128,16,128]{3,2,1,0:T(8,128)(2,1)} %x_hbm.1) | copy-start | bytes 12582916
  0.7 1.1 %copy-start.2 = (f32[6,8,16,128]{3,2,1,0:T(8,128)S(1)}, f32[6,8,16,128]{3,2,1,0:T(8,128)}, u32[]{:S(2)}) copy-start(f32[6,8,16,128]{3,2,1,0:T(8,128)} %st_hbm.1) | copy-start | bytes 1179652
  1.9 8.4 %copy-start.3 = (bf16[3,3,128,12]{2,3,1,0:T(8,128)(2,1)S(1)}, bf16[3,3,128,12]{2,3,1,0:T(8,128)(2,1)}, u32[]{:S(2)}) copy-start(bf16[3,3,128,12]{2,3,1,0:T(8,128)(2,1)} %param.9) | copy-start | bytes 82948
  1.9 8.4 %copy-start.4 = (f32[128]{0:T(128)S(1)}, f32[128]{0:T(128)}, u32[]{:S(2)}) copy-start(f32[128]{0:T(128)} %param.8) | copy-start | bytes 1540
  1.9 8.4 %copy-start.5 = (f32[12]{0:T(128)S(1)}, f32[12]{0:T(128)}, u32[]{:S(2)}) copy-start(f32[12]{0:T(128)} %refs_0_.2) | copy-start | bytes 148
  4.9 20.0 %collective-permute-start = (bf16[8,176,128]{2,1,0:T(8,128)(2,1)S(1)}, bf16[8,176,128]{2,1,0:T(8,128)(2,1)S(1)}, u32[]{:S(2)}, u32[]{:S(2)}) collective-permute-start(bf16[8,176,128]{2,1,0:T(8,128)(2,1)S(1)} %get-tuple-element.44), channel_id=1, source_target_pairs={{0,4},{4,0},{8,12},{12,8},{16,20},{20,16},{24,28},{28,24},{1,5},{5... | collective-permute-start | bytes 1081352 | tf_op jit(solution)/shard_map/ppermute | solution.py:44
  7.0 17.9 %collective-permute-start.1 = (bf16[8,176,128]{2,1,0:T(8,128)(2,1)S(1)}, bf16[8,176,128]{2,1,0:T(8,128)(2,1)S(1)}, u32[]{:S(2)}, u32[]{:S(2)}) collective-permute-start(bf16[8,176,128]{2,1,0:T(8,128)(2,1)S(1)} %get-tuple-element.45), channel_id=1, source_target_pairs={{4,8},{8,4},{12,16},{16,12},{20,24},{24,20},{28,0},{0,28},{5,9},{9... | collective-permute-start | bytes 1081352 | tf_op jit(solution)/shard_map/ppermute | solution.py:44
  26.0 6.6 %collective-permute-start.2 = (bf16[8,128,128]{2,1,0:T(8,128)(2,1)S(1)}, bf16[8,128,128]{2,1,0:T(8,128)(2,1)S(1)}, u32[]{:S(2)}, u32[]{:S(2)}) collective-permute-start(bf16[8,128,128]{2,1,0:T(8,128)(2,1)S(1)} %get-tuple-element.48), channel_id=1, source_target_pairs={{0,1},{1,0},{2,3},{3,2},{4,5},{5,4},{6,7},{7,6},{8,9},{9,8},{10,11... | collective-permute-start | bytes 786440 | tf_op jit(solution)/shard_map/ppermute | solution.py:44
  27.3 7.7 %collective-permute-start.3 = (bf16[8,128,128]{2,1,0:T(8,128)(2,1)S(1)}, bf16[8,128,128]{2,1,0:T(8,128)(2,1)S(1)}, u32[]{:S(2)}, u32[]{:S(2)}) collective-permute-start(bf16[8,128,128]{2,1,0:T(8,128)(2,1)S(1)} %get-tuple-element.49), channel_id=1, source_target_pairs={{1,2},{2,1},{5,6},{6,5},{9,10},{10,9},{13,14},{14,13},{17,18},{18,... | collective-permute-start | bytes 786440 | tf_op jit(solution)/shard_map/ppermute | solution.py:44
  37.0 6.5 %collective-permute-start.6 = (bf16[4,128,128]{2,1,0:T(8,128)(2,1)S(1)}, bf16[4,128,128]{2,1,0:T(8,128)(2,1)S(1)}, u32[]{:S(2)}, u32[]{:S(2)}) collective-permute-start(bf16[4,128,128]{2,1,0:T(8,128)(2,1)S(1)} %get-tuple-element.69), channel_id=1, source_target_pairs={{0,4},{4,0},{8,12},{12,8},{16,20},{20,16},{24,28},{28,24},{1,5},{5... | collective-permute-start | bytes 393224 | tf_op jit(solution)/shard_map/ppermute | solution.py:44
  37.1 7.1 %collective-permute-start.7 = (bf16[4,128,128]{2,1,0:T(8,128)(2,1)S(1)}, bf16[4,128,128]{2,1,0:T(8,128)(2,1)S(1)}, u32[]{:S(2)}, u32[]{:S(2)}) collective-permute-start(bf16[4,128,128]{2,1,0:T(8,128)(2,1)S(1)} %get-tuple-element.70), channel_id=1, source_target_pairs={{4,8},{8,4},{12,16},{16,12},{20,24},{24,20},{28,0},{0,28},{5,9},{9... | collective-permute-start | bytes 393224 | tf_op jit(solution)/shard_map/ppermute | solution.py:44
  41.8 6.9 %collective-permute-start.4 = (bf16[4,128,128]{2,1,0:T(8,128)(2,1)S(1)}, bf16[4,128,128]{2,1,0:T(8,128)(2,1)S(1)}, u32[]{:S(2)}, u32[]{:S(2)}) collective-permute-start(bf16[4,128,128]{2,1,0:T(8,128)(2,1)S(1)} %get-tuple-element.58), channel_id=1, source_target_pairs={{0,4},{4,0},{8,12},{12,8},{16,20},{20,16},{24,28},{28,24},{1,5},{5... | collective-permute-start | bytes 393224 | tf_op jit(solution)/shard_map/ppermute | solution.py:44
  41.9 6.8 %collective-permute-start.5 = (bf16[4,128,128]{2,1,0:T(8,128)(2,1)S(1)}, bf16[4,128,128]{2,1,0:T(8,128)(2,1)S(1)}, u32[]{:S(2)}, u32[]{:S(2)}) collective-permute-start(bf16[4,128,128]{2,1,0:T(8,128)(2,1)S(1)} %get-tuple-element.59), channel_id=1, source_target_pairs={{4,8},{8,4},{12,16},{16,12},{20,24},{24,20},{28,0},{0,28},{5,9},{9... | collective-permute-start | bytes 393224 | tf_op jit(solution)/shard_map/ppermute | solution.py:44

commit v8 on v7

--- a/solution.py
+++ b/solution.py
@@ -99,6 +99,11 @@
     return [first, (x - first.astype(f32)).astype(bf16)]
 
 
+def two_terms_stacked(x):
+    first = x.astype(bf16).astype(f32)
+    return jnp.concatenate([first, x - first], axis=0).astype(bf16)
+
+
 def nt(lhs, rhs):
     return lax.dot_general(lhs, rhs, (((1,), (1,)), ((), ())), preferred_element_type=f32)
 
@@ -140,8 +145,8 @@
             x32_ref[n * REACH : (n + 1) * REACH] = st_ref[n, lv, 0:REACH]
             x32_ref[size + n * REACH : size + (n + 1) * REACH] = st_ref[n, lv, rows - REACH :]
         lo, hi = x32_ref[0:size], x32_ref[size : 2 * size]
-        outa_ref[lv, ch:] = jnp.concatenate(two_terms(jnp.where(even, hi, lo)), axis=0)
-        outb_ref[lv, ch:] = jnp.concatenate(two_terms(jnp.where(even, lo, hi)), axis=0)
+        outa_ref[lv, ch:] = two_terms_stacked(jnp.where(even, hi, lo))
+        outb_ref[lv, ch:] = two_terms_stacked(jnp.where(even, lo, hi))
         return carry
 
     lax.fori_loop(0, levels, one, 0)
@@ -269,7 +274,7 @@
     low, high = jnp.where(even, got_b, got_a), jnp.where(even, got_a, got_b)
     halo_ref[...] = jnp.zeros_like(halo_ref)
     for k, x in enumerate((low, high)):
-        x_ref[...] = x[ch : ch + size] + x[ch + size :]
+        x_ref[0:size] = x[ch : ch + size] + x[ch + size :]
         for r in range(REACH):
             halo_ref[0, k * REACH + r, 0:nvar] = x_ref[pl.ds(r, nvar, stride=REACH), :]
     low, high = low[0:ch].T, high[0:ch].T
@@ -277,9 +282,10 @@
     row_ref[0, 1] = high.astype(bf16)
     spot = lanes((VG, WIDE)) % SLOT
     near = (spot >= SIDE - REACH) & (spot < SIDE + REACH)
-    terms = two_terms(jnp.where(near, own_ref[0, 0], roll(own_ref[0, 1], SIDE)))
-    firsts = [low[0:SIDE]] + [first_ref[0, r * SIDE : (r + 1) * SIDE].astype(f32) for r in range(rows)] + [high[0:SIDE]]
-    lasts = [low[cols - SIDE :]] + [last_ref[0, r * SIDE : (r + 1) * SIDE].astype(f32) for r in range(rows)]
+    terms = two_terms_stacked(jnp.where(near, own_ref[0, 0], roll(own_ref[0, 1], SIDE)))
+    first, last = first_ref[0].astype(f32), last_ref[0].astype(f32)
+    firsts = [low[0:SIDE]] + [first[r * SIDE : (r + 1) * SIDE] for r in range(rows)] + [high[0:SIDE]]
+    lasts = [low[cols - SIDE :]] + [last[r * SIDE : (r + 1) * SIDE] for r in range(rows)]
     lasts += [high[cols - SIDE :]]
     for r in range(rows + 2):
         w_ref[0, 0, r * SENT : r * SENT + SIDE] = firsts[r]
@@ -289,7 +295,7 @@
     first, last = w_ref[0, 0].astype(bf16), w_ref[0, 1].astype(bf16)
     for out, pick in ((outa_ref, jnp.where(lat_even, last, first)), (outb_ref, jnp.where(lat_even, first, last))):
         out[0, 0:count] = pick
-        out[0, count:] = jnp.concatenate(terms, axis=0)
+        out[0, count:] = terms
 
 
 def edge_kernel(row_ref, g0_ref, g1_ref, w1_ref, w2_ref, b1_ref, ps0_ref, ps1_ref, pe_ref, e_ref, s_ref, h_ref):
@@ -737,7 +743,7 @@
         lev,
         [(flags, None)] + [(x, each) for x in (lon_a, lon_b, first, last, own)],
         [(sds(*x), each) for x in shapes],
-        [pltpu.VMEM((lev, 2, sent_rows, ch), f32), pltpu.VMEM((nvar * REACH, WIDE), f32)],
+        [pltpu.VMEM((lev, 2, sent_rows, ch), f32), pltpu.VMEM((VG * REACH, WIDE), f32)],
         2**22,
         PACK_UNROLL,
         [each],

time: 53.4 us -> 53.4 us (level)
  no operation moved by 1% of the time
where the time goes in v8:
time: 53.4 us; the launch traced here: 53.1 us
  Pallas kernels  33.9 us (63%)
  starting transfers between devices  14.2 us (27%)
  waiting for transfers between devices  3.08 us (6%)
  local copies, waits for them, and re-layouts  1.17 us (2%)
  between operations  0.79 us (1%)
    pallas_call x5, Pallas kernels, whole(): pl.pallas_call(run, in_specs=[smem if x is flags else vmem for x, _ in in...  21.3 us
    ppermute x8, starting transfers between devices, swap(): lax.ppermute(block, axis, swap_pairs(lax.axis_size(axis), first, closed))  14.2 us
    pallas_call x2, Pallas kernels, body(): pl.pallas_call(run, in_specs=[smem if x is flags else vmem for x, _ in in...  8.86 us
    ppermute x8, waiting for transfers between devices, swap(): lax.ppermute(block, axis, swap_pairs(lax.axis_size(axis), first, closed))  3.08 us
    pallas_call x1, Pallas kernels, body(): pl.pallas_call(rows_kernel, in_specs=[smem] + [pl.BlockSpec(memory_space=...  2.95 us
    unnamed x12, local copies, waits for them, and re-layouts  1.17 us
  transfers between devices with their start and end apart: 8, of which 2 were waited for; matrix products, arithmetic and copies ran while one was open for 0% of the time, Pallas kernels for 44%

profile of v8, /device:TPU:1, one launch (start us, length us, event | category | flops | bytes accessed | tf_op | source)
XLA Modules:
  0.0 53.1 jit_solution(5042491266459088057)
XLA Ops:
  0.6 0.0 copy-start.1
  0.7 0.0 copy-start
  0.7 0.1 pad_add_fusion.flag_ref.refs_0_
  0.7 0.0 copy-start.2
  0.7 1.1 %copy-done.2 = f32[6,8,16,128]{3,2,1,0:T(8,128)S(1)} copy-done((f32[6,8,16,128]{3,2,1,0:T(8,128)S(1)}, f32[6,8,16,128]{3,2,1,0:T(8,128)}, u32[]{:S(2)}) %copy-start.2) | copy-done | bytes 393240
  1.9 0.0 copy-start.3
  1.9 0.0 copy-start.4
  1.9 0.0 copy-start.5
  1.9 3.0 %shard_map.79 = (bf16[8,176,128]{2,1,0:T(8,128)(2,1)S(1)}, bf16[8,176,128]{2,1,0:T(8,128)(2,1)S(1)}) custom-call(s32[3]{0:T(128)S(1)} %pad_add_fusion.flag_ref.refs_0_, bf16[8,128,16,128]{3,2,1,0:T(8,128)(2,1)} %x_hbm.1, f32[6,8,16,128]{3,2,1,0:T(8,128)S(1)} %copy-done.2), custom_call_target="tpu_custom_call" | custom-call | tf_op jit(solution)/shard_map/pallas_call | solution.py:682
  4.9 2.1 %collective-permute-start = (bf16[8,176,128]{2,1,0:T(8,128)(2,1)S(1)}, bf16[8,176,128]{2,1,0:T(8,128)(2,1)S(1)}, u32[]{:S(2)}, u32[]{:S(2)}) collective-permute-start(bf16[8,176,128]{2,1,0:T(8,128)(2,1)S(1)} %get-tuple-element.44), channel_id=1, source_target_pairs={{0,4},{4,0},{8,12},{12,8},{16,20},{20,16},{24,28},{28,24},{1,5},{5... | collective-permute-start | bytes 1081352 | tf_op jit(solution)/shard_map/ppermute | solution.py:44
  7.0 3.3 %collective-permute-start.1 = (bf16[8,176,128]{2,1,0:T(8,128)(2,1)S(1)}, bf16[8,176,128]{2,1,0:T(8,128)(2,1)S(1)}, u32[]{:S(2)}, u32[]{:S(2)}) collective-permute-start(bf16[8,176,128]{2,1,0:T(8,128)(2,1)S(1)} %get-tuple-element.45), channel_id=1, source_target_pairs={{4,8},{8,4},{12,16},{16,12},{20,24},{24,20},{28,0},{0,28},{5,9},{9... | collective-permute-start | bytes 1081352 | tf_op jit(solution)/shard_map/ppermute | solution.py:44
  10.3 0.0 copy-done.1
  10.3 0.0 copy-done.3
  10.3 0.0 copy-done.4
  10.3 0.0 copy-done.5
  10.3 0.7 %shard_map.77 = (bf16[1536,256]{1,0:T(8,128)(2,1)S(1)}, bf16[96,512]{1,0:T(8,128)(2,1)S(1)}, bf16[144,128]{1,0:T(8,128)(2,1)S(1)}, bf16[96,128]{1,0:T(8,128)(2,1...) custom-call(s32[3]{0:T(128)S(1)} %pad_add_fusion.flag_ref.refs_0_, ...), custom_call_target="tpu_custom_call" | custom-call | tf_op jit(solution)/shard_map/pallas_call | solution.py:701
  11.0 0.0 copy-done
  11.0 13.9 %shard_map.78 = (bf16[8,2,128,128]{3,2,1,0:T(8,128)(2,1)S(1)}, bf16[8,2,128,128]{3,2,1,0:T(8,128)(2,1)S(1)}, bf16[8,128,128]{2,1,0:T(8,128)(2,1)S(1)}, bf16[8,12...) custom-call(bf16[8,128,16,128]{3,2,1,0:T(8,128)(2,1)S(1)} %copy-done, ...), custom_call_target="tpu_custom_call" | custom-call | flops 5435817984 | bytes 1048576 | tf_op jit(solution)/shard_map/pallas_call | solution.py:670
  24.9 0.0 collective-permute-done.refs_1_
  24.9 0.0 collective-permute-done.1.refs_2_
  24.9 1.0 %shard_map.80 = (bf16[8,2,128,128]{3,2,1,0:T(8,128)(2,1)S(1)}, f32[8,8,8,128]{3,2,1,0:T(8,128)S(1)}, bf16[8,128,128]{2,1,0:T(8,128)(2,1)S(1)}, bf16[8,128,128]{2,1,0:T(8,128)(2,1)S(1)}) custom-call(s32[3]{0:T(128)S(1)} %pad_add_fusion.flag_ref.refs_0_, bf16[8,176,128]{2,1,0:T(8,128)(2,1)S(1)} %collective-permute-done.refs_1_, ...), custom_call_target="tpu_custom_call" | custom-call | flops 4194304 | bytes 1048576 | tf_op jit(solution)/shard_map/pallas_call | solution.py:670
  26.0 1.3 %collective-permute-start.2 = (bf16[8,128,128]{2,1,0:T(8,128)(2,1)S(1)}, bf16[8,128,128]{2,1,0:T(8,128)(2,1)S(1)}, u32[]{:S(2)}, u32[]{:S(2)}) collective-permute-start(bf16[8,128,128]{2,1,0:T(8,128)(2,1)S(1)} %get-tuple-element.48), channel_id=1, source_target_pairs={{0,1},{1,0},{2,3},{3,2},{4,5},{5,4},{6,7},{7,6},{8,9},{9,8},{10,11... | collective-permute-start | bytes 786440 | tf_op jit(solution)/shard_map/ppermute | solution.py:44
  27.3 3.0 %collective-permute-start.3 = (bf16[8,128,128]{2,1,0:T(8,128)(2,1)S(1)}, bf16[8,128,128]{2,1,0:T(8,128)(2,1)S(1)}, u32[]{:S(2)}, u32[]{:S(2)}) collective-permute-start(bf16[8,128,128]{2,1,0:T(8,128)(2,1)S(1)} %get-tuple-element.49), channel_id=1, source_target_pairs={{1,2},{2,1},{5,6},{6,5},{9,10},{10,9},{13,14},{14,13},{17,18},{18,... | collective-permute-start | bytes 786440 | tf_op jit(solution)/shard_map/ppermute | solution.py:44
  30.3 2.3 %shard_map.81.refs_11_ = f32[8,6,16,128]{3,2,1,0:T(8,128)S(1)} custom-call(bf16[8,2,128,128]{3,2,1,0:T(8,128)(2,1)S(1)} %get-tuple-element.47.refs_0_.refs_3_, bf16[8,2,128,128]{3,2,1,0:T(8,128)(2,1)S(1)} %get-tuple-element.52.refs_1_, bf16[8,2,128,128]{3,2,1,0:T(8,128)(2,1)S(1)} %get-tuple-element.53.refs_2_, bf16[1152,128]{1,0:T(8,128)(2,1)S(1)} %bitcast.9, ...), custom_call_target="tpu_custom_call" | custom-call | flops 679477248 | bytes 1048576 | tf_op jit(solution)/shard_map/pallas_call | solution.py:670
  32.6 0.0 collective-permute-done.2.refs_4_
  32.6 2.4 %collective-permute-done.3.refs_5_ = bf16[8,128,128]{2,1,0:T(8,128)(2,1)S(1)} collective-permute-done((bf16[8,128,128]{2,1,0:T(8,128)(2,1)S(1)}, bf16[8,128,128]{2,1,0:T(8,128)(2,1)S(1)}, u32[]{:S(2)}, u32[]{:S(2)}) %collective-permute-start.3) | collective-permute-done | bytes 262176 | tf_op jit(solution)/shard_map/ppermute | solution.py:44
  34.9 2.1 %shard_map.83 = (f32[4,2,8,128]{3,2,1,0:T(8,128)S(1)}, f32[4,4,16,128]{3,2,1,0:T(8,128)S(1)}, f32[4,4,16,128]{3,2,1,0:T(8,128)S(1)}, f32[4,6,16,128]{3,2,1,0:T(8...) custom-call(s32[3]{0:T(128)S(1)} %pad_add_fusion.flag_ref.refs_0_, ...), custom_call_target="tpu_custom_call" | custom-call | flops 402653184 | bytes 1048576 | tf_op jit(solution)/shard_map/pallas_call | solution.py:670
  37.0 0.1 collective-permute-start.6
  37.1 2.6 %collective-permute-start.7 = (bf16[4,128,128]{2,1,0:T(8,128)(2,1)S(1)}, bf16[4,128,128]{2,1,0:T(8,128)(2,1)S(1)}, u32[]{:S(2)}, u32[]{:S(2)}) collective-permute-start(bf16[4,128,128]{2,1,0:T(8,128)(2,1)S(1)} %get-tuple-element.70), channel_id=1, source_target_pairs={{4,8},{8,4},{12,16},{16,12},{20,24},{24,20},{28,0},{0,28},{5,9},{9... | collective-permute-start | bytes 393224 | tf_op jit(solution)/shard_map/ppermute | solution.py:44
  39.7 2.1 %shard_map.82 = (f32[4,2,8,128]{3,2,1,0:T(8,128)S(1)}, f32[4,4,16,128]{3,2,1,0:T(8,128)S(1)}, f32[4,4,16,128]{3,2,1,0:T(8,128)S(1)}, f32[4,6,16,128]{3,2,1,0:T(8...) custom-call(s32[3]{0:T(128)S(1)} %pad_add_fusion.flag_ref.refs_0_, ...), custom_call_target="tpu_custom_call" | custom-call | flops 402653184 | bytes 1048576 | tf_op jit(solution)/shard_map/pallas_call | solution.py:670
  41.8 0.1 collective-permute-start.4
  41.9 1.7 %collective-permute-start.5 = (bf16[4,128,128]{2,1,0:T(8,128)(2,1)S(1)}, bf16[4,128,128]{2,1,0:T(8,128)(2,1)S(1)}, u32[]{:S(2)}, u32[]{:S(2)}) collective-permute-start(bf16[4,128,128]{2,1,0:T(8,128)(2,1)S(1)} %get-tuple-element.59), channel_id=1, source_target_pairs={{4,8},{8,4},{12,16},{16,12},{20,24},{24,20},{28,0},{0,28},{5,9},{9... | collective-permute-start | bytes 393224 | tf_op jit(solution)/shard_map/ppermute | solution.py:44
  43.6 0.0 collective-permute-done.6.refs_5_
  43.6 0.7 %collective-permute-done.7.refs_6_ = bf16[4,128,128]{2,1,0:T(8,128)(2,1)S(1)} collective-permute-done((bf16[4,128,128]{2,1,0:T(8,128)(2,1)S(1)}, bf16[4,128,128]{2,1,0:T(8,128)(2,1)S(1)}, u32[]{:S(2)}, u32[]{:S(2)}) %collective-permute-start.7) | collective-permute-done | bytes 131104 | tf_op jit(solution)/shard_map/ppermute | solution.py:44
  44.2 4.4 %shard_map.84 = (f32[12,8,16,128]{3,2,1,0:T(8,128)}, f32[6,8,16,128]{3,2,1,0:T(8,128)}) custom-call(s32[3]{0:T(128)S(1)} %pad_add_fusion.flag_ref.refs_0_, f32[8,16,16,128]{3,2,1,0:T(8,128)S(1)} %get-tuple-element.41.refs_6_.refs_7_.refs_12_.refs_13_.refs_1_, f32[4,6,16,128]{3,2,1,0:T(8,128)S(1)} %get-tuple-element.66.refs_2_, ...), custom_call_target="tpu_custom_call" | custom-call | flops 67108864 | bytes 2097152 | tf_op jit(solution)/shard_map/pallas_call | solution.py:832
  48.7 0.0 collective-permute-done.4.refs_5_
  48.7 0.0 collective-permute-done.5.refs_6_
  48.7 4.4 %shard_map.85 = (f32[12,8,16,128]{3,2,1,0:T(8,128)}, f32[6,8,16,128]{3,2,1,0:T(8,128)}) custom-call(s32[3]{0:T(128)S(1)} %pad_add_fusion.flag_ref.refs_0_, f32[8,16,16,128]{3,2,1,0:T(8,128)S(1)} %get-tuple-element.41.refs_6_.refs_7_.refs_12_.refs_13_.refs_1_, ...), custom_call_target="tpu_custom_call", output_to_operand_aliasing={{0}: (14, {}), {1}: (15, {})} | custom-call | flops 67108864 | bytes 2097152 | tf_op jit(solution)/shard_map/pallas_call | solution.py:832
Async XLA Ops:
  0.6 9.6 %copy-start.1 = (bf16[3,3,128,128]{3,2,1,0:T(8,128)(2,1)S(1)}, bf16[3,3,128,128]{3,2,1,0:T(8,128)(2,1)}, u32[]{:S(2)}) copy-start(bf16[3,3,128,128]{3,2,1,0:T(8,128)(2,1)} %param.7) | copy-start | bytes 884740
  0.7 10.4 %copy-start = (bf16[8,128,16,128]{3,2,1,0:T(8,128)(2,1)S(1)}, bf16[8,128,16,128]{3,2,1,0:T(8,128)(2,1)}, u32[]{:S(2)}) copy-start(bf16[8,128,16,128]{3,2,1,0:T(8,128)(2,1)} %x_hbm.1) | copy-start | bytes 12582916
  0.7 1.1 %copy-start.2 = (f32[6,8,16,128]{3,2,1,0:T(8,128)S(1)}, f32[6,8,16,128]{3,2,1,0:T(8,128)}, u32[]{:S(2)}) copy-start(f32[6,8,16,128]{3,2,1,0:T(8,128)} %st_hbm.1) | copy-start | bytes 1179652
  1.9 8.4 %copy-start.3 = (bf16[3,3,128,12]{2,3,1,0:T(8,128)(2,1)S(1)}, bf16[3,3,128,12]{2,3,1,0:T(8,128)(2,1)}, u32[]{:S(2)}) copy-start(bf16[3,3,128,12]{2,3,1,0:T(8,128)(2,1)} %param.9) | copy-start | bytes 82948
  1.9 8.4 %copy-start.4 = (f32[128]{0:T(128)S(1)}, f32[128]{0:T(128)}, u32[]{:S(2)}) copy-start(f32[128]{0:T(128)} %param.8) | copy-start | bytes 1540
  1.9 8.4 %copy-start.5 = (f32[12]{0:T(128)S(1)}, f32[12]{0:T(128)}, u32[]{:S(2)}) copy-start(f32[12]{0:T(128)} %refs_0_.2) | copy-start | bytes 148
  4.9 20.0 %collective-permute-start = (bf16[8,176,128]{2,1,0:T(8,128)(2,1)S(1)}, bf16[8,176,128]{2,1,0:T(8,128)(2,1)S(1)}, u32[]{:S(2)}, u32[]{:S(2)}) collective-permute-start(bf16[8,176,128]{2,1,0:T(8,128)(2,1)S(1)} %get-tuple-element.44), channel_id=1, source_target_pairs={{0,4},{4,0},{8,12},{12,8},{16,20},{20,16},{24,28},{28,24},{1,5},{5... | collective-permute-start | bytes 1081352 | tf_op jit(solution)/shard_map/ppermute | solution.py:44
  7.0 17.9 %collective-permute-start.1 = (bf16[8,176,128]{2,1,0:T(8,128)(2,1)S(1)}, bf16[8,176,128]{2,1,0:T(8,128)(2,1)S(1)}, u32[]{:S(2)}, u32[]{:S(2)}) collective-permute-start(bf16[8,176,128]{2,1,0:T(8,128)(2,1)S(1)} %get-tuple-element.45), channel_id=1, source_target_pairs={{4,8},{8,4},{12,16},{16,12},{20,24},{24,20},{28,0},{0,28},{5,9},{9... | collective-permute-start | bytes 1081352 | tf_op jit(solution)/shard_map/ppermute | solution.py:44
  26.0 6.6 %collective-permute-start.2 = (bf16[8,128,128]{2,1,0:T(8,128)(2,1)S(1)}, bf16[8,128,128]{2,1,0:T(8,128)(2,1)S(1)}, u32[]{:S(2)}, u32[]{:S(2)}) collective-permute-start(bf16[8,128,128]{2,1,0:T(8,128)(2,1)S(1)} %get-tuple-element.48), channel_id=1, source_target_pairs={{0,1},{1,0},{2,3},{3,2},{4,5},{5,4},{6,7},{7,6},{8,9},{9,8},{10,11... | collective-permute-start | bytes 786440 | tf_op jit(solution)/shard_map/ppermute | solution.py:44
  27.3 7.7 %collective-permute-start.3 = (bf16[8,128,128]{2,1,0:T(8,128)(2,1)S(1)}, bf16[8,128,128]{2,1,0:T(8,128)(2,1)S(1)}, u32[]{:S(2)}, u32[]{:S(2)}) collective-permute-start(bf16[8,128,128]{2,1,0:T(8,128)(2,1)S(1)} %get-tuple-element.49), channel_id=1, source_target_pairs={{1,2},{2,1},{5,6},{6,5},{9,10},{10,9},{13,14},{14,13},{17,18},{18,... | collective-permute-start | bytes 786440 | tf_op jit(solution)/shard_map/ppermute | solution.py:44
  37.0 6.5 %collective-permute-start.6 = (bf16[4,128,128]{2,1,0:T(8,128)(2,1)S(1)}, bf16[4,128,128]{2,1,0:T(8,128)(2,1)S(1)}, u32[]{:S(2)}, u32[]{:S(2)}) collective-permute-start(bf16[4,128,128]{2,1,0:T(8,128)(2,1)S(1)} %get-tuple-element.69), channel_id=1, source_target_pairs={{0,4},{4,0},{8,12},{12,8},{16,20},{20,16},{24,28},{28,24},{1,5},{5... | collective-permute-start | bytes 393224 | tf_op jit(solution)/shard_map/ppermute | solution.py:44
  37.1 7.1 %collective-permute-start.7 = (bf16[4,128,128]{2,1,0:T(8,128)(2,1)S(1)}, bf16[4,128,128]{2,1,0:T(8,128)(2,1)S(1)}, u32[]{:S(2)}, u32[]{:S(2)}) collective-permute-start(bf16[4,128,128]{2,1,0:T(8,128)(2,1)S(1)} %get-tuple-element.70), channel_id=1, source_target_pairs={{4,8},{8,4},{12,16},{16,12},{20,24},{24,20},{28,0},{0,28},{5,9},{9... | collective-permute-start | bytes 393224 | tf_op jit(solution)/shard_map/ppermute | solution.py:44
  41.8 6.9 %collective-permute-start.4 = (bf16[4,128,128]{2,1,0:T(8,128)(2,1)S(1)}, bf16[4,128,128]{2,1,0:T(8,128)(2,1)S(1)}, u32[]{:S(2)}, u32[]{:S(2)}) collective-permute-start(bf16[4,128,128]{2,1,0:T(8,128)(2,1)S(1)} %get-tuple-element.58), channel_id=1, source_target_pairs={{0,4},{4,0},{8,12},{12,8},{16,20},{20,16},{24,28},{28,24},{1,5},{5... | collective-permute-start | bytes 393224 | tf_op jit(solution)/shard_map/ppermute | solution.py:44
  41.9 6.8 %collective-permute-start.5 = (bf16[4,128,128]{2,1,0:T(8,128)(2,1)S(1)}, bf16[4,128,128]{2,1,0:T(8,128)(2,1)S(1)}, u32[]{:S(2)}, u32[]{:S(2)}) collective-permute-start(bf16[4,128,128]{2,1,0:T(8,128)(2,1)S(1)} %get-tuple-element.59), channel_id=1, source_target_pairs={{4,8},{8,4},{12,16},{16,12},{20,24},{24,20},{28,0},{0,28},{5,9},{9... | collective-permute-start | bytes 393224 | tf_op jit(solution)/shard_map/ppermute | solution.py:44
